TPU v7x, 32 devices: a whole 2x2x4 slice. The times are simulated.
32 devices in a mesh: grp: 16 (over z, y, x), tile: 2 (over core).
Axes of the slice: x: 2, y: 2, z: 4, core: 2. Of those that a mesh axis runs over, the one named last changes fastest.
Arguments:
- starting_realizations: float32 [1024, 2, 4, 16, 128], P('grp', None, None, 'tile'), may hold values from -6 to 6
- diffusivity: float32 [4, 128], replicated, may hold values from 0.1 to 0.24
- eastward_velocity: float32 [4], replicated, may hold values from -0.4 to 0.4
- northward_velocity: float32 [4], replicated, may hold values from -0.4 to 0.4
- obs_cell: int32 [2, 16, 256], P('tile'), may hold values from 0 to 2047
- obs_count: int32 [2, 16], P('tile', 'grp'), may hold values from 1 to 256
- obs_value: float32 [2, 16, 256], P('tile', 'grp'), may hold values from -15 to 15
- obs_weight: float32 [2, 16, 256], P('tile', 'grp'), may hold values from 0.05 to 0.5
Outputs:
- analysis: bfloat16 [1024, 2, 4, 16, 128], P('grp', None, None, 'tile')
All inputs are finite; a program needn't handle non-finite values.
Results may differ from a plain program's by a relative error of at most 0.0062.
Values may be sent and summed in bfloat16 or wider, within the bound.
No kernel may reach another device: no remote copies, remote signals or barrier semaphores. Data moves between devices by JAX's collectives and lax.ppermute only.
A program may use at most 128 MiB of HBM per device.

v0:
```python
import functools

import jax
import jax.numpy as jnp
from jax import lax
from jax.experimental import pallas as pl
from jax.experimental.pallas import tpu as pltpu
from jax.sharding import PartitionSpec as P

SPAN = 8
STEPS = 2
EDGE = SPAN // 2

ROWS = (((1,), (1,)), ((), ()))


def params(mebibytes, **kw):
    return pltpu.CompilerParams(vmem_limit_bytes=mebibytes * 2**20, **kw)


def cost(flops, size):
    return pl.CostEstimate(flops=flops, bytes_accessed=size, transcendentals=0)


def vmem(count):
    return [pl.BlockSpec(memory_space=pltpu.VMEM)] * count


def hbm(count):
    return [pl.BlockSpec(memory_space=pltpu.HBM)] * count


def smem(count):
    return [pl.BlockSpec(memory_space=pltpu.SMEM)] * count


def dot(a, b, **kw):
    return jnp.dot(a, b, preferred_element_type=jnp.float32, **kw)


def split(x):
    high = x.astype(jnp.bfloat16)
    return high, (x - high.astype(jnp.float32)).astype(jnp.bfloat16)


def dot3(a, b):
    (a_high, a_low), (b_high, b_low) = split(a), split(b)
    return dot(a_high, b_high) + (dot(a_high, b_low) + dot(a_low, b_high))


def dot_rows(a, b):
    return lax.dot_general(a, b, ROWS, preferred_element_type=jnp.float32)


def permutation(size, shift):
    row = lax.broadcasted_iota(jnp.int32, (size, size), 0)
    column = lax.broadcasted_iota(jnp.int32, (size, size), 1)
    return (lax.rem(row + shift + size, size) == column).astype(jnp.bfloat16)


def eye(size):
    row = lax.broadcasted_iota(jnp.int32, (size, size), 0)
    column = lax.broadcasted_iota(jnp.int32, (size, size), 1)
    return row == column


def column_of(row):
    return jnp.sum(jnp.where(eye(row.shape[1]), row, 0.0), axis=1, keepdims=True)


def row_of(column):
    return jnp.sum(jnp.where(eye(column.shape[0]), column, 0.0), axis=0, keepdims=True)


def forecast_rows(read, first, last, coefficients):
    middle, east, west, north, south = coefficients

    def step(below, here, above):
        columns = here.shape[2]
        return (
            middle * here
            + east * above
            + west * below
            + north * pltpu.roll(here, columns - 1, 2)
            + south * pltpu.roll(here, 1, 2)
        )

    rows, once, twice = [read(first - 2), read(first - 1)], [], []
    for r in range(first - 1, last + 1):
        rows.append(read(r + 1))
        once.append(step(*rows[-3:]))
        if r >= first + 1:
            new = step(*once[-3:])
            twice.append((r - 1, new.reshape(-1, new.shape[2]).astype(jnp.bfloat16)))
    return twice


def model_rows(diffusivity, eastward, northward):
    levels, columns = diffusivity.shape
    place = lax.broadcasted_iota(jnp.int32, (levels, 3, columns), 1)
    speeds = jnp.where(place == 1, eastward[:, None, None], northward[:, None, None])
    return jnp.where(place == 0, diffusivity[:, None, :], speeds)


def coefficients_of(model, level):
    spread, u, w = (
        jnp.broadcast_to(model[level, i : i + 1, :], (8, model.shape[2])) for i in range(3)
    )
    u, w = 0.5 * u, 0.5 * w
    return 1.0 - 4.0 * spread, spread - u, spread + u, spread - w, spread + w


def row_reader(level, var, own, low, high):
    span, columns = own.shape[2], own.shape[4]

    def read(r):
        ref, at = (low, r + span) if r < 0 else (own, r) if r < span else (high, r - span)
        return ref[var, level, at].reshape(-1, 8, columns)

    return read


def pack_rows(pairs, identity, store, first):
    lanes = pairs[0].shape[0] // 2
    packed = []
    for pair in pairs:
        turned = dot_rows(identity, pair)
        parts = [turned[:, i * lanes : (i + 1) * lanes].reshape(-1, SPAN, lanes) for i in range(2)]
        packed.append(jnp.concatenate(parts, axis=1).astype(jnp.bfloat16))
    for i, value in enumerate(packed):
        at = first + i * 2 * SPAN
        store[:, at : at + 2 * SPAN, :] = value


def inner_kernel(variables, own, model, slabs, fields, packed):
    lanes, _, span, columns = own.shape
    members = lanes // variables
    count = span - 2 * STEPS
    coefficients = coefficients_of(model, pl.program_id(0))
    view = own.reshape(lanes * span, columns)
    reads, made = [], []
    for var in range(variables):

        def read(r):
            rows = view[pl.ds(var * span + r, members, stride=variables * span), :]
            reads.append((var, r, rows))
            return rows.reshape(-1, 8, columns)

        for r, value in forecast_rows(read, STEPS, span - STEPS, coefficients):
            made.append((var, r, value))
    identity = permutation(columns, 0)
    pairs = []
    for first in range(STEPS, span - STEPS, 2):
        rows = [one for r in (first, first + 1) for _, at, one in made if at == r]
        pairs.append(jnp.concatenate(rows, axis=0))
    pack_rows(pairs, identity, packed, 0)
    for var, r, value in made:
        fields[0, r - STEPS, var * members : (var + 1) * members, :] = value
    for var, r, rows in reads:
        slabs[var, 0, r] = rows


def inner(own, model, variables):
    lanes, levels, span, columns = own.shape
    members = lanes // variables
    blocks = columns // SPAN
    count = span - 2 * STEPS
    return pl.pallas_call(
        functools.partial(inner_kernel, variables),
        grid=(levels,),
        out_shape=[
            jax.ShapeDtypeStruct((variables, levels, span, members, columns), jnp.float32),
            jax.ShapeDtypeStruct((levels, count, lanes, columns), jnp.bfloat16),
            jax.ShapeDtypeStruct((blocks, levels * count * SPAN, lanes), jnp.bfloat16),
        ],
        in_specs=[pl.BlockSpec((lanes, 1, span, columns), lambda level: (0, level, 0, 0))] + vmem(1),
        out_specs=[
            pl.BlockSpec((variables, 1, span, members, columns), lambda level: (0, level, 0, 0, 0)),
            pl.BlockSpec((1, count, lanes, columns), lambda level: (level, 0, 0, 0)),
            pl.BlockSpec((blocks, count * SPAN, lanes), lambda level: (0, level, 0)),
        ],
        compiler_params=params(50),
        cost_estimate=cost(2 * 10**9, 4 * 2**20),
    )(own, model)


def outer_kernel(near, own, *rest):
    sides, rest = rest[:near], rest[near:]
    model, centre, grid, packed, fields, sems = rest
    variables, levels, span, members, columns = own.shape
    rows = variables * members
    pairs = (2 * EDGE + span) // 2

    copies = []
    for r in range(STEPS, span - STEPS):
        half, pair = divmod(r + EDGE, pairs)
        place = grid.at[:, pair, pl.ds(half * rows, rows)]
        copies.append(pltpu.make_async_copy(centre.at[:, r - STEPS], place, sems.at[r - STEPS]))
        copies[-1].start()

    @pl.loop(0, levels)
    def _(level):
        coefficients = coefficients_of(model, level)
        made = []
        for var in range(variables):
            read = row_reader(level, var, own, sides[0], sides[-1])
            for first, last in ((-EDGE, STEPS), (span - STEPS, span + EDGE)):
                for r, value in forecast_rows(read, first, last, coefficients):
                    made.append((var, r, value))
        for var, r, value in made:
            half, pair = divmod(r + EDGE, pairs)
            at = half * rows + var * members
            grid[level, pair, at : at + members, :] = value
            if 0 <= r < span:
                pair, half = divmod(r if r < STEPS else r - span + 2 * STEPS, 2)
                at = half * rows + var * members
                fields[level, pair, at : at + members, :] = value

    identity = permutation(columns, 0)
    for level in range(0, levels, 2):
        batch = [fields[at, pair] for at in range(level, min(levels, level + 2)) for pair in range(STEPS)]
        pack_rows(batch, identity, packed, level * STEPS * 2 * SPAN)
    for copy in copies:
        copy.wait()


def outer(dims, own, sides, model, centre):
    members, variables, levels, span, columns = dims
    lanes = members * variables
    blocks = columns // SPAN
    near = len(sides)
    pairs = (2 * EDGE + span) // 2
    return pl.pallas_call(
        functools.partial(outer_kernel, near),
        out_shape=[
            jax.ShapeDtypeStruct((levels, pairs, 2 * lanes, columns), jnp.bfloat16),
            jax.ShapeDtypeStruct((blocks, levels * 2 * STEPS * SPAN, lanes), jnp.bfloat16),
        ],
        in_specs=vmem(2 + near) + hbm(1),
        out_specs=vmem(2),
        scratch_shapes=[
            pltpu.VMEM((levels, STEPS, 2 * lanes, columns), jnp.bfloat16),
            pltpu.SemaphoreType.DMA((span - 2 * STEPS,)),
        ],
        compiler_params=params(16),
        cost_estimate=cost(2 * 10**9, 8 * 2**20),
    )(own, *sides, model, centre)


def pick_kernel(variables, together, grid, rim, cells, out, region, codes):
    levels, pairs, twice, columns = grid.shape
    rows = twice // 2
    members = rows // variables
    blocks, slots = cells.shape
    width = 2 * EDGE + SPAN
    part = pairs * width
    entries = levels * part
    share = rim.shape[1]

    orders = jnp.concatenate(
        [permutation(columns, -EDGE), permutation(columns, SPAN - EDGE)], axis=0
    )
    batch = next(n for n in (4, 2, 1) if pairs % n == 0)
    for level in range(levels):
        for start in range(0, pairs, batch):
            turned = [
                dot_rows(orders, grid[level, start + i]).astype(jnp.bfloat16) for i in range(batch)
            ]
            for i, value in enumerate(turned):
                at = (level * pairs + start + i) * width
                for first in range(2):
                    for j in range(columns // width):
                        row = first * columns + j * width
                        region[2 * j + first, at : at + width, :] = value[row : row + width, :]

    cell = cells[...]
    second = cell >= 2 * entries
    cell = jnp.where(second, cell - 2 * entries, cell)
    level = lax.shift_right_logical(cell, (2 * part).bit_length() - 1)
    inside = cell - level * (2 * part)
    lower = inside >= part
    code = level * part + jnp.where(lower, inside - part + entries, inside)
    codes[...] = jnp.where(second, code + 2 * entries, code).astype(jnp.float32)

    left = lax.broadcasted_iota(jnp.int32, (slots // 2, rows), 1) < members
    lane = lax.broadcasted_iota(jnp.int32, (slots, entries), 1).astype(jnp.float32)

    @pl.loop(0, blocks // together)
    def _(step):
        made = []
        for i in range(together):
            block = step * together + i
            at = column_of(codes[pl.ds(block, 1), :])
            second = at >= 2.0 * entries
            at = jnp.where(second, at - 2.0 * entries, at)
            lower = at >= 1.0 * entries
            at = jnp.where(lower, at - 1.0 * entries, at)
            pick = jnp.where(lane == at, 1.0, 0.0).astype(jnp.bfloat16)
            found = dot(pick, region[block])
            total = jnp.where(lower, found[:, rows:], found[:, :rows])
            other = pltpu.roll(total, members, 1)
            to_left = jnp.where(second, other, total)[: slots // 2]
            to_right = jnp.where(second, total, other)[slots // 2 :]
            made.append(jnp.where(left, to_left, to_right).astype(jnp.bfloat16))
        for i, value in enumerate(made):
            block = step * together + i
            out[block, share:, :] = value
            out[block, :share, :] = rim[block]


def pick(variables, grid, rim, cells):
    levels, pairs, twice, columns = grid.shape
    blocks, slots = cells.shape
    _, share, lanes = rim.shape
    together = next(n for n in (4, 2, 1) if blocks % n == 0)
    return pl.pallas_call(
        functools.partial(pick_kernel, variables, together),
        out_shape=jax.ShapeDtypeStruct((blocks, share + slots // 2, lanes), jnp.bfloat16),
        in_specs=vmem(3),
        out_specs=pl.BlockSpec(memory_space=pltpu.VMEM),
        scratch_shapes=[
            pltpu.VMEM((blocks, levels * pairs * (2 * EDGE + SPAN), twice), jnp.bfloat16),
            pltpu.VMEM((blocks, slots), jnp.float32),
        ],
        compiler_params=params(20),
        cost_estimate=cost(4 * 10**9, 4 * 2**20),
    )(grid, rim, cells)


def join(a, b, left, members):
    return (
        jnp.where(left, a, pltpu.roll(b, members, 1)),
        jnp.where(left, pltpu.roll(a, members, 1), b),
    )


def batches(count, size):
    return [range(at, min(count, at + size)) for at in range(0, count, size)]


def left_lanes(shape):
    return lax.broadcasted_iota(jnp.int32, shape, 1) < shape[1] // 2


def deviations(states, raw, dev, at, size):
    groups, _, lanes = states.shape
    members = lanes // 2
    left = left_lanes((size, lanes))
    sums = [jnp.zeros((size, lanes), jnp.float32)] * 2
    for batch in batches(groups // 2, 4):
        made = [
            join(
                states[2 * j, :size, :].astype(jnp.float32),
                states[2 * j + 1, :size, :].astype(jnp.float32),
                left,
                members,
            )
            for j in batch
        ]
        for j, pair in zip(batch, made):
            here = slice(j * lanes, (j + 1) * lanes)
            for var in range(2):
                raw[var * size : (var + 1) * size, here] = pair[var]
            sums = [total + one for total, one in zip(sums, pair)]
    centre = jnp.concatenate([jnp.sum(x, axis=1, keepdims=True) for x in sums], axis=0)
    centre = centre * (1.0 / (groups * members))
    dev[at : at + 2 * size, :] = (raw[...] - centre).astype(jnp.bfloat16)
    return centre


def prepare_kernel(states, dev, centre, raw):
    mean = deviations(states, raw, dev, 0, states.shape[1])
    centre[...] = jnp.broadcast_to(mean, centre.shape)


def prepare(states):
    groups, near, lanes = states.shape
    total = groups * lanes // 2
    return pl.pallas_call(
        prepare_kernel,
        out_shape=[
            jax.ShapeDtypeStruct((2 * near, total), jnp.bfloat16),
            jax.ShapeDtypeStruct((2 * near, lanes), jnp.float32),
        ],
        in_specs=vmem(1),
        out_specs=vmem(2),
        scratch_shapes=[pltpu.VMEM((2 * near, total), jnp.float32)],
        compiler_params=params(6),
        cost_estimate=cost(10**8, 2 * 2**20),
    )(states)


def analyse_kernel(first, means, second, count, value, weight, out, raw, dev, obs, scaled_ref):
    groups, _, lanes = second.shape
    near = first.shape[0] // 2
    half = obs.shape[0] // 2
    far = second.shape[1] - half
    side = near + far
    slots = 2 * half
    members = lanes // 2
    total_members = groups * members
    left = left_lanes((half, lanes))

    for batch in batches(groups // 2, 4):
        made = [
            join(
                second[2 * j, far:, :].astype(jnp.float32),
                second[2 * j + 1, far:, :].astype(jnp.float32),
                left,
                members,
            )
            for j in batch
        ]
        for j, pair in zip(batch, made):
            here = slice(j * lanes, (j + 1) * lanes)
            obs[:half, here], obs[half:, here] = pair

    used = lax.broadcasted_iota(jnp.int32, (1, slots), 1) < count[0, 0]
    root = column_of(jnp.where(used, jnp.sqrt(weight[...]), 0.0))
    observed = obs[...]
    mean = jnp.sum(observed, axis=1, keepdims=True) * (1.0 / total_members)
    scaled = (observed - mean) * root
    energy = jnp.sum(jnp.sum(scaled * scaled, axis=1, keepdims=True), axis=0, keepdims=True)
    scaled_ref[...] = scaled.astype(jnp.bfloat16)
    misfit = row_of(root * (column_of(value[...]) - mean))

    c = total_members - 1.0
    s = energy * (1.0 / total_members) + c
    inverse = 1.0 / s
    a = c * inverse
    p = 1.5 - 0.5 * a
    p2 = p * p
    p3 = p2 * p
    base = 1.5 * p - 0.5 * a * p3
    q0 = -0.75 - 0.5 * (p3 - 1.5 * a * p2)
    q1 = -0.5 * (0.75 * a * p - 1.5 * p2)
    q2 = -0.5 * (0.75 * p - 0.125 * a)
    small = dot_rows(scaled_ref[...], scaled_ref[...]) * inverse
    diagonal = eye(slots)
    square = dot3(small, small)
    tail = dot3(square, jnp.where(diagonal, q2, 0.0) + 0.0625 * small)
    poly = jnp.where(diagonal, q0, 0.0) + q1 * small + tail

    def apply(vector):
        inner_part = jnp.sum(poly * vector, axis=1, keepdims=True)
        return jnp.sum(small * inner_part, axis=0, keepdims=True) + base * vector

    gain = apply(apply(misfit)) * inverse
    stretch = jnp.sqrt(a)
    alpha, factor = stretch * base, stretch * inverse
    centre = deviations(second, raw, dev, 0, far)
    cross = jnp.concatenate(
        [dot_rows(first[...], scaled_ref[...]), dot_rows(dev[...], scaled_ref[...])], axis=0
    )
    centre = jnp.concatenate([means[:, 0:1], centre], axis=0)
    shift = centre + jnp.sum(cross * gain, axis=1, keepdims=True)
    mix = (dot3(cross, poly) * factor).astype(jnp.bfloat16)
    parts = ((first, 0, near, 0), (dev, 2 * near, far, near))
    for batch in batches(groups // 2, 2):
        made = []
        for j in batch:
            here = slice(j * lanes, (j + 1) * lanes)
            new = dot(mix, scaled_ref[:, here]) + shift
            for ref, at, size, row in parts:
                one = new[at : at + 2 * size] + alpha * ref[:, here].astype(jnp.float32)
                pair = join(one[:size], one[size:], left_lanes((size, lanes)), members)
                made += [(2 * j + i, row, x.astype(jnp.bfloat16)) for i, x in enumerate(pair)]
        for group, row, value in made:
            out[group, row : row + value.shape[0], :] = value


def analyse(first, means, second, count, value, weight):
    groups, _, lanes = second.shape
    near = first.shape[0] // 2
    slots = value.shape[1]
    far = second.shape[1] - slots // 2
    total = groups * lanes // 2
    return pl.pallas_call(
        analyse_kernel,
        out_shape=jax.ShapeDtypeStruct((groups, near + far, lanes), jnp.bfloat16),
        in_specs=vmem(3) + smem(1) + vmem(2),
        out_specs=pl.BlockSpec(memory_space=pltpu.VMEM),
        scratch_shapes=[
            pltpu.VMEM((2 * far, total), jnp.float32),
            pltpu.VMEM((2 * far, total), jnp.bfloat16),
            pltpu.VMEM((slots, total), jnp.float32),
            pltpu.VMEM((slots, total), jnp.bfloat16),
        ],
        compiler_params=params(16),
        cost_estimate=cost(4 * 10**9, 4 * 2**20),
    )(first, means, second, count, value, weight)


def restore_kernel(blocks, out, turned):
    members, variables, levels, span, columns = out.shape
    lanes = members * variables
    identity = permutation(lanes, 0)
    near = span - 2 * STEPS
    for level in range(levels):
        made = []
        for r in range(0, span, 2):
            if STEPS <= r < span - STEPS:
                at = level * near + r - STEPS
            else:
                at = levels * near + level * 2 * STEPS + (r if r < STEPS else r - near)
            both = blocks[:, at * SPAN : (at + 2) * SPAN, :].astype(jnp.float32)
            for i in range(2):
                one = both[:, i * SPAN : (i + 1) * SPAN, :].reshape(columns, lanes)
                made.append((r + i, dot_rows(identity, one.astype(jnp.bfloat16))))
        for r, rows in made:
            turned[level % 2, pl.ds(r, lanes, stride=span), :] = rows
        for var in range(variables):
            half = turned[level % 2, var * members * span : (var + 1) * members * span, :]
            out[:, var, level] = half.reshape(members, span, columns).astype(jnp.bfloat16)


def restore(dims, blocks):
    members, variables, levels, span, columns = dims
    return pl.pallas_call(
        restore_kernel,
        out_shape=jax.ShapeDtypeStruct((members, variables, levels, span, columns), jnp.bfloat16),
        in_specs=vmem(1),
        out_specs=pl.BlockSpec(memory_space=pltpu.VMEM),
        scratch_shapes=[pltpu.VMEM((2, variables * members * span, columns), jnp.float32)],
        compiler_params=params(8),
        cost_estimate=cost(2 * 10**9, 2 * 2**20),
    )(blocks)


def neighbours(field, axis):
    count = lax.axis_size(axis)
    low = lax.ppermute(field, axis, [(i, (i + 1) % count) for i in range(count)])
    if count == 2:
        return (low,)
    return low, lax.ppermute(field, axis, [((i + 1) % count, i) for i in range(count)])


def exchange(blocks):
    return lax.all_to_all(blocks, "grp", split_axis=0, concat_axis=0, tiled=True)


def on_device(start, diffusivity, eastward, northward, cells, count, value, weight):
    members, variables, levels, span, columns = dims = start.shape
    model = model_rows(diffusivity, eastward, northward)
    whole = start.reshape(members * variables, levels, span, columns)
    own, centre, near = inner(whole, model, variables)
    sides = neighbours(own, "tile")
    first, means = prepare(exchange(near))
    grid, rim = outer(dims, own, sides, model, centre)
    second = exchange(pick(variables, grid, rim, cells[0]))
    updated = analyse(first, means, second, count, value[0], weight[0])
    return restore(dims, exchange(updated))


def solution(mesh):
    return jax.shard_map(
        on_device,
        mesh=mesh,
        in_specs=(
            P("grp", None, None, "tile", None),
            P(),
            P(),
            P(),
            P("tile", None, None),
            P("tile", "grp"),
            P("tile", "grp", None),
            P("tile", "grp", None),
        ),
        out_specs=P("grp", None, None, "tile", None),
        check_vma=False,
    )
```

profile of v0, /device:TPU:0, one launch (start us, length us, event | category | flops | bytes accessed | tf_op | source)
XLA Modules:
  0.0 93.4 jit_solution(15934040203247096705)
XLA Ops:
  0.0 0.8 select_select_fusion.model.rest_1_
  0.8 4.8 %shard_map.82 = (f32[2,4,8,64,128]{4,3,2,1,0:T(8,128)S(1)}, bf16[4,4,128,128]{3,2,1,0:T(8,128)(2,1)S(1)}, bf16[16,128,128]{2,1,0:T(8,128)(2,1)}) custom-call(f32[128,4,8,128]{3,2,1,0:T(8,128)} %bitcast.7, f32[4,3,128]{2,1,0:T(4,128)S(1)} %select_select_fusion.model.rest_1_), custom_call_target="tpu_custom_call" | custom-call | flops 2000000000 | bytes 4194304 | tf_op jit(solution)/shard_map/pallas_call | solution.py:168
  5.6 0.5 collective-permute-start
  6.0 7.9 %all-to-all-start = ((bf16[16,128,128]{2,1,0:T(8,128)(2,1)}), bf16[16,128,128]{2,1,0:T(8,128)(2,1)S(1)}, u32[]{:S(2)}, u32[]{:S(2)}) async-start(bf16[16,128,128]{2,1,0:T(8,128)(2,1)} %get-tuple-element.12), calls=%async_computation | async-start | bytes 1048576 | tf_op jit(solution)/shard_map/all_to_all | solution.py:539
  13.9 0.0 collective-permute-done.rest_0_
  13.9 0.0 copy-start
  13.9 7.6 %shard_map.84 = (bf16[4,8,256,128]{3,2,1,0:T(8,128)(2,1)S(1)}, bf16[16,128,128]{2,1,0:T(8,128)(2,1)S(1)}) custom-call(f32[2,4,8,64,128]{4,3,2,1,0:T(8,128)S(1)} %get-tuple-element.15.own, f32[2,4,8,64,128]{4,3,2,1,0:T(8,128)} %collective-permute-done.rest_0_, f32[4,3,128]{2,1,0:T(4,128)S(1)} %select_select_fusion.model.rest_1_, ...), custom_call_target="tpu_custom_call" | custom-call | flops 2000000000 | bytes 8388608 | tf_op jit(solution)/shard_map/pallas_call | solution.py:233
  21.5 0.0 copy-done
  21.5 4.5 %shard_map.85 = bf16[16,256,128]{2,1,0:T(8,128)(2,1)} custom-call(bf16[4,8,256,128]{3,2,1,0:T(8,128)(2,1)S(1)} %get-tuple-element.17.grid, bf16[16,128,128]{2,1,0:T(8,128)(2,1)S(1)} %get-tuple-element.18.rim, s32[16,256]{1,0:T(8,128)S(1)} %bitcast.4), custom_call_target="tpu_custom_call" | custom-call | flops 4000000000 | bytes 4194304 | tf_op jit(solution)/shard_map/pallas_call | solution.py:316
  26.0 0.0 copy-start.1
  26.0 0.0 copy-start.2
  26.0 3.3 %all-to-all-done.states = bf16[16,128,128]{2,1,0:T(8,128)(2,1)S(1)} async-done(((bf16[16,128,128]{2,1,0:T(8,128)(2,1)}), bf16[16,128,128]{2,1,0:T(8,128)(2,1)S(1)}, u32[]{:S(2)}, u32[]{:S(2)}) %all-to-all-start) | async-done | bytes 524320 | tf_op jit(solution)/shard_map/all_to_all | solution.py:539
  29.3 4.2 %all-to-all-start.1 = ((bf16[16,256,128]{2,1,0:T(8,128)(2,1)}), bf16[16,256,128]{2,1,0:T(8,128)(2,1)S(1)}, u32[]{:S(2)}, u32[]{:S(2)}) async-start(bf16[16,256,128]{2,1,0:T(8,128)(2,1)} %shard_map.85), calls=%async_computation.1 | async-start | bytes 2097152 | tf_op jit(solution)/shard_map/all_to_all | solution.py:539
  34.2 0.4 shard_map.83
  34.7 22.9 %all-to-all-done.1.second = bf16[16,256,128]{2,1,0:T(8,128)(2,1)S(1)} async-done(((bf16[16,256,128]{2,1,0:T(8,128)(2,1)}), bf16[16,256,128]{2,1,0:T(8,128)(2,1)S(1)}, u32[]{:S(2)}, u32[]{:S(2)}) %all-to-all-start.1) | async-done | bytes 1048608 | tf_op jit(solution)/shard_map/all_to_all | solution.py:539
  57.6 0.0 copy-done.1
  57.6 0.0 copy-done.2
  57.6 3.2 %shard_map.86 = bf16[16,256,128]{2,1,0:T(8,128)(2,1)S(1)} custom-call(bf16[256,1024]{1,0:T(8,128)(2,1)S(1)} %get-tuple-element.13.first, f32[256,128]{1,0:T(8,128)S(1)} %get-tuple-element.14.means, bf16[16,256,128]{2,1,0:T(8,128)(2,1)S(1)} %all-to-all-done.1.second, s32[1,1]{1,0:T(1,128)S(6)} %copy.9.count, f32[1,256]{1,0:T(1,128)S(1)} %bitcast.5, ...), custom_call_target="tpu_custom_call" | custom-call | flops 4000000000 | bytes 4194304 | tf_op jit(solution)/shard_map/pallas_call | solution.py:478
  60.8 30.6 %all_to_all.15.blocks = bf16[16,256,128]{2,1,0:T(8,128)(2,1)S(1)} all-to-all(bf16[16,256,128]{2,1,0:T(8,128)(2,1)S(1)} %shard_map.86), channel_id=1, replica_groups=mesh['grp'=16,'tile'=2] {'grp'}, dimensions={0} | all-to-all | bytes 2097152 | tf_op jit(solution)/shard_map/all_to_all | solution.py:539
  91.4 2.0 %shard_map.87 = bf16[64,2,4,8,128]{4,3,2,1,0:T(8,128)(2,1)} custom-call(bf16[16,256,128]{2,1,0:T(8,128)(2,1)S(1)} %all_to_all.15.blocks), custom_call_target="tpu_custom_call" | custom-call | flops 2000000000 | bytes 2097152 | tf_op jit(solution)/shard_map/pallas_call | solution.py:519
  (1 shorter events, 0.0 us)
Async XLA Ops:
  5.6 8.3 %collective-permute-start = (f32[2,4,8,64,128]{4,3,2,1,0:T(8,128)S(1)}, f32[2,4,8,64,128]{4,3,2,1,0:T(8,128)}, u32[]{:S(2)}, u32[]{:S(2)}) collective-permute-start(f32[2,4,8,64,128]{4,3,2,1,0:T(8,128)S(1)} %get-tuple-element.15.own), channel_id=1, source_target_pairs={{0,1},{1,0},{2,3},{3,2},{4,5},{5,4},{6,7},{7,6},{8,9},{9,8},{10,11... | collective-permute-start | bytes 6291464 | tf_op jit(solution)/shard_map/ppermute | solution.py:532
  6.0 23.3 %all-to-all-start = ((bf16[16,128,128]{2,1,0:T(8,128)(2,1)}), bf16[16,128,128]{2,1,0:T(8,128)(2,1)S(1)}, u32[]{:S(2)}, u32[]{:S(2)}) async-start(bf16[16,128,128]{2,1,0:T(8,128)(2,1)} %get-tuple-element.12), calls=%async_computation | async-start | bytes 1048576 | tf_op jit(solution)/shard_map/all_to_all | solution.py:539
  13.9 7.6 %copy-start = (s32[1,16,256]{2,1,0:T(8,128)S(1)}, s32[1,16,256]{2,1,0:T(8,128)}, u32[]{:S(2)}) copy-start(s32[1,16,256]{2,1,0:T(8,128)} %param.12) | copy-start | bytes 49156
  26.0 31.6 %copy-start.1 = (f32[1,1,256]{2,1,0:T(1,128)S(1)}, f32[1,1,256]{2,1,0:T(1,128)}, u32[]{:S(2)}) copy-start(f32[1,1,256]{2,1,0:T(1,128)} %param.14) | copy-start | bytes 3076
  26.0 31.6 %copy-start.2 = (f32[1,1,256]{2,1,0:T(1,128)S(1)}, f32[1,1,256]{2,1,0:T(1,128)}, u32[]{:S(2)}) copy-start(f32[1,1,256]{2,1,0:T(1,128)} %param.15) | copy-start | bytes 3076
  29.3 28.3 %all-to-all-start.1 = ((bf16[16,256,128]{2,1,0:T(8,128)(2,1)}), bf16[16,256,128]{2,1,0:T(8,128)(2,1)S(1)}, u32[]{:S(2)}, u32[]{:S(2)}) async-start(bf16[16,256,128]{2,1,0:T(8,128)(2,1)} %shard_map.85), calls=%async_computation.1 | async-start | bytes 2097152 | tf_op jit(solution)/shard_map/all_to_all | solution.py:539
where the time goes:
time: 93.8 us; the launch traced here: 93.4 us
  blocking collectives  30.6 us (33%)
  waiting for transfers between devices  26.2 us (28%)
  Pallas kernels  22.5 us (24%)
  starting transfers between devices  12.6 us (13%)
    all_to_all x1, blocking collectives, exchange(): lax.all_to_all(blocks, 'grp', split_axis=0, concat_axis=0, tiled=True)  30.6 us
    all_to_all x2, waiting for transfers between devices, exchange(): lax.all_to_all(blocks, 'grp', split_axis=0, concat_axis=0, tiled=True)  26.2 us
    all_to_all x2, starting transfers between devices, exchange(): lax.all_to_all(blocks, 'grp', split_axis=0, concat_axis=0, tiled=True)  12.1 us
    pallas_call x1, Pallas kernels, outer(): pl.pallas_call(functools.partial(outer_kernel, near), out_shape=[jax.Shap...  7.56 us
    pallas_call x1, Pallas kernels, inner(): pl.pallas_call(functools.partial(inner_kernel, variables), grid=(levels,)...  4.78 us
    pallas_call x1, Pallas kernels, pick(): pl.pallas_call(functools.partial(pick_kernel, variables, together), out_s...  4.54 us
    pallas_call x1, Pallas kernels, analyse(): pl.pallas_call(analyse_kernel, out_shape=jax.ShapeDtypeStruct((groups, ne...  3.16 us
    pallas_call x1, Pallas kernels, restore(): pl.pallas_call(restore_kernel, out_shape=jax.ShapeDtypeStruct((members, v...  1.99 us
  transfers between devices with their start and end apart: 3, of which 2 were waited for; matrix products, arithmetic and copies ran while one was open for 0% of the time, Pallas kernels for 13%

commit v1 on v0

--- a/solution.py
+++ b/solution.py
@@ -95,18 +95,10 @@
     return twice
 
 
-def model_rows(diffusivity, eastward, northward):
-    levels, columns = diffusivity.shape
-    place = lax.broadcasted_iota(jnp.int32, (levels, 3, columns), 1)
-    speeds = jnp.where(place == 1, eastward[:, None, None], northward[:, None, None])
-    return jnp.where(place == 0, diffusivity[:, None, :], speeds)
-
-
-def coefficients_of(model, level):
-    spread, u, w = (
-        jnp.broadcast_to(model[level, i : i + 1, :], (8, model.shape[2])) for i in range(3)
-    )
-    u, w = 0.5 * u, 0.5 * w
+def coefficients_of(level, diff, east, north):
+    spread = jnp.broadcast_to(diff[level : level + 1, :], (8, diff.shape[1]))
+    u = 0.5 * east[level]
+    w = 0.5 * north[level]
     return 1.0 - 4.0 * spread, spread - u, spread + u, spread - w, spread + w
 
 
@@ -132,56 +124,84 @@
         store[:, at : at + 2 * SPAN, :] = value
 
 
-def inner_kernel(variables, own, model, slabs, fields, packed):
-    lanes, _, span, columns = own.shape
+def inner_kernel(variables, own, *refs):
+    raw, (slabs, fields, packed, model) = refs[:3], refs[3:7]
+    local, (whole, staged, in_sems, raw_sems, out_sems) = refs[7:10], refs[10:]
+    lanes, levels, span, columns = own.shape
     members = lanes // variables
     count = span - 2 * STEPS
-    coefficients = coefficients_of(model, pl.program_id(0))
-    view = own.reshape(lanes * span, columns)
-    reads, made = [], []
-    for var in range(variables):
-
-        def read(r):
-            rows = view[pl.ds(var * span + r, members, stride=variables * span), :]
-            reads.append((var, r, rows))
-            return rows.reshape(-1, 8, columns)
-
-        for r, value in forecast_rows(read, STEPS, span - STEPS, coefficients):
-            made.append((var, r, value))
+    copies = [pltpu.make_async_copy(x, y, raw_sems.at[i]) for i, (x, y) in enumerate(zip(raw, local))]
+    arrivals = [
+        pltpu.make_async_copy(own.at[:, level], whole.at[level], in_sems.at[level])
+        for level in range(levels)
+    ]
+    for copy in copies + arrivals:
+        copy.start()
+    for copy in copies:
+        copy.wait()
     identity = permutation(columns, 0)
-    pairs = []
-    for first in range(STEPS, span - STEPS, 2):
-        rows = [one for r in (first, first + 1) for _, at, one in made if at == r]
-        pairs.append(jnp.concatenate(rows, axis=0))
-    pack_rows(pairs, identity, packed, 0)
-    for var, r, value in made:
-        fields[0, r - STEPS, var * members : (var + 1) * members, :] = value
-    for var, r, rows in reads:
-        slabs[var, 0, r] = rows
-
-
-def inner(own, model, variables):
+    leaving = []
+    for level in range(levels):
+        coefficients = coefficients_of(level, *local)
+        for i, one in enumerate(coefficients):
+            model[level, i] = one
+        arrivals[level].wait()
+        view = whole.at[level].reshape(lanes * span, columns)
+        reads, made = [], []
+        for var in range(variables):
+
+            def read(r):
+                rows = view[pl.ds(var * span + r, members, stride=variables * span), :]
+                reads.append((var, r, rows))
+                return rows.reshape(-1, 8, columns)
+
+            for r, value in forecast_rows(read, STEPS, span - STEPS, coefficients):
+                made.append((var, r, value))
+        pairs = []
+        for first in range(STEPS, span - STEPS, 2):
+            rows = [one for r in (first, first + 1) for _, at, one in made if at == r]
+            pairs.append(jnp.concatenate(rows, axis=0))
+        pack_rows(pairs, identity, staged.at[level], 0)
+        here = pl.ds(level * count * SPAN, count * SPAN)
+        leaving.append(pltpu.make_async_copy(staged.at[level], packed.at[:, here], out_sems.at[level]))
+        leaving[-1].start()
+        for var, r, value in made:
+            fields[level, r - STEPS, var * members : (var + 1) * members, :] = value
+        for var, r, rows in reads:
+            slabs[var, level, r] = rows
+    for copy in leaving:
+        copy.wait()
+
+
+def inner(own, raw, variables):
     lanes, levels, span, columns = own.shape
     members = lanes // variables
     blocks = columns // SPAN
     count = span - 2 * STEPS
+    fixed = [pltpu.with_memory_space_constraint(x, pltpu.HBM) for x in (own, *raw)]
     return pl.pallas_call(
         functools.partial(inner_kernel, variables),
-        grid=(levels,),
         out_shape=[
             jax.ShapeDtypeStruct((variables, levels, span, members, columns), jnp.float32),
             jax.ShapeDtypeStruct((levels, count, lanes, columns), jnp.bfloat16),
             jax.ShapeDtypeStruct((blocks, levels * count * SPAN, lanes), jnp.bfloat16),
-        ],
-        in_specs=[pl.BlockSpec((lanes, 1, span, columns), lambda level: (0, level, 0, 0))] + vmem(1),
-        out_specs=[
-            pl.BlockSpec((variables, 1, span, members, columns), lambda level: (0, level, 0, 0, 0)),
-            pl.BlockSpec((1, count, lanes, columns), lambda level: (level, 0, 0, 0)),
-            pl.BlockSpec((blocks, count * SPAN, lanes), lambda level: (0, level, 0)),
-        ],
-        compiler_params=params(50),
+            jax.ShapeDtypeStruct((levels, 5, 8, columns), jnp.float32),
+        ],
+        in_specs=hbm(4),
+        out_specs=vmem(2) + hbm(1) + vmem(1),
+        scratch_shapes=[
+            pltpu.VMEM(raw[0].shape, jnp.float32),
+            pltpu.SMEM(raw[1].shape, jnp.float32),
+            pltpu.SMEM(raw[2].shape, jnp.float32),
+            pltpu.VMEM((levels, lanes, span, columns), jnp.float32),
+            pltpu.VMEM((levels, blocks, count * SPAN, lanes), jnp.bfloat16),
+            pltpu.SemaphoreType.DMA((levels,)),
+            pltpu.SemaphoreType.DMA((3,)),
+            pltpu.SemaphoreType.DMA((levels,)),
+        ],
+        compiler_params=params(10),
         cost_estimate=cost(2 * 10**9, 4 * 2**20),
-    )(own, model)
+    )(*fixed)
 
 
 def outer_kernel(near, own, *rest):
@@ -200,7 +220,7 @@
 
     @pl.loop(0, levels)
     def _(level):
-        coefficients = coefficients_of(model, level)
+        coefficients = [model[level, i] for i in range(5)]
         made = []
         for var in range(variables):
             read = row_reader(level, var, own, sides[0], sides[-1])
@@ -458,9 +478,11 @@
     parts = ((first, 0, near, 0), (dev, 2 * near, far, near))
     for batch in batches(groups // 2, 2):
         made = []
+        wide = slice(batch[0] * lanes, (batch[-1] + 1) * lanes)
+        both = dot(mix, scaled_ref[:, wide]) + shift
         for j in batch:
             here = slice(j * lanes, (j + 1) * lanes)
-            new = dot(mix, scaled_ref[:, here]) + shift
+            new = both[:, (j - batch[0]) * lanes :][:, :lanes]
             for ref, at, size, row in parts:
                 one = new[at : at + 2 * size] + alpha * ref[:, here].astype(jnp.float32)
                 pair = join(one[:size], one[size:], left_lanes((size, lanes)), members)
@@ -541,9 +563,8 @@
 
 def on_device(start, diffusivity, eastward, northward, cells, count, value, weight):
     members, variables, levels, span, columns = dims = start.shape
-    model = model_rows(diffusivity, eastward, northward)
     whole = start.reshape(members * variables, levels, span, columns)
-    own, centre, near = inner(whole, model, variables)
+    own, centre, near, model = inner(whole, (diffusivity, eastward, northward), variables)
     sides = neighbours(own, "tile")
     first, means = prepare(exchange(near))
     grid, rim = outer(dims, own, sides, model, centre)

time: 93.8 us -> 92.4 us (0.985)
  transfers between devices with their start and end apart: 3 -> 3, of which waited for: 2 -> 2; matrix products, arithmetic and copies ran while one was open for 0% -> 0% of each run, Pallas kernels for 13% -> 14%
where the time goes in v1:
time: 92.4 us; the launch traced here: 92 us
  blocking collectives  30.6 us (33%)
  waiting for transfers between devices  26.2 us (28%)
  Pallas kernels  21.8 us (24%)
  starting transfers between devices  12.6 us (14%)
    all_to_all x1, blocking collectives, exchange(): lax.all_to_all(blocks, 'grp', split_axis=0, concat_axis=0, tiled=True)  30.6 us
    all_to_all x2, waiting for transfers between devices, exchange(): lax.all_to_all(blocks, 'grp', split_axis=0, concat_axis=0, tiled=True)  26.2 us
    all_to_all x2, starting transfers between devices, exchange(): lax.all_to_all(blocks, 'grp', split_axis=0, concat_axis=0, tiled=True)  12.1 us
    pallas_call x1, Pallas kernels, outer(): pl.pallas_call(functools.partial(outer_kernel, near), out_shape=[jax.Shap...  7.56 us
    pallas_call x1, Pallas kernels, pick(): pl.pallas_call(functools.partial(pick_kernel, variables, together), out_s...  4.54 us
    pallas_call x1, Pallas kernels, inner(): pl.pallas_call(functools.partial(inner_kernel, variables), out_shape=[jax...  4.3 us
    pallas_call x1, Pallas kernels, analyse(): pl.pallas_call(analyse_kernel, out_shape=jax.ShapeDtypeStruct((groups, ne...  2.94 us
    pallas_call x1, Pallas kernels, restore(): pl.pallas_call(restore_kernel, out_shape=jax.ShapeDtypeStruct((members, v...  2 us
  transfers between devices with their start and end apart: 3, of which 2 were waited for; matrix products, arithmetic and copies ran while one was open for 0% of the time, Pallas kernels for 14%

profile of v1, /device:TPU:0, one launch (start us, length us, event | category | flops | bytes accessed | tf_op | source)
XLA Modules:
  0.0 92.0 jit_solution(10463425625449941889)
XLA Ops:
  0.0 4.3 %shard_map.82 = (f32[2,4,8,64,128]{4,3,2,1,0:T(8,128)S(1)}, bf16[4,4,128,128]{3,2,1,0:T(8,128)(2,1)S(1)}, bf16[16,128,128]{2,1,0:T(8,128)(2,1)}, f32[4,5,8,128]{3,2,1,0:T(8,128)S(1)}) custom-call(f32[128,4,8,128]{3,2,1,0:T(8,128)} %bitcast.7, f32[4,128]{1,0:T(4,128)} %refs_0_.1, f32[4]{0:T(128)} %refs_1_.1, f32[4]{0:T(128)} %refs_2_.1), custom_call_target="tpu_custom_call" | custom-call | flops 2000000000 | bytes 4194304 | tf_op jit(solution)/shard_map/pallas_call | solution.py:182
  4.3 0.5 collective-permute-start
  4.8 7.9 %all-to-all-start = ((bf16[16,128,128]{2,1,0:T(8,128)(2,1)}), bf16[16,128,128]{2,1,0:T(8,128)(2,1)S(1)}, u32[]{:S(2)}, u32[]{:S(2)}) async-start(bf16[16,128,128]{2,1,0:T(8,128)(2,1)} %get-tuple-element.13), calls=%async_computation | async-start | bytes 1048576 | tf_op jit(solution)/shard_map/all_to_all | solution.py:561
  12.7 0.0 collective-permute-done.rest_0_
  12.7 0.0 copy-start
  12.7 7.6 %shard_map.84 = (bf16[4,8,256,128]{3,2,1,0:T(8,128)(2,1)S(1)}, bf16[16,128,128]{2,1,0:T(8,128)(2,1)S(1)}) custom-call(f32[2,4,8,64,128]{4,3,2,1,0:T(8,128)S(1)} %get-tuple-element.16.own, f32[2,4,8,64,128]{4,3,2,1,0:T(8,128)} %collective-permute-done.rest_0_, f32[4,5,8,128]{3,2,1,0:T(8,128)S(1)} %get-tuple-element.17.rest_1_, ...), custom_call_target="tpu_custom_call" | custom-call | flops 2000000000 | bytes 8388608 | tf_op jit(solution)/shard_map/pallas_call | solution.py:253
  20.3 0.0 copy-done
  20.3 4.5 %shard_map.85 = bf16[16,256,128]{2,1,0:T(8,128)(2,1)} custom-call(bf16[4,8,256,128]{3,2,1,0:T(8,128)(2,1)S(1)} %get-tuple-element.19.grid, bf16[16,128,128]{2,1,0:T(8,128)(2,1)S(1)} %get-tuple-element.20.rim, s32[16,256]{1,0:T(8,128)S(1)} %bitcast.4), custom_call_target="tpu_custom_call" | custom-call | flops 4000000000 | bytes 4194304 | tf_op jit(solution)/shard_map/pallas_call | solution.py:336
  24.9 0.0 copy-start.1
  24.9 0.0 copy-start.2
  24.9 3.3 %all-to-all-done.states = bf16[16,128,128]{2,1,0:T(8,128)(2,1)S(1)} async-done(((bf16[16,128,128]{2,1,0:T(8,128)(2,1)}), bf16[16,128,128]{2,1,0:T(8,128)(2,1)S(1)}, u32[]{:S(2)}, u32[]{:S(2)}) %all-to-all-start) | async-done | bytes 524320 | tf_op jit(solution)/shard_map/all_to_all | solution.py:561
  28.2 4.2 %all-to-all-start.1 = ((bf16[16,256,128]{2,1,0:T(8,128)(2,1)}), bf16[16,256,128]{2,1,0:T(8,128)(2,1)S(1)}, u32[]{:S(2)}, u32[]{:S(2)}) async-start(bf16[16,256,128]{2,1,0:T(8,128)(2,1)} %shard_map.85), calls=%async_computation.1 | async-start | bytes 2097152 | tf_op jit(solution)/shard_map/all_to_all | solution.py:561
  33.1 0.4 shard_map.83
  33.5 22.9 %all-to-all-done.1.second = bf16[16,256,128]{2,1,0:T(8,128)(2,1)S(1)} async-done(((bf16[16,256,128]{2,1,0:T(8,128)(2,1)}), bf16[16,256,128]{2,1,0:T(8,128)(2,1)S(1)}, u32[]{:S(2)}, u32[]{:S(2)}) %all-to-all-start.1) | async-done | bytes 1048608 | tf_op jit(solution)/shard_map/all_to_all | solution.py:561
  56.4 0.0 copy-done.1
  56.4 0.0 copy-done.2
  56.4 2.9 %shard_map.86 = bf16[16,256,128]{2,1,0:T(8,128)(2,1)S(1)} custom-call(bf16[256,1024]{1,0:T(8,128)(2,1)S(1)} %get-tuple-element.14.first, f32[256,128]{1,0:T(8,128)S(1)} %get-tuple-element.15.means, bf16[16,256,128]{2,1,0:T(8,128)(2,1)S(1)} %all-to-all-done.1.second, s32[1,1]{1,0:T(1,128)S(6)} %copy.9.count, f32[1,256]{1,0:T(1,128)S(1)} %bitcast.5, ...), custom_call_target="tpu_custom_call" | custom-call | flops 4000000000 | bytes 4194304 | tf_op jit(solution)/shard_map/pallas_call | solution.py:500
  59.4 30.6 %all_to_all.15.blocks = bf16[16,256,128]{2,1,0:T(8,128)(2,1)S(1)} all-to-all(bf16[16,256,128]{2,1,0:T(8,128)(2,1)S(1)} %shard_map.86), channel_id=1, replica_groups=mesh['grp'=16,'tile'=2] {'grp'}, dimensions={0} | all-to-all | bytes 2097152 | tf_op jit(solution)/shard_map/all_to_all | solution.py:561
  90.0 2.0 %shard_map.87 = bf16[64,2,4,8,128]{4,3,2,1,0:T(8,128)(2,1)} custom-call(bf16[16,256,128]{2,1,0:T(8,128)(2,1)S(1)} %all_to_all.15.blocks), custom_call_target="tpu_custom_call" | custom-call | flops 2000000000 | bytes 2097152 | tf_op jit(solution)/shard_map/pallas_call | solution.py:541
Async XLA Ops:
  4.3 8.4 %collective-permute-start = (f32[2,4,8,64,128]{4,3,2,1,0:T(8,128)S(1)}, f32[2,4,8,64,128]{4,3,2,1,0:T(8,128)}, u32[]{:S(2)}, u32[]{:S(2)}) collective-permute-start(f32[2,4,8,64,128]{4,3,2,1,0:T(8,128)S(1)} %get-tuple-element.16.own), channel_id=1, source_target_pairs={{0,1},{1,0},{2,3},{3,2},{4,5},{5,4},{6,7},{7,6},{8,9},{9,8},{10,11... | collective-permute-start | bytes 6291464 | tf_op jit(solution)/shard_map/ppermute | solution.py:554
  4.8 23.4 %all-to-all-start = ((bf16[16,128,128]{2,1,0:T(8,128)(2,1)}), bf16[16,128,128]{2,1,0:T(8,128)(2,1)S(1)}, u32[]{:S(2)}, u32[]{:S(2)}) async-start(bf16[16,128,128]{2,1,0:T(8,128)(2,1)} %get-tuple-element.13), calls=%async_computation | async-start | bytes 1048576 | tf_op jit(solution)/shard_map/all_to_all | solution.py:561
  12.7 7.6 %copy-start = (s32[1,16,256]{2,1,0:T(8,128)S(1)}, s32[1,16,256]{2,1,0:T(8,128)}, u32[]{:S(2)}) copy-start(s32[1,16,256]{2,1,0:T(8,128)} %param.12) | copy-start | bytes 49156
  24.9 31.6 %copy-start.1 = (f32[1,1,256]{2,1,0:T(1,128)S(1)}, f32[1,1,256]{2,1,0:T(1,128)}, u32[]{:S(2)}) copy-start(f32[1,1,256]{2,1,0:T(1,128)} %param.14) | copy-start | bytes 3076
  24.9 31.6 %copy-start.2 = (f32[1,1,256]{2,1,0:T(1,128)S(1)}, f32[1,1,256]{2,1,0:T(1,128)}, u32[]{:S(2)}) copy-start(f32[1,1,256]{2,1,0:T(1,128)} %param.15) | copy-start | bytes 3076
  28.2 28.2 %all-to-all-start.1 = ((bf16[16,256,128]{2,1,0:T(8,128)(2,1)}), bf16[16,256,128]{2,1,0:T(8,128)(2,1)S(1)}, u32[]{:S(2)}, u32[]{:S(2)}) async-start(bf16[16,256,128]{2,1,0:T(8,128)(2,1)} %shard_map.85), calls=%async_computation.1 | async-start | bytes 2097152 | tf_op jit(solution)/shard_map/all_to_all | solution.py:561

commit v2 on v1

--- a/solution.py
+++ b/solution.py
@@ -41,11 +41,6 @@
 def split(x):
     high = x.astype(jnp.bfloat16)
     return high, (x - high.astype(jnp.float32)).astype(jnp.bfloat16)
-
-
-def dot3(a, b):
-    (a_high, a_low), (b_high, b_low) = split(a), split(b)
-    return dot(a_high, b_high) + (dot(a_high, b_low) + dot(a_low, b_high))
 
 
 def dot_rows(a, b):
@@ -131,10 +126,15 @@
     members = lanes // variables
     count = span - 2 * STEPS
     copies = [pltpu.make_async_copy(x, y, raw_sems.at[i]) for i, (x, y) in enumerate(zip(raw, local))]
-    arrivals = [
-        pltpu.make_async_copy(own.at[:, level], whole.at[level], in_sems.at[level])
-        for level in range(levels)
-    ]
+    together = whole.shape[2]
+    arrivals = []
+    for i in range(levels // together):
+        for part in range(2):
+            here = pl.ds(part * (lanes // 2), lanes // 2)
+            source = own.at[here, pl.ds(i * together, together)]
+            arrivals.append(
+                pltpu.make_async_copy(source, whole.at[i, here], in_sems.at[2 * i + part])
+            )
     for copy in copies + arrivals:
         copy.start()
     for copy in copies:
@@ -145,13 +145,17 @@
         coefficients = coefficients_of(level, *local)
         for i, one in enumerate(coefficients):
             model[level, i] = one
-        arrivals[level].wait()
-        view = whole.at[level].reshape(lanes * span, columns)
+        step, inside = divmod(level, together)
+        if inside == 0:
+            arrivals[2 * step].wait()
+            arrivals[2 * step + 1].wait()
+        view = whole.at[step].reshape(lanes * together * span, columns)
         reads, made = [], []
         for var in range(variables):
 
             def read(r):
-                rows = view[pl.ds(var * span + r, members, stride=variables * span), :]
+                at = (var * together + inside) * span + r
+                rows = view[pl.ds(at, members, stride=variables * together * span), :]
                 reads.append((var, r, rows))
                 return rows.reshape(-1, 8, columns)
 
@@ -178,6 +182,7 @@
     members = lanes // variables
     blocks = columns // SPAN
     count = span - 2 * STEPS
+    together = 2 if levels % 2 == 0 else 1
     fixed = [pltpu.with_memory_space_constraint(x, pltpu.HBM) for x in (own, *raw)]
     return pl.pallas_call(
         functools.partial(inner_kernel, variables),
@@ -193,9 +198,9 @@
             pltpu.VMEM(raw[0].shape, jnp.float32),
             pltpu.SMEM(raw[1].shape, jnp.float32),
             pltpu.SMEM(raw[2].shape, jnp.float32),
-            pltpu.VMEM((levels, lanes, span, columns), jnp.float32),
+            pltpu.VMEM((levels // together, lanes, together, span, columns), jnp.float32),
             pltpu.VMEM((levels, blocks, count * SPAN, lanes), jnp.bfloat16),
-            pltpu.SemaphoreType.DMA((levels,)),
+            pltpu.SemaphoreType.DMA((2 * levels // together,)),
             pltpu.SemaphoreType.DMA((3,)),
             pltpu.SemaphoreType.DMA((levels,)),
         ],
@@ -457,8 +462,9 @@
     q2 = -0.5 * (0.75 * p - 0.125 * a)
     small = dot_rows(scaled_ref[...], scaled_ref[...]) * inverse
     diagonal = eye(slots)
-    square = dot3(small, small)
-    tail = dot3(square, jnp.where(diagonal, q2, 0.0) + 0.0625 * small)
+    once = small.astype(jnp.bfloat16)
+    square = dot(once, once).astype(jnp.bfloat16)
+    tail = dot(square, (jnp.where(diagonal, q2, 0.0) + 0.0625 * small).astype(jnp.bfloat16))
     poly = jnp.where(diagonal, q0, 0.0) + q1 * small + tail
 
     def apply(vector):
@@ -474,7 +480,9 @@
     )
     centre = jnp.concatenate([means[:, 0:1], centre], axis=0)
     shift = centre + jnp.sum(cross * gain, axis=1, keepdims=True)
-    mix = (dot3(cross, poly) * factor).astype(jnp.bfloat16)
+    once = cross.astype(jnp.bfloat16)
+    mix = sum(dot(once, part) for part in split(poly))
+    mix = (mix * factor).astype(jnp.bfloat16)
     parts = ((first, 0, near, 0), (dev, 2 * near, far, near))
     for batch in batches(groups // 2, 2):
         made = []

time: 92.4 us -> 92.4 us (level)
  no operation moved by 1% of the time
where the time goes in v2:
time: 92.4 us; the launch traced here: 92 us
  blocking collectives  30.6 us (33%)
  waiting for transfers between devices  26.2 us (28%)
  Pallas kernels  21.8 us (24%)
  starting transfers between devices  12.6 us (14%)
    all_to_all x1, blocking collectives, exchange(): lax.all_to_all(blocks, 'grp', split_axis=0, concat_axis=0, tiled=True)  30.6 us
    all_to_all x2, waiting for transfers between devices, exchange(): lax.all_to_all(blocks, 'grp', split_axis=0, concat_axis=0, tiled=True)  26.2 us
    all_to_all x2, starting transfers between devices, exchange(): lax.all_to_all(blocks, 'grp', split_axis=0, concat_axis=0, tiled=True)  12.1 us
    pallas_call x1, Pallas kernels, outer(): pl.pallas_call(functools.partial(outer_kernel, near), out_shape=[jax.Shap...  7.56 us
    pallas_call x1, Pallas kernels, inner(): pl.pallas_call(functools.partial(inner_kernel, variables), out_shape=[jax...  4.58 us
    pallas_call x1, Pallas kernels, pick(): pl.pallas_call(functools.partial(pick_kernel, variables, together), out_s...  4.53 us
    pallas_call x1, Pallas kernels, analyse(): pl.pallas_call(analyse_kernel, out_shape=jax.ShapeDtypeStruct((groups, ne...  2.7 us
    pallas_call x1, Pallas kernels, restore(): pl.pallas_call(restore_kernel, out_shape=jax.ShapeDtypeStruct((members, v...  1.99 us
  transfers between devices with their start and end apart: 3, of which 2 were waited for; matrix products, arithmetic and copies ran while one was open for 0% of the time, Pallas kernels for 14%

profile of v2, /device:TPU:0, one launch (start us, length us, event | category | flops | bytes accessed | tf_op | source)
XLA Modules:
  0.0 92.0 jit_solution(1257484999266784994)
XLA Ops:
  0.0 4.6 %shard_map.82 = (f32[2,4,8,64,128]{4,3,2,1,0:T(8,128)S(1)}, bf16[4,4,128,128]{3,2,1,0:T(8,128)(2,1)S(1)}, bf16[16,128,128]{2,1,0:T(8,128)(2,1)}, f32[4,5,8,128]{3,2,1,0:T(8,128)S(1)}) custom-call(f32[128,4,8,128]{3,2,1,0:T(8,128)} %bitcast.7, f32[4,128]{1,0:T(4,128)} %refs_0_.1, f32[4]{0:T(128)} %refs_1_.1, f32[4]{0:T(128)} %refs_2_.1), custom_call_target="tpu_custom_call" | custom-call | flops 2000000000 | bytes 4194304 | tf_op jit(solution)/shard_map/pallas_call | solution.py:187
  4.6 0.5 collective-permute-start
  5.1 7.9 %all-to-all-start = ((bf16[16,128,128]{2,1,0:T(8,128)(2,1)}), bf16[16,128,128]{2,1,0:T(8,128)(2,1)S(1)}, u32[]{:S(2)}, u32[]{:S(2)}) async-start(bf16[16,128,128]{2,1,0:T(8,128)(2,1)} %get-tuple-element.13), calls=%async_computation | async-start | bytes 1048576 | tf_op jit(solution)/shard_map/all_to_all | solution.py:569
  13.0 0.0 collective-permute-done.rest_0_
  13.0 0.0 copy-start
  13.0 7.6 %shard_map.84 = (bf16[4,8,256,128]{3,2,1,0:T(8,128)(2,1)S(1)}, bf16[16,128,128]{2,1,0:T(8,128)(2,1)S(1)}) custom-call(f32[2,4,8,64,128]{4,3,2,1,0:T(8,128)S(1)} %get-tuple-element.16.own, f32[2,4,8,64,128]{4,3,2,1,0:T(8,128)} %collective-permute-done.rest_0_, f32[4,5,8,128]{3,2,1,0:T(8,128)S(1)} %get-tuple-element.17.rest_1_, ...), custom_call_target="tpu_custom_call" | custom-call | flops 2000000000 | bytes 8388608 | tf_op jit(solution)/shard_map/pallas_call | solution.py:258
  20.6 0.0 copy-done
  20.6 4.5 %shard_map.85 = bf16[16,256,128]{2,1,0:T(8,128)(2,1)} custom-call(bf16[4,8,256,128]{3,2,1,0:T(8,128)(2,1)S(1)} %get-tuple-element.19.grid, bf16[16,128,128]{2,1,0:T(8,128)(2,1)S(1)} %get-tuple-element.20.rim, s32[16,256]{1,0:T(8,128)S(1)} %bitcast.4), custom_call_target="tpu_custom_call" | custom-call | flops 4000000000 | bytes 4194304 | tf_op jit(solution)/shard_map/pallas_call | solution.py:341
  25.1 0.0 copy-start.1
  25.1 0.0 copy-start.2
  25.1 3.3 %all-to-all-done.states = bf16[16,128,128]{2,1,0:T(8,128)(2,1)S(1)} async-done(((bf16[16,128,128]{2,1,0:T(8,128)(2,1)}), bf16[16,128,128]{2,1,0:T(8,128)(2,1)S(1)}, u32[]{:S(2)}, u32[]{:S(2)}) %all-to-all-start) | async-done | bytes 524320 | tf_op jit(solution)/shard_map/all_to_all | solution.py:569
  28.5 4.2 %all-to-all-start.1 = ((bf16[16,256,128]{2,1,0:T(8,128)(2,1)}), bf16[16,256,128]{2,1,0:T(8,128)(2,1)S(1)}, u32[]{:S(2)}, u32[]{:S(2)}) async-start(bf16[16,256,128]{2,1,0:T(8,128)(2,1)} %shard_map.85), calls=%async_computation.1 | async-start | bytes 2097152 | tf_op jit(solution)/shard_map/all_to_all | solution.py:569
  33.3 0.4 shard_map.83
  33.8 22.9 %all-to-all-done.1.second = bf16[16,256,128]{2,1,0:T(8,128)(2,1)S(1)} async-done(((bf16[16,256,128]{2,1,0:T(8,128)(2,1)}), bf16[16,256,128]{2,1,0:T(8,128)(2,1)S(1)}, u32[]{:S(2)}, u32[]{:S(2)}) %all-to-all-start.1) | async-done | bytes 1048608 | tf_op jit(solution)/shard_map/all_to_all | solution.py:569
  56.7 0.0 copy-done.1
  56.7 0.0 copy-done.2
  56.7 2.7 %shard_map.86 = bf16[16,256,128]{2,1,0:T(8,128)(2,1)S(1)} custom-call(bf16[256,1024]{1,0:T(8,128)(2,1)S(1)} %get-tuple-element.14.first, f32[256,128]{1,0:T(8,128)S(1)} %get-tuple-element.15.means, bf16[16,256,128]{2,1,0:T(8,128)(2,1)S(1)} %all-to-all-done.1.second, s32[1,1]{1,0:T(1,128)S(6)} %copy.9.count, f32[1,256]{1,0:T(1,128)S(1)} %bitcast.5, ...), custom_call_target="tpu_custom_call" | custom-call | flops 4000000000 | bytes 4194304 | tf_op jit(solution)/shard_map/pallas_call | solution.py:508
  59.4 30.6 %all_to_all.15.blocks = bf16[16,256,128]{2,1,0:T(8,128)(2,1)S(1)} all-to-all(bf16[16,256,128]{2,1,0:T(8,128)(2,1)S(1)} %shard_map.86), channel_id=1, replica_groups=mesh['grp'=16,'tile'=2] {'grp'}, dimensions={0} | all-to-all | bytes 2097152 | tf_op jit(solution)/shard_map/all_to_all | solution.py:569
  90.0 2.0 %shard_map.87 = bf16[64,2,4,8,128]{4,3,2,1,0:T(8,128)(2,1)} custom-call(bf16[16,256,128]{2,1,0:T(8,128)(2,1)S(1)} %all_to_all.15.blocks), custom_call_target="tpu_custom_call" | custom-call | flops 2000000000 | bytes 2097152 | tf_op jit(solution)/shard_map/pallas_call | solution.py:549
Async XLA Ops:
  4.6 8.4 %collective-permute-start = (f32[2,4,8,64,128]{4,3,2,1,0:T(8,128)S(1)}, f32[2,4,8,64,128]{4,3,2,1,0:T(8,128)}, u32[]{:S(2)}, u32[]{:S(2)}) collective-permute-start(f32[2,4,8,64,128]{4,3,2,1,0:T(8,128)S(1)} %get-tuple-element.16.own), channel_id=1, source_target_pairs={{0,1},{1,0},{2,3},{3,2},{4,5},{5,4},{6,7},{7,6},{8,9},{9,8},{10,11... | collective-permute-start | bytes 6291464 | tf_op jit(solution)/shard_map/ppermute | solution.py:562
  5.1 23.4 %all-to-all-start = ((bf16[16,128,128]{2,1,0:T(8,128)(2,1)}), bf16[16,128,128]{2,1,0:T(8,128)(2,1)S(1)}, u32[]{:S(2)}, u32[]{:S(2)}) async-start(bf16[16,128,128]{2,1,0:T(8,128)(2,1)} %get-tuple-element.13), calls=%async_computation | async-start | bytes 1048576 | tf_op jit(solution)/shard_map/all_to_all | solution.py:569
  13.0 7.6 %copy-start = (s32[1,16,256]{2,1,0:T(8,128)S(1)}, s32[1,16,256]{2,1,0:T(8,128)}, u32[]{:S(2)}) copy-start(s32[1,16,256]{2,1,0:T(8,128)} %param.12) | copy-start | bytes 49156
  25.1 31.6 %copy-start.1 = (f32[1,1,256]{2,1,0:T(1,128)S(1)}, f32[1,1,256]{2,1,0:T(1,128)}, u32[]{:S(2)}) copy-start(f32[1,1,256]{2,1,0:T(1,128)} %param.14) | copy-start | bytes 3076
  25.1 31.6 %copy-start.2 = (f32[1,1,256]{2,1,0:T(1,128)S(1)}, f32[1,1,256]{2,1,0:T(1,128)}, u32[]{:S(2)}) copy-start(f32[1,1,256]{2,1,0:T(1,128)} %param.15) | copy-start | bytes 3076
  28.5 28.2 %all-to-all-start.1 = ((bf16[16,256,128]{2,1,0:T(8,128)(2,1)}), bf16[16,256,128]{2,1,0:T(8,128)(2,1)S(1)}, u32[]{:S(2)}, u32[]{:S(2)}) async-start(bf16[16,256,128]{2,1,0:T(8,128)(2,1)} %shard_map.85), calls=%async_computation.1 | async-start | bytes 2097152 | tf_op jit(solution)/shard_map/all_to_all | solution.py:569

commit v3 on v2

--- a/solution.py
+++ b/solution.py
@@ -182,7 +182,7 @@
     members = lanes // variables
     blocks = columns // SPAN
     count = span - 2 * STEPS
-    together = 2 if levels % 2 == 0 else 1
+    together = 1
     fixed = [pltpu.with_memory_space_constraint(x, pltpu.HBM) for x in (own, *raw)]
     return pl.pallas_call(
         functools.partial(inner_kernel, variables),
@@ -211,15 +211,21 @@
 
 def outer_kernel(near, own, *rest):
     sides, rest = rest[:near], rest[near:]
-    model, centre, grid, packed, fields, sems = rest
+    model, centre, grid, packed, staged, sems, out_sems = rest
     variables, levels, span, members, columns = own.shape
-    rows = variables * members
+    rows_each = variables * members
     pairs = (2 * EDGE + span) // 2
+    size = STEPS * 2 * SPAN
+    identity = permutation(columns, 0)
+
+    def leave(level):
+        here = pl.ds(pl.multiple_of(level * size, size), size)
+        return pltpu.make_async_copy(staged.at[level], packed.at[:, here], out_sems.at[level])
 
     copies = []
     for r in range(STEPS, span - STEPS):
         half, pair = divmod(r + EDGE, pairs)
-        place = grid.at[:, pair, pl.ds(half * rows, rows)]
+        place = grid.at[:, pair, pl.ds(half * rows_each, rows_each)]
         copies.append(pltpu.make_async_copy(centre.at[:, r - STEPS], place, sems.at[r - STEPS]))
         copies[-1].start()
 
@@ -232,24 +238,24 @@
             for first, last in ((-EDGE, STEPS), (span - STEPS, span + EDGE)):
                 for r, value in forecast_rows(read, first, last, coefficients):
                     made.append((var, r, value))
+        sheets = []
+        for first in (0, span - STEPS):
+            rows = [one for r in range(first, first + STEPS) for _, at, one in made if at == r]
+            sheets.append(jnp.concatenate(rows, axis=0))
+        pack_rows(sheets, identity, staged.at[level], 0)
+        leave(level).start()
         for var, r, value in made:
             half, pair = divmod(r + EDGE, pairs)
-            at = half * rows + var * members
+            at = half * rows_each + var * members
             grid[level, pair, at : at + members, :] = value
-            if 0 <= r < span:
-                pair, half = divmod(r if r < STEPS else r - span + 2 * STEPS, 2)
-                at = half * rows + var * members
-                fields[level, pair, at : at + members, :] = value
-
-    identity = permutation(columns, 0)
-    for level in range(0, levels, 2):
-        batch = [fields[at, pair] for at in range(level, min(levels, level + 2)) for pair in range(STEPS)]
-        pack_rows(batch, identity, packed, level * STEPS * 2 * SPAN)
+
+    for level in range(levels):
+        leave(level).wait()
     for copy in copies:
         copy.wait()
 
 
-def outer(dims, own, sides, model, centre):
+def outer(dims, own, sides, model, centre, slots):
     members, variables, levels, span, columns = dims
     lanes = members * variables
     blocks = columns // SPAN
@@ -259,20 +265,23 @@
         functools.partial(outer_kernel, near),
         out_shape=[
             jax.ShapeDtypeStruct((levels, pairs, 2 * lanes, columns), jnp.bfloat16),
-            jax.ShapeDtypeStruct((blocks, levels * 2 * STEPS * SPAN, lanes), jnp.bfloat16),
+            jax.ShapeDtypeStruct(
+                (blocks, levels * 2 * STEPS * SPAN + slots // 2, lanes), jnp.bfloat16
+            ),
         ],
         in_specs=vmem(2 + near) + hbm(1),
-        out_specs=vmem(2),
+        out_specs=vmem(1) + hbm(1),
         scratch_shapes=[
-            pltpu.VMEM((levels, STEPS, 2 * lanes, columns), jnp.bfloat16),
+            pltpu.VMEM((levels, blocks, 2 * STEPS * SPAN, lanes), jnp.bfloat16),
             pltpu.SemaphoreType.DMA((span - 2 * STEPS,)),
+            pltpu.SemaphoreType.DMA((levels,)),
         ],
         compiler_params=params(16),
         cost_estimate=cost(2 * 10**9, 8 * 2**20),
     )(own, *sides, model, centre)
 
 
-def pick_kernel(variables, together, grid, rim, cells, out, region, codes):
+def pick_kernel(variables, together, grid, _, cells, out, region, codes, staged, sems):
     levels, pairs, twice, columns = grid.shape
     rows = twice // 2
     members = rows // variables
@@ -280,23 +289,23 @@
     width = 2 * EDGE + SPAN
     part = pairs * width
     entries = levels * part
-    share = rim.shape[1]
-
-    orders = jnp.concatenate(
-        [permutation(columns, -EDGE), permutation(columns, SPAN - EDGE)], axis=0
-    )
+    share = out.shape[1] - slots // 2
+
+    order = permutation(columns, -EDGE)
     batch = next(n for n in (4, 2, 1) if pairs % n == 0)
     for level in range(levels):
         for start in range(0, pairs, batch):
-            turned = [
-                dot_rows(orders, grid[level, start + i]).astype(jnp.bfloat16) for i in range(batch)
-            ]
-            for i, value in enumerate(turned):
+            made = []
+            for i in range(batch):
+                even = dot_rows(order, grid[level, start + i])
+                odd = jnp.concatenate([even[SPAN:], even[:SPAN]], axis=0)
+                made.append((even.astype(jnp.bfloat16), odd.astype(jnp.bfloat16)))
+            for i, both in enumerate(made):
                 at = (level * pairs + start + i) * width
-                for first in range(2):
+                for first, value in enumerate(both):
                     for j in range(columns // width):
-                        row = first * columns + j * width
-                        region[2 * j + first, at : at + width, :] = value[row : row + width, :]
+                        piece = value[j * width : (j + 1) * width, :]
+                        region[2 * j + first, at : at + width, :] = piece
 
     cell = cells[...]
     second = cell >= 2 * entries
@@ -309,6 +318,11 @@
 
     left = lax.broadcasted_iota(jnp.int32, (slots // 2, rows), 1) < members
     lane = lax.broadcasted_iota(jnp.int32, (slots, entries), 1).astype(jnp.float32)
+
+    def leave(step):
+        here = pl.ds(step * together, together)
+        place = out.at[here, pl.ds(share, slots // 2)]
+        return pltpu.make_async_copy(staged.at[here], place, sems.at[step])
 
     @pl.loop(0, blocks // together)
     def _(step):
@@ -328,28 +342,32 @@
             to_right = jnp.where(second, total, other)[slots // 2 :]
             made.append(jnp.where(left, to_left, to_right).astype(jnp.bfloat16))
         for i, value in enumerate(made):
-            block = step * together + i
-            out[block, share:, :] = value
-            out[block, :share, :] = rim[block]
-
-
-def pick(variables, grid, rim, cells):
+            staged[step * together + i] = value
+        leave(step).start()
+
+    for step in range(blocks // together):
+        leave(step).wait()
+
+
+def pick(variables, grid, packed, cells):
     levels, pairs, twice, columns = grid.shape
     blocks, slots = cells.shape
-    _, share, lanes = rim.shape
     together = next(n for n in (4, 2, 1) if blocks % n == 0)
     return pl.pallas_call(
         functools.partial(pick_kernel, variables, together),
-        out_shape=jax.ShapeDtypeStruct((blocks, share + slots // 2, lanes), jnp.bfloat16),
-        in_specs=vmem(3),
-        out_specs=pl.BlockSpec(memory_space=pltpu.VMEM),
+        out_shape=jax.ShapeDtypeStruct(packed.shape, packed.dtype),
+        in_specs=vmem(1) + hbm(1) + vmem(1),
+        out_specs=pl.BlockSpec(memory_space=pltpu.HBM),
         scratch_shapes=[
             pltpu.VMEM((blocks, levels * pairs * (2 * EDGE + SPAN), twice), jnp.bfloat16),
             pltpu.VMEM((blocks, slots), jnp.float32),
+            pltpu.VMEM((blocks, slots // 2, packed.shape[2]), jnp.bfloat16),
+            pltpu.SemaphoreType.DMA((blocks // together,)),
         ],
+        input_output_aliases={1: 0},
         compiler_params=params(20),
         cost_estimate=cost(4 * 10**9, 4 * 2**20),
-    )(grid, rim, cells)
+    )(grid, packed, cells)
 
 
 def join(a, b, left, members):
@@ -575,8 +593,8 @@
     own, centre, near, model = inner(whole, (diffusivity, eastward, northward), variables)
     sides = neighbours(own, "tile")
     first, means = prepare(exchange(near))
-    grid, rim = outer(dims, own, sides, model, centre)
-    second = exchange(pick(variables, grid, rim, cells[0]))
+    grid, packed = outer(dims, own, sides, model, centre, cells.shape[2])
+    second = exchange(pick(variables, grid, packed, cells[0]))
     updated = analyse(first, means, second, count, value[0], weight[0])
     return restore(dims, exchange(updated))
 

time: 92.4 us -> 91.9 us (level)
  transfers between devices with their start and end apart: 3 -> 3, of which waited for: 2 -> 2; matrix products, arithmetic and copies ran while one was open for 0% -> 0% of each run, Pallas kernels for 14% -> 13%
where the time goes in v3:
time: 91.9 us; the launch traced here: 91.5 us
  blocking collectives  30.6 us (33%)
  waiting for transfers between devices  26.4 us (29%)
  Pallas kernels  21.2 us (23%)
  starting transfers between devices  12.6 us (14%)
    all_to_all x1, blocking collectives, exchange(): lax.all_to_all(blocks, 'grp', split_axis=0, concat_axis=0, tiled=True)  30.6 us
    all_to_all x2, waiting for transfers between devices, exchange(): lax.all_to_all(blocks, 'grp', split_axis=0, concat_axis=0, tiled=True)  26.4 us
    all_to_all x2, starting transfers between devices, exchange(): lax.all_to_all(blocks, 'grp', split_axis=0, concat_axis=0, tiled=True)  12.1 us
    pallas_call x1, Pallas kernels, outer(): pl.pallas_call(functools.partial(outer_kernel, near), out_shape=[jax.Shap...  7.89 us
    pallas_call x1, Pallas kernels, inner(): pl.pallas_call(functools.partial(inner_kernel, variables), out_shape=[jax...  4.43 us
    pallas_call x1, Pallas kernels, pick(): pl.pallas_call(functools.partial(pick_kernel, variables, together), out_s...  3.74 us
    pallas_call x1, Pallas kernels, analyse(): pl.pallas_call(analyse_kernel, out_shape=jax.ShapeDtypeStruct((groups, ne...  2.7 us
    pallas_call x1, Pallas kernels, restore(): pl.pallas_call(restore_kernel, out_shape=jax.ShapeDtypeStruct((members, v...  1.99 us
  transfers between devices with their start and end apart: 3, of which 2 were waited for; matrix products, arithmetic and copies ran while one was open for 0% of the time, Pallas kernels for 13%

profile of v3, /device:TPU:0, one launch (start us, length us, event | category | flops | bytes accessed | tf_op | source)
XLA Modules:
  0.0 91.5 jit_solution(9855308616847999778)
XLA Ops:
  0.0 4.4 %shard_map.82 = (f32[2,4,8,64,128]{4,3,2,1,0:T(8,128)S(1)}, bf16[4,4,128,128]{3,2,1,0:T(8,128)(2,1)S(1)}, bf16[16,128,128]{2,1,0:T(8,128)(2,1)}, f32[4,5,8,128]{3,2,1,0:T(8,128)S(1)}) custom-call(f32[128,4,8,128]{3,2,1,0:T(8,128)} %bitcast.7, f32[4,128]{1,0:T(4,128)} %refs_0_.1, f32[4]{0:T(128)} %refs_1_.1, f32[4]{0:T(128)} %refs_2_.1), custom_call_target="tpu_custom_call" | custom-call | flops 2000000000 | bytes 4194304 | tf_op jit(solution)/shard_map/pallas_call | solution.py:187
  4.4 0.5 collective-permute-start
  5.0 7.9 %all-to-all-start = ((bf16[16,128,128]{2,1,0:T(8,128)(2,1)}), bf16[16,128,128]{2,1,0:T(8,128)(2,1)S(1)}, u32[]{:S(2)}, u32[]{:S(2)}) async-start(bf16[16,128,128]{2,1,0:T(8,128)(2,1)} %get-tuple-element.13), calls=%async_computation | async-start | bytes 1048576 | tf_op jit(solution)/shard_map/all_to_all | solution.py:587
  12.9 0.0 collective-permute-done.rest_0_
  12.9 0.0 copy-start
  12.9 7.9 %shard_map.84 = (bf16[4,8,256,128]{3,2,1,0:T(8,128)(2,1)S(1)}, bf16[16,256,128]{2,1,0:T(8,128)(2,1)}) custom-call(f32[2,4,8,64,128]{4,3,2,1,0:T(8,128)S(1)} %get-tuple-element.16.own, f32[2,4,8,64,128]{4,3,2,1,0:T(8,128)} %collective-permute-done.rest_0_, f32[4,5,8,128]{3,2,1,0:T(8,128)S(1)} %get-tuple-element.17.rest_1_, ...), custom_call_target="tpu_custom_call" | custom-call | flops 2000000000 | bytes 8388608 | tf_op jit(solution)/shard_map/pallas_call | solution.py:264
  20.8 0.0 copy-done
  20.8 3.7 %shard_map.85 = bf16[16,256,128]{2,1,0:T(8,128)(2,1)} custom-call(bf16[4,8,256,128]{3,2,1,0:T(8,128)(2,1)S(1)} %get-tuple-element.19.grid, bf16[16,256,128]{2,1,0:T(8,128)(2,1)} %get-tuple-element.20._, s32[16,256]{1,0:T(8,128)S(1)} %bitcast.4), custom_call_target="tpu_custom_call", output_to_operand_aliasing={{}: (1, {})} | custom-call | flops 4000000000 | bytes 4194304 | tf_op jit(solution)/shard_map/pallas_call | solution.py:356
  24.5 0.0 copy-start.1
  24.5 0.0 copy-start.2
  24.6 3.8 %all-to-all-done.states = bf16[16,128,128]{2,1,0:T(8,128)(2,1)S(1)} async-done(((bf16[16,128,128]{2,1,0:T(8,128)(2,1)}), bf16[16,128,128]{2,1,0:T(8,128)(2,1)S(1)}, u32[]{:S(2)}, u32[]{:S(2)}) %all-to-all-start) | async-done | bytes 524320 | tf_op jit(solution)/shard_map/all_to_all | solution.py:587
  28.3 4.2 %all-to-all-start.1 = ((bf16[16,256,128]{2,1,0:T(8,128)(2,1)}), bf16[16,256,128]{2,1,0:T(8,128)(2,1)S(1)}, u32[]{:S(2)}, u32[]{:S(2)}) async-start(bf16[16,256,128]{2,1,0:T(8,128)(2,1)} %shard_map.85), calls=%async_computation.1 | async-start | bytes 2097152 | tf_op jit(solution)/shard_map/all_to_all | solution.py:587
  33.2 0.4 shard_map.83
  33.6 22.6 %all-to-all-done.1.second = bf16[16,256,128]{2,1,0:T(8,128)(2,1)S(1)} async-done(((bf16[16,256,128]{2,1,0:T(8,128)(2,1)}), bf16[16,256,128]{2,1,0:T(8,128)(2,1)S(1)}, u32[]{:S(2)}, u32[]{:S(2)}) %all-to-all-start.1) | async-done | bytes 1048608 | tf_op jit(solution)/shard_map/all_to_all | solution.py:587
  56.3 0.0 copy-done.1
  56.3 0.0 copy-done.2
  56.3 2.7 %shard_map.86 = bf16[16,256,128]{2,1,0:T(8,128)(2,1)S(1)} custom-call(bf16[256,1024]{1,0:T(8,128)(2,1)S(1)} %get-tuple-element.14.first, f32[256,128]{1,0:T(8,128)S(1)} %get-tuple-element.15.means, bf16[16,256,128]{2,1,0:T(8,128)(2,1)S(1)} %all-to-all-done.1.second, s32[1,1]{1,0:T(1,128)S(6)} %copy.11.count, f32[1,256]{1,0:T(1,128)S(1)} %bitcast.5, ...), custom_call_target="tpu_custom_call" | custom-call | flops 4000000000 | bytes 4194304 | tf_op jit(solution)/shard_map/pallas_call | solution.py:526
  59.0 30.6 %all_to_all.15.blocks = bf16[16,256,128]{2,1,0:T(8,128)(2,1)S(1)} all-to-all(bf16[16,256,128]{2,1,0:T(8,128)(2,1)S(1)} %shard_map.86), channel_id=1, replica_groups=mesh['grp'=16,'tile'=2] {'grp'}, dimensions={0} | all-to-all | bytes 2097152 | tf_op jit(solution)/shard_map/all_to_all | solution.py:587
  89.6 2.0 %shard_map.87 = bf16[64,2,4,8,128]{4,3,2,1,0:T(8,128)(2,1)} custom-call(bf16[16,256,128]{2,1,0:T(8,128)(2,1)S(1)} %all_to_all.15.blocks), custom_call_target="tpu_custom_call" | custom-call | flops 2000000000 | bytes 2097152 | tf_op jit(solution)/shard_map/pallas_call | solution.py:567
Async XLA Ops:
  4.4 8.4 %collective-permute-start = (f32[2,4,8,64,128]{4,3,2,1,0:T(8,128)S(1)}, f32[2,4,8,64,128]{4,3,2,1,0:T(8,128)}, u32[]{:S(2)}, u32[]{:S(2)}) collective-permute-start(f32[2,4,8,64,128]{4,3,2,1,0:T(8,128)S(1)} %get-tuple-element.16.own), channel_id=1, source_target_pairs={{0,1},{1,0},{2,3},{3,2},{4,5},{5,4},{6,7},{7,6},{8,9},{9,8},{10,11... | collective-permute-start | bytes 6291464 | tf_op jit(solution)/shard_map/ppermute | solution.py:580
  5.0 23.4 %all-to-all-start = ((bf16[16,128,128]{2,1,0:T(8,128)(2,1)}), bf16[16,128,128]{2,1,0:T(8,128)(2,1)S(1)}, u32[]{:S(2)}, u32[]{:S(2)}) async-start(bf16[16,128,128]{2,1,0:T(8,128)(2,1)} %get-tuple-element.13), calls=%async_computation | async-start | bytes 1048576 | tf_op jit(solution)/shard_map/all_to_all | solution.py:587
  12.9 7.9 %copy-start = (s32[1,16,256]{2,1,0:T(8,128)S(1)}, s32[1,16,256]{2,1,0:T(8,128)}, u32[]{:S(2)}) copy-start(s32[1,16,256]{2,1,0:T(8,128)} %param.12) | copy-start | bytes 49156
  24.5 31.7 %copy-start.1 = (f32[1,1,256]{2,1,0:T(1,128)S(1)}, f32[1,1,256]{2,1,0:T(1,128)}, u32[]{:S(2)}) copy-start(f32[1,1,256]{2,1,0:T(1,128)} %param.14) | copy-start | bytes 3076
  24.5 31.7 %copy-start.2 = (f32[1,1,256]{2,1,0:T(1,128)S(1)}, f32[1,1,256]{2,1,0:T(1,128)}, u32[]{:S(2)}) copy-start(f32[1,1,256]{2,1,0:T(1,128)} %param.15) | copy-start | bytes 3076
  28.3 28.0 %all-to-all-start.1 = ((bf16[16,256,128]{2,1,0:T(8,128)(2,1)}), bf16[16,256,128]{2,1,0:T(8,128)(2,1)S(1)}, u32[]{:S(2)}, u32[]{:S(2)}) async-start(bf16[16,256,128]{2,1,0:T(8,128)(2,1)} %shard_map.85), calls=%async_computation.1 | async-start | bytes 2097152 | tf_op jit(solution)/shard_map/all_to_all | solution.py:587

commit v4 on v3

--- a/solution.py
+++ b/solution.py
@@ -67,26 +67,31 @@
     return jnp.sum(jnp.where(eye(column.shape[0]), column, 0.0), axis=0, keepdims=True)
 
 
-def forecast_rows(read, first, last, coefficients):
+def both_ways(columns):
+    pair = jnp.concatenate([permutation(columns, -1), permutation(columns, 1)], axis=1)
+    return jnp.concatenate([pair, pair], axis=0)
+
+
+def forecast_rows(read, first, last, coefficients, shifts):
     middle, east, west, north, south = coefficients
 
-    def step(below, here, above):
-        columns = here.shape[2]
-        return (
-            middle * here
-            + east * above
-            + west * below
-            + north * pltpu.roll(here, columns - 1, 2)
-            + south * pltpu.roll(here, 1, 2)
-        )
-
-    rows, once, twice = [read(first - 2), read(first - 1)], [], []
-    for r in range(first - 1, last + 1):
-        rows.append(read(r + 1))
-        once.append(step(*rows[-3:]))
-        if r >= first + 1:
-            new = step(*once[-3:])
-            twice.append((r - 1, new.reshape(-1, new.shape[2]).astype(jnp.bfloat16)))
+    def step(below, here, above, ahead, behind):
+        return middle * here + east * above + west * below + north * ahead + south * behind
+
+    rows = [read(r) for r in range(first - 2, last + 2)]
+    tiles, _, columns = rows[0].shape
+    flat = jnp.concatenate(rows[1:-1], axis=0).reshape(-1, columns)
+    moved = dot(jnp.concatenate(split(flat), axis=1), shifts)
+    ahead = moved[:, :columns].reshape(-1, 8, columns)
+    behind = moved[:, columns:].reshape(-1, 8, columns)
+    once, twice = [], []
+    for i, r in enumerate(range(first - 1, last + 1)):
+        here = slice(i * tiles, (i + 1) * tiles)
+        once.append(step(*rows[i : i + 3], ahead[here], behind[here]))
+        if i >= 2:
+            one = once[-2]
+            new = step(*once[-3:], pltpu.roll(one, columns - 1, 2), pltpu.roll(one, 1, 2))
+            twice.append((r - 1, new.reshape(-1, columns).astype(jnp.bfloat16)))
     return twice
 
 
@@ -140,6 +145,7 @@
     for copy in copies:
         copy.wait()
     identity = permutation(columns, 0)
+    shifts = both_ways(columns)
     leaving = []
     for level in range(levels):
         coefficients = coefficients_of(level, *local)
@@ -159,7 +165,7 @@
                 reads.append((var, r, rows))
                 return rows.reshape(-1, 8, columns)
 
-            for r, value in forecast_rows(read, STEPS, span - STEPS, coefficients):
+            for r, value in forecast_rows(read, STEPS, span - STEPS, coefficients, shifts):
                 made.append((var, r, value))
         pairs = []
         for first in range(STEPS, span - STEPS, 2):
@@ -211,12 +217,25 @@
 
 def outer_kernel(near, own, *rest):
     sides, rest = rest[:near], rest[near:]
-    model, centre, grid, packed, staged, sems, out_sems = rest
+    model, centre, grid, packed, staged, near_tiles, sems, out_sems, near_sems = rest
     variables, levels, span, members, columns = own.shape
     rows_each = variables * members
     pairs = (2 * EDGE + span) // 2
     size = STEPS * 2 * SPAN
     identity = permutation(columns, 0)
+    shifts = both_ways(columns)
+
+    def arrive(level):
+        return [
+            pltpu.make_async_copy(
+                side.at[:, level], near_tiles.at[i, :, level], near_sems.at[i, level]
+            )
+            for i, side in enumerate(sides)
+        ]
+
+    for level in range(levels):
+        for copy in arrive(level):
+            copy.start()
 
     def leave(level):
         here = pl.ds(pl.multiple_of(level * size, size), size)
@@ -231,12 +250,14 @@
 
     @pl.loop(0, levels)
     def _(level):
+        for copy in arrive(level):
+            copy.wait()
         coefficients = [model[level, i] for i in range(5)]
         made = []
         for var in range(variables):
-            read = row_reader(level, var, own, sides[0], sides[-1])
+            read = row_reader(level, var, own, near_tiles.at[0], near_tiles.at[near - 1])
             for first, last in ((-EDGE, STEPS), (span - STEPS, span + EDGE)):
-                for r, value in forecast_rows(read, first, last, coefficients):
+                for r, value in forecast_rows(read, first, last, coefficients, shifts):
                     made.append((var, r, value))
         sheets = []
         for first in (0, span - STEPS):
@@ -269,16 +290,18 @@
                 (blocks, levels * 2 * STEPS * SPAN + slots // 2, lanes), jnp.bfloat16
             ),
         ],
-        in_specs=vmem(2 + near) + hbm(1),
+        in_specs=vmem(1) + hbm(near) + vmem(1) + hbm(1),
         out_specs=vmem(1) + hbm(1),
         scratch_shapes=[
             pltpu.VMEM((levels, blocks, 2 * STEPS * SPAN, lanes), jnp.bfloat16),
+            pltpu.VMEM((near, *own.shape), jnp.float32),
             pltpu.SemaphoreType.DMA((span - 2 * STEPS,)),
             pltpu.SemaphoreType.DMA((levels,)),
+            pltpu.SemaphoreType.DMA((near, levels)),
         ],
         compiler_params=params(16),
         cost_estimate=cost(2 * 10**9, 8 * 2**20),
-    )(own, *sides, model, centre)
+    )(own, *(pltpu.with_memory_space_constraint(x, pltpu.HBM) for x in sides), model, centre)
 
 
 def pick_kernel(variables, together, grid, _, cells, out, region, codes, staged, sems):

time: 91.9 us -> 91.8 us (level)
  Pallas kernels: 21.2 us -> 18.4 us
  waiting for transfers between devices: 26.4 us -> 29.1 us
    pallas_call x1, Pallas kernels: 7.89 us -> 5.21 us  [outer(): pl.pallas_call(functools.partial(outer_kernel, near), out_shape=[jax.Shap...]
    all_to_all x2, waiting for transfers between devices: 26.4 us -> 29.1 us  [exchange(): lax.all_to_all(blocks, 'grp', split_axis=0, concat_axis=0, tiled=True)]
  transfers between devices with their start and end apart: 3 -> 3, of which waited for: 2 -> 2; matrix products, arithmetic and copies ran while one was open for 0% -> 0% of each run, Pallas kernels for 13% -> 10%
where the time goes in v4:
time: 91.8 us; the launch traced here: 91.4 us
  blocking collectives  30.6 us (33%)
  waiting for transfers between devices  29.1 us (32%)
  Pallas kernels  18.4 us (20%)
  starting transfers between devices  12.6 us (14%)
    all_to_all x1, blocking collectives, exchange(): lax.all_to_all(blocks, 'grp', split_axis=0, concat_axis=0, tiled=True)  30.6 us
    all_to_all x2, waiting for transfers between devices, exchange(): lax.all_to_all(blocks, 'grp', split_axis=0, concat_axis=0, tiled=True)  29.1 us
    all_to_all x2, starting transfers between devices, exchange(): lax.all_to_all(blocks, 'grp', split_axis=0, concat_axis=0, tiled=True)  12.1 us
    pallas_call x1, Pallas kernels, outer(): pl.pallas_call(functools.partial(outer_kernel, near), out_shape=[jax.Shap...  5.21 us
    pallas_call x1, Pallas kernels, inner(): pl.pallas_call(functools.partial(inner_kernel, variables), out_shape=[jax...  4.31 us
    pallas_call x1, Pallas kernels, pick(): pl.pallas_call(functools.partial(pick_kernel, variables, together), out_s...  3.74 us
    pallas_call x1, Pallas kernels, analyse(): pl.pallas_call(analyse_kernel, out_shape=jax.ShapeDtypeStruct((groups, ne...  2.7 us
    pallas_call x1, Pallas kernels, restore(): pl.pallas_call(restore_kernel, out_shape=jax.ShapeDtypeStruct((members, v...  1.99 us
  transfers between devices with their start and end apart: 3, of which 2 were waited for; matrix products, arithmetic and copies ran while one was open for 0% of the time, Pallas kernels for 10%

profile of v4, /device:TPU:0, one launch (start us, length us, event | category | flops | bytes accessed | tf_op | source)
XLA Modules:
  0.0 91.4 jit_solution(17920206733152733746)
XLA Ops:
  0.0 4.3 %shard_map.82 = (f32[2,4,8,64,128]{4,3,2,1,0:T(8,128)S(1)}, bf16[4,4,128,128]{3,2,1,0:T(8,128)(2,1)S(1)}, bf16[16,128,128]{2,1,0:T(8,128)(2,1)}, f32[4,5,8,128]{3,2,1,0:T(8,128)S(1)}) custom-call(f32[128,4,8,128]{3,2,1,0:T(8,128)} %bitcast.7, f32[4,128]{1,0:T(4,128)} %refs_0_.1, f32[4]{0:T(128)} %refs_1_.1, f32[4]{0:T(128)} %refs_2_.1), custom_call_target="tpu_custom_call" | custom-call | flops 2000000000 | bytes 4194304 | tf_op jit(solution)/shard_map/pallas_call | solution.py:193
  4.3 0.5 collective-permute-start
  4.8 7.9 %all-to-all-start = ((bf16[16,128,128]{2,1,0:T(8,128)(2,1)}), bf16[16,128,128]{2,1,0:T(8,128)(2,1)S(1)}, u32[]{:S(2)}, u32[]{:S(2)}) async-start(bf16[16,128,128]{2,1,0:T(8,128)(2,1)} %get-tuple-element.13), calls=%async_computation | async-start | bytes 1048576 | tf_op jit(solution)/shard_map/all_to_all | solution.py:610
  12.7 0.0 collective-permute-done.rest_0_
  12.7 0.0 copy-start
  12.8 5.2 %shard_map.84 = (bf16[4,8,256,128]{3,2,1,0:T(8,128)(2,1)S(1)}, bf16[16,256,128]{2,1,0:T(8,128)(2,1)}) custom-call(f32[2,4,8,64,128]{4,3,2,1,0:T(8,128)S(1)} %get-tuple-element.16.own, f32[2,4,8,64,128]{4,3,2,1,0:T(8,128)} %collective-permute-done.rest_0_, f32[4,5,8,128]{3,2,1,0:T(8,128)S(1)} %get-tuple-element.17.rest_1_, ...), custom_call_target="tpu_custom_call" | custom-call | flops 2000000000 | bytes 8388608 | tf_op jit(solution)/shard_map/pallas_call | solution.py:285
  18.0 0.0 copy-done
  18.0 3.7 %shard_map.85 = bf16[16,256,128]{2,1,0:T(8,128)(2,1)} custom-call(bf16[4,8,256,128]{3,2,1,0:T(8,128)(2,1)S(1)} %get-tuple-element.19.grid, bf16[16,256,128]{2,1,0:T(8,128)(2,1)} %get-tuple-element.20._, s32[16,256]{1,0:T(8,128)S(1)} %bitcast.4), custom_call_target="tpu_custom_call", output_to_operand_aliasing={{}: (1, {})} | custom-call | flops 4000000000 | bytes 4194304 | tf_op jit(solution)/shard_map/pallas_call | solution.py:379
  21.7 0.0 copy-start.1
  21.7 0.0 copy-start.2
  21.8 6.4 %all-to-all-done.states = bf16[16,128,128]{2,1,0:T(8,128)(2,1)S(1)} async-done(((bf16[16,128,128]{2,1,0:T(8,128)(2,1)}), bf16[16,128,128]{2,1,0:T(8,128)(2,1)S(1)}, u32[]{:S(2)}, u32[]{:S(2)}) %all-to-all-start) | async-done | bytes 524320 | tf_op jit(solution)/shard_map/all_to_all | solution.py:610
  28.2 4.2 %all-to-all-start.1 = ((bf16[16,256,128]{2,1,0:T(8,128)(2,1)}), bf16[16,256,128]{2,1,0:T(8,128)(2,1)S(1)}, u32[]{:S(2)}, u32[]{:S(2)}) async-start(bf16[16,256,128]{2,1,0:T(8,128)(2,1)} %shard_map.85), calls=%async_computation.1 | async-start | bytes 2097152 | tf_op jit(solution)/shard_map/all_to_all | solution.py:610
  33.1 0.4 shard_map.83
  33.5 22.6 %all-to-all-done.1.second = bf16[16,256,128]{2,1,0:T(8,128)(2,1)S(1)} async-done(((bf16[16,256,128]{2,1,0:T(8,128)(2,1)}), bf16[16,256,128]{2,1,0:T(8,128)(2,1)S(1)}, u32[]{:S(2)}, u32[]{:S(2)}) %all-to-all-start.1) | async-done | bytes 1048608 | tf_op jit(solution)/shard_map/all_to_all | solution.py:610
  56.2 0.0 copy-done.1
  56.2 0.0 copy-done.2
  56.2 2.7 %shard_map.86 = bf16[16,256,128]{2,1,0:T(8,128)(2,1)S(1)} custom-call(bf16[256,1024]{1,0:T(8,128)(2,1)S(1)} %get-tuple-element.14.first, f32[256,128]{1,0:T(8,128)S(1)} %get-tuple-element.15.means, bf16[16,256,128]{2,1,0:T(8,128)(2,1)S(1)} %all-to-all-done.1.second, s32[1,1]{1,0:T(1,128)S(6)} %copy.11.count, f32[1,256]{1,0:T(1,128)S(1)} %bitcast.5, ...), custom_call_target="tpu_custom_call" | custom-call | flops 4000000000 | bytes 4194304 | tf_op jit(solution)/shard_map/pallas_call | solution.py:549
  58.9 30.6 %all_to_all.15.blocks = bf16[16,256,128]{2,1,0:T(8,128)(2,1)S(1)} all-to-all(bf16[16,256,128]{2,1,0:T(8,128)(2,1)S(1)} %shard_map.86), channel_id=1, replica_groups=mesh['grp'=16,'tile'=2] {'grp'}, dimensions={0} | all-to-all | bytes 2097152 | tf_op jit(solution)/shard_map/all_to_all | solution.py:610
  89.4 2.0 %shard_map.87 = bf16[64,2,4,8,128]{4,3,2,1,0:T(8,128)(2,1)} custom-call(bf16[16,256,128]{2,1,0:T(8,128)(2,1)S(1)} %all_to_all.15.blocks), custom_call_target="tpu_custom_call" | custom-call | flops 2000000000 | bytes 2097152 | tf_op jit(solution)/shard_map/pallas_call | solution.py:590
Async XLA Ops:
  4.3 8.4 %collective-permute-start = (f32[2,4,8,64,128]{4,3,2,1,0:T(8,128)S(1)}, f32[2,4,8,64,128]{4,3,2,1,0:T(8,128)}, u32[]{:S(2)}, u32[]{:S(2)}) collective-permute-start(f32[2,4,8,64,128]{4,3,2,1,0:T(8,128)S(1)} %get-tuple-element.16.own), channel_id=1, source_target_pairs={{0,1},{1,0},{2,3},{3,2},{4,5},{5,4},{6,7},{7,6},{8,9},{9,8},{10,11... | collective-permute-start | bytes 6291464 | tf_op jit(solution)/shard_map/ppermute | solution.py:603
  4.8 23.4 %all-to-all-start = ((bf16[16,128,128]{2,1,0:T(8,128)(2,1)}), bf16[16,128,128]{2,1,0:T(8,128)(2,1)S(1)}, u32[]{:S(2)}, u32[]{:S(2)}) async-start(bf16[16,128,128]{2,1,0:T(8,128)(2,1)} %get-tuple-element.13), calls=%async_computation | async-start | bytes 1048576 | tf_op jit(solution)/shard_map/all_to_all | solution.py:610
  12.7 5.2 %copy-start = (s32[1,16,256]{2,1,0:T(8,128)S(1)}, s32[1,16,256]{2,1,0:T(8,128)}, u32[]{:S(2)}) copy-start(s32[1,16,256]{2,1,0:T(8,128)} %param.12) | copy-start | bytes 49156
  21.7 34.4 %copy-start.1 = (f32[1,1,256]{2,1,0:T(1,128)S(1)}, f32[1,1,256]{2,1,0:T(1,128)}, u32[]{:S(2)}) copy-start(f32[1,1,256]{2,1,0:T(1,128)} %param.14) | copy-start | bytes 3076
  21.7 34.4 %copy-start.2 = (f32[1,1,256]{2,1,0:T(1,128)S(1)}, f32[1,1,256]{2,1,0:T(1,128)}, u32[]{:S(2)}) copy-start(f32[1,1,256]{2,1,0:T(1,128)} %param.15) | copy-start | bytes 3076
  28.2 28.0 %all-to-all-start.1 = ((bf16[16,256,128]{2,1,0:T(8,128)(2,1)}), bf16[16,256,128]{2,1,0:T(8,128)(2,1)S(1)}, u32[]{:S(2)}, u32[]{:S(2)}) async-start(bf16[16,256,128]{2,1,0:T(8,128)(2,1)} %shard_map.85), calls=%async_computation.1 | async-start | bytes 2097152 | tf_op jit(solution)/shard_map/all_to_all | solution.py:610

commit v5 on v4

--- a/solution.py
+++ b/solution.py
@@ -96,7 +96,7 @@
 
 
 def coefficients_of(level, diff, east, north):
-    spread = jnp.broadcast_to(diff[level : level + 1, :], (8, diff.shape[1]))
+    spread = jnp.broadcast_to(diff[pl.ds(level, 1), :], (8, diff.shape[1]))
     u = 0.5 * east[level]
     w = 0.5 * north[level]
     return 1.0 - 4.0 * spread, spread - u, spread + u, spread - w, spread + w
@@ -130,38 +130,36 @@
     lanes, levels, span, columns = own.shape
     members = lanes // variables
     count = span - 2 * STEPS
+    def arrive(level):
+        return pltpu.make_async_copy(own.at[:, level], whole.at[level], in_sems.at[level])
+
+    def leave(level):
+        size = count * SPAN
+        here = pl.ds(pl.multiple_of(level * size, size), size)
+        return pltpu.make_async_copy(staged.at[level], packed.at[:, here], out_sems.at[level])
+
     copies = [pltpu.make_async_copy(x, y, raw_sems.at[i]) for i, (x, y) in enumerate(zip(raw, local))]
-    together = whole.shape[2]
-    arrivals = []
-    for i in range(levels // together):
-        for part in range(2):
-            here = pl.ds(part * (lanes // 2), lanes // 2)
-            source = own.at[here, pl.ds(i * together, together)]
-            arrivals.append(
-                pltpu.make_async_copy(source, whole.at[i, here], in_sems.at[2 * i + part])
-            )
-    for copy in copies + arrivals:
+    for copy in copies:
         copy.start()
+    for level in range(levels):
+        arrive(level).start()
+    identity = permutation(columns, 0)
+    shifts = both_ways(columns)
     for copy in copies:
         copy.wait()
-    identity = permutation(columns, 0)
-    shifts = both_ways(columns)
-    leaving = []
-    for level in range(levels):
+
+    @pl.loop(0, levels)
+    def _(level):
         coefficients = coefficients_of(level, *local)
         for i, one in enumerate(coefficients):
             model[level, i] = one
-        step, inside = divmod(level, together)
-        if inside == 0:
-            arrivals[2 * step].wait()
-            arrivals[2 * step + 1].wait()
-        view = whole.at[step].reshape(lanes * together * span, columns)
+        arrive(level).wait()
+        view = whole.at[level].reshape(lanes * span, columns)
         reads, made = [], []
         for var in range(variables):
 
             def read(r):
-                at = (var * together + inside) * span + r
-                rows = view[pl.ds(at, members, stride=variables * together * span), :]
+                rows = view[pl.ds(var * span + r, members, stride=variables * span), :]
                 reads.append((var, r, rows))
                 return rows.reshape(-1, 8, columns)
 
@@ -172,15 +170,14 @@
             rows = [one for r in (first, first + 1) for _, at, one in made if at == r]
             pairs.append(jnp.concatenate(rows, axis=0))
         pack_rows(pairs, identity, staged.at[level], 0)
-        here = pl.ds(level * count * SPAN, count * SPAN)
-        leaving.append(pltpu.make_async_copy(staged.at[level], packed.at[:, here], out_sems.at[level]))
-        leaving[-1].start()
+        leave(level).start()
         for var, r, value in made:
             fields[level, r - STEPS, var * members : (var + 1) * members, :] = value
         for var, r, rows in reads:
             slabs[var, level, r] = rows
-    for copy in leaving:
-        copy.wait()
+
+    for level in range(levels):
+        leave(level).wait()
 
 
 def inner(own, raw, variables):
@@ -188,7 +185,6 @@
     members = lanes // variables
     blocks = columns // SPAN
     count = span - 2 * STEPS
-    together = 1
     fixed = [pltpu.with_memory_space_constraint(x, pltpu.HBM) for x in (own, *raw)]
     return pl.pallas_call(
         functools.partial(inner_kernel, variables),
@@ -204,9 +200,9 @@
             pltpu.VMEM(raw[0].shape, jnp.float32),
             pltpu.SMEM(raw[1].shape, jnp.float32),
             pltpu.SMEM(raw[2].shape, jnp.float32),
-            pltpu.VMEM((levels // together, lanes, together, span, columns), jnp.float32),
+            pltpu.VMEM((levels, lanes, span, columns), jnp.float32),
             pltpu.VMEM((levels, blocks, count * SPAN, lanes), jnp.bfloat16),
-            pltpu.SemaphoreType.DMA((2 * levels // together,)),
+            pltpu.SemaphoreType.DMA((levels,)),
             pltpu.SemaphoreType.DMA((3,)),
             pltpu.SemaphoreType.DMA((levels,)),
         ],
@@ -316,7 +312,9 @@
 
     order = permutation(columns, -EDGE)
     batch = next(n for n in (4, 2, 1) if pairs % n == 0)
-    for level in range(levels):
+
+    @pl.loop(0, levels)
+    def _(level):
         for start in range(0, pairs, batch):
             made = []
             for i in range(batch):
@@ -324,11 +322,11 @@
                 odd = jnp.concatenate([even[SPAN:], even[:SPAN]], axis=0)
                 made.append((even.astype(jnp.bfloat16), odd.astype(jnp.bfloat16)))
             for i, both in enumerate(made):
-                at = (level * pairs + start + i) * width
+                at = pl.multiple_of((level * pairs + start + i) * width, width)
                 for first, value in enumerate(both):
                     for j in range(columns // width):
                         piece = value[j * width : (j + 1) * width, :]
-                        region[2 * j + first, at : at + width, :] = piece
+                        region[2 * j + first, pl.ds(at, width), :] = piece
 
     cell = cells[...]
     second = cell >= 2 * entries
@@ -567,21 +565,25 @@
     lanes = members * variables
     identity = permutation(lanes, 0)
     near = span - 2 * STEPS
-    for level in range(levels):
+
+    @pl.loop(0, levels)
+    def _(level):
+        slot = lax.rem(level, 2)
         made = []
         for r in range(0, span, 2):
             if STEPS <= r < span - STEPS:
                 at = level * near + r - STEPS
             else:
                 at = levels * near + level * 2 * STEPS + (r if r < STEPS else r - near)
-            both = blocks[:, at * SPAN : (at + 2) * SPAN, :].astype(jnp.float32)
+            here = pl.ds(pl.multiple_of(at * SPAN, 2 * SPAN), 2 * SPAN)
+            both = blocks[:, here, :].astype(jnp.float32)
             for i in range(2):
                 one = both[:, i * SPAN : (i + 1) * SPAN, :].reshape(columns, lanes)
                 made.append((r + i, dot_rows(identity, one.astype(jnp.bfloat16))))
         for r, rows in made:
-            turned[level % 2, pl.ds(r, lanes, stride=span), :] = rows
+            turned[slot, pl.ds(r, lanes, stride=span), :] = rows
         for var in range(variables):
-            half = turned[level % 2, var * members * span : (var + 1) * members * span, :]
+            half = turned[slot, var * members * span : (var + 1) * members * span, :]
             out[:, var, level] = half.reshape(members, span, columns).astype(jnp.bfloat16)
 
 

time: 91.8 us -> 92.2 us (level)
  Pallas kernels: 18.4 us -> 19.4 us
  transfers between devices with their start and end apart: 3 -> 3, of which waited for: 2 -> 2; matrix products, arithmetic and copies ran while one was open for 0% -> 0% of each run, Pallas kernels for 10% -> 11%
where the time goes in v5:
time: 92.2 us; the launch traced here: 91.8 us
  blocking collectives  30.6 us (33%)
  waiting for transfers between devices  28.5 us (31%)
  Pallas kernels  19.4 us (21%)
  starting transfers between devices  12.6 us (14%)
    all_to_all x1, blocking collectives, exchange(): lax.all_to_all(blocks, 'grp', split_axis=0, concat_axis=0, tiled=True)  30.6 us
    all_to_all x2, waiting for transfers between devices, exchange(): lax.all_to_all(blocks, 'grp', split_axis=0, concat_axis=0, tiled=True)  28.5 us
    all_to_all x2, starting transfers between devices, exchange(): lax.all_to_all(blocks, 'grp', split_axis=0, concat_axis=0, tiled=True)  12.1 us
    pallas_call x1, Pallas kernels, outer(): pl.pallas_call(functools.partial(outer_kernel, near), out_shape=[jax.Shap...  5.21 us
    pallas_call x1, Pallas kernels, pick(): pl.pallas_call(functools.partial(pick_kernel, variables, together), out_s...  4.29 us
    pallas_call x1, Pallas kernels, inner(): pl.pallas_call(functools.partial(inner_kernel, variables), out_shape=[jax...  4.24 us
    pallas_call x1, Pallas kernels, analyse(): pl.pallas_call(analyse_kernel, out_shape=jax.ShapeDtypeStruct((groups, ne...  2.7 us
    pallas_call x1, Pallas kernels, restore(): pl.pallas_call(restore_kernel, out_shape=jax.ShapeDtypeStruct((members, v...  2.46 us
  transfers between devices with their start and end apart: 3, of which 2 were waited for; matrix products, arithmetic and copies ran while one was open for 0% of the time, Pallas kernels for 11%

profile of v5, /device:TPU:0, one launch (start us, length us, event | category | flops | bytes accessed | tf_op | source)
XLA Modules:
  0.0 91.8 jit_solution(410934069665405114)
XLA Ops:
  0.0 4.2 %shard_map.82 = (f32[2,4,8,64,128]{4,3,2,1,0:T(8,128)S(1)}, bf16[4,4,128,128]{3,2,1,0:T(8,128)(2,1)S(1)}, bf16[16,128,128]{2,1,0:T(8,128)(2,1)}, f32[4,5,8,128]{3,2,1,0:T(8,128)S(1)}) custom-call(f32[128,4,8,128]{3,2,1,0:T(8,128)} %bitcast.7, f32[4,128]{1,0:T(4,128)} %refs_0_.1, f32[4]{0:T(128)} %refs_1_.1, f32[4]{0:T(128)} %refs_2_.1), custom_call_target="tpu_custom_call" | custom-call | flops 2000000000 | bytes 4194304 | tf_op jit(solution)/shard_map/pallas_call | solution.py:189
  4.3 0.5 collective-permute-start
  4.8 7.9 %all-to-all-start = ((bf16[16,128,128]{2,1,0:T(8,128)(2,1)}), bf16[16,128,128]{2,1,0:T(8,128)(2,1)S(1)}, u32[]{:S(2)}, u32[]{:S(2)}) async-start(bf16[16,128,128]{2,1,0:T(8,128)(2,1)} %get-tuple-element.13), calls=%async_computation | async-start | bytes 1048576 | tf_op jit(solution)/shard_map/all_to_all | solution.py:612
  12.7 0.0 collective-permute-done.rest_0_
  12.7 0.0 copy-start
  12.7 5.2 %shard_map.84 = (bf16[4,8,256,128]{3,2,1,0:T(8,128)(2,1)S(1)}, bf16[16,256,128]{2,1,0:T(8,128)(2,1)}) custom-call(f32[2,4,8,64,128]{4,3,2,1,0:T(8,128)S(1)} %get-tuple-element.16.own, f32[2,4,8,64,128]{4,3,2,1,0:T(8,128)} %collective-permute-done.rest_0_, f32[4,5,8,128]{3,2,1,0:T(8,128)S(1)} %get-tuple-element.17.rest_1_, ...), custom_call_target="tpu_custom_call" | custom-call | flops 2000000000 | bytes 8388608 | tf_op jit(solution)/shard_map/pallas_call | solution.py:281
  17.9 0.0 copy-done
  17.9 4.3 %shard_map.85 = bf16[16,256,128]{2,1,0:T(8,128)(2,1)} custom-call(bf16[4,8,256,128]{3,2,1,0:T(8,128)(2,1)S(1)} %get-tuple-element.19.grid, bf16[16,256,128]{2,1,0:T(8,128)(2,1)} %get-tuple-element.20._, s32[16,256]{1,0:T(8,128)S(1)} %bitcast.4), custom_call_target="tpu_custom_call", output_to_operand_aliasing={{}: (1, {})} | custom-call | flops 4000000000 | bytes 4194304 | tf_op jit(solution)/shard_map/pallas_call | solution.py:377
  22.2 0.0 copy-start.1
  22.2 0.0 copy-start.2
  22.2 5.9 %all-to-all-done.states = bf16[16,128,128]{2,1,0:T(8,128)(2,1)S(1)} async-done(((bf16[16,128,128]{2,1,0:T(8,128)(2,1)}), bf16[16,128,128]{2,1,0:T(8,128)(2,1)S(1)}, u32[]{:S(2)}, u32[]{:S(2)}) %all-to-all-start) | async-done | bytes 524320 | tf_op jit(solution)/shard_map/all_to_all | solution.py:612
  28.1 4.2 %all-to-all-start.1 = ((bf16[16,256,128]{2,1,0:T(8,128)(2,1)}), bf16[16,256,128]{2,1,0:T(8,128)(2,1)S(1)}, u32[]{:S(2)}, u32[]{:S(2)}) async-start(bf16[16,256,128]{2,1,0:T(8,128)(2,1)} %shard_map.85), calls=%async_computation.1 | async-start | bytes 2097152 | tf_op jit(solution)/shard_map/all_to_all | solution.py:612
  33.0 0.4 shard_map.83
  33.5 22.6 %all-to-all-done.1.second = bf16[16,256,128]{2,1,0:T(8,128)(2,1)S(1)} async-done(((bf16[16,256,128]{2,1,0:T(8,128)(2,1)}), bf16[16,256,128]{2,1,0:T(8,128)(2,1)S(1)}, u32[]{:S(2)}, u32[]{:S(2)}) %all-to-all-start.1) | async-done | bytes 1048608 | tf_op jit(solution)/shard_map/all_to_all | solution.py:612
  56.1 0.0 copy-done.1
  56.1 0.0 copy-done.2
  56.1 2.7 %shard_map.86 = bf16[16,256,128]{2,1,0:T(8,128)(2,1)S(1)} custom-call(bf16[256,1024]{1,0:T(8,128)(2,1)S(1)} %get-tuple-element.14.first, f32[256,128]{1,0:T(8,128)S(1)} %get-tuple-element.15.means, bf16[16,256,128]{2,1,0:T(8,128)(2,1)S(1)} %all-to-all-done.1.second, s32[1,1]{1,0:T(1,128)S(6)} %copy.11.count, f32[1,256]{1,0:T(1,128)S(1)} %bitcast.5, ...), custom_call_target="tpu_custom_call" | custom-call | flops 4000000000 | bytes 4194304 | tf_op jit(solution)/shard_map/pallas_call | solution.py:547
  58.8 30.6 %all_to_all.15.blocks = bf16[16,256,128]{2,1,0:T(8,128)(2,1)S(1)} all-to-all(bf16[16,256,128]{2,1,0:T(8,128)(2,1)S(1)} %shard_map.86), channel_id=1, replica_groups=mesh['grp'=16,'tile'=2] {'grp'}, dimensions={0} | all-to-all | bytes 2097152 | tf_op jit(solution)/shard_map/all_to_all | solution.py:612
  89.4 2.5 %shard_map.87 = bf16[64,2,4,8,128]{4,3,2,1,0:T(8,128)(2,1)} custom-call(bf16[16,256,128]{2,1,0:T(8,128)(2,1)S(1)} %all_to_all.15.blocks), custom_call_target="tpu_custom_call" | custom-call | flops 2000000000 | bytes 2097152 | tf_op jit(solution)/shard_map/pallas_call | solution.py:592
Async XLA Ops:
  4.3 8.4 %collective-permute-start = (f32[2,4,8,64,128]{4,3,2,1,0:T(8,128)S(1)}, f32[2,4,8,64,128]{4,3,2,1,0:T(8,128)}, u32[]{:S(2)}, u32[]{:S(2)}) collective-permute-start(f32[2,4,8,64,128]{4,3,2,1,0:T(8,128)S(1)} %get-tuple-element.16.own), channel_id=1, source_target_pairs={{0,1},{1,0},{2,3},{3,2},{4,5},{5,4},{6,7},{7,6},{8,9},{9,8},{10,11... | collective-permute-start | bytes 6291464 | tf_op jit(solution)/shard_map/ppermute | solution.py:605
  4.8 23.4 %all-to-all-start = ((bf16[16,128,128]{2,1,0:T(8,128)(2,1)}), bf16[16,128,128]{2,1,0:T(8,128)(2,1)S(1)}, u32[]{:S(2)}, u32[]{:S(2)}) async-start(bf16[16,128,128]{2,1,0:T(8,128)(2,1)} %get-tuple-element.13), calls=%async_computation | async-start | bytes 1048576 | tf_op jit(solution)/shard_map/all_to_all | solution.py:612
  12.7 5.2 %copy-start = (s32[1,16,256]{2,1,0:T(8,128)S(1)}, s32[1,16,256]{2,1,0:T(8,128)}, u32[]{:S(2)}) copy-start(s32[1,16,256]{2,1,0:T(8,128)} %param.12) | copy-start | bytes 49156
  22.2 33.9 %copy-start.1 = (f32[1,1,256]{2,1,0:T(1,128)S(1)}, f32[1,1,256]{2,1,0:T(1,128)}, u32[]{:S(2)}) copy-start(f32[1,1,256]{2,1,0:T(1,128)} %param.14) | copy-start | bytes 3076
  22.2 33.9 %copy-start.2 = (f32[1,1,256]{2,1,0:T(1,128)S(1)}, f32[1,1,256]{2,1,0:T(1,128)}, u32[]{:S(2)}) copy-start(f32[1,1,256]{2,1,0:T(1,128)} %param.15) | copy-start | bytes 3076
  28.1 28.0 %all-to-all-start.1 = ((bf16[16,256,128]{2,1,0:T(8,128)(2,1)}), bf16[16,256,128]{2,1,0:T(8,128)(2,1)S(1)}, u32[]{:S(2)}, u32[]{:S(2)}) async-start(bf16[16,256,128]{2,1,0:T(8,128)(2,1)} %shard_map.85), calls=%async_computation.1 | async-start | bytes 2097152 | tf_op jit(solution)/shard_map/all_to_all | solution.py:612

commit v6 on v5

--- a/solution.py
+++ b/solution.py
@@ -141,7 +141,7 @@
     copies = [pltpu.make_async_copy(x, y, raw_sems.at[i]) for i, (x, y) in enumerate(zip(raw, local))]
     for copy in copies:
         copy.start()
-    for level in range(levels):
+    for level in range(min(2, levels)):
         arrive(level).start()
     identity = permutation(columns, 0)
     shifts = both_ways(columns)
@@ -154,6 +154,11 @@
         for i, one in enumerate(coefficients):
             model[level, i] = one
         arrive(level).wait()
+
+        @pl.when(level + 2 < levels)
+        def _():
+            arrive(level + 2).start()
+
         view = whole.at[level].reshape(lanes * span, columns)
         reads, made = [], []
         for var in range(variables):
@@ -312,9 +317,7 @@
 
     order = permutation(columns, -EDGE)
     batch = next(n for n in (4, 2, 1) if pairs % n == 0)
-
-    @pl.loop(0, levels)
-    def _(level):
+    for level in range(levels):
         for start in range(0, pairs, batch):
             made = []
             for i in range(batch):
@@ -322,11 +325,11 @@
                 odd = jnp.concatenate([even[SPAN:], even[:SPAN]], axis=0)
                 made.append((even.astype(jnp.bfloat16), odd.astype(jnp.bfloat16)))
             for i, both in enumerate(made):
-                at = pl.multiple_of((level * pairs + start + i) * width, width)
+                at = (level * pairs + start + i) * width
                 for first, value in enumerate(both):
                     for j in range(columns // width):
                         piece = value[j * width : (j + 1) * width, :]
-                        region[2 * j + first, pl.ds(at, width), :] = piece
+                        region[2 * j + first, at : at + width, :] = piece
 
     cell = cells[...]
     second = cell >= 2 * entries
@@ -560,42 +563,55 @@
     )(first, means, second, count, value, weight)
 
 
-def restore_kernel(blocks, out, turned):
+def restore_kernel(blocks, out, turned, staged, sems):
     members, variables, levels, span, columns = out.shape
     lanes = members * variables
     identity = permutation(lanes, 0)
     near = span - 2 * STEPS
-
-    @pl.loop(0, levels)
-    def _(level):
-        slot = lax.rem(level, 2)
+    for level in range(levels):
         made = []
         for r in range(0, span, 2):
             if STEPS <= r < span - STEPS:
                 at = level * near + r - STEPS
             else:
                 at = levels * near + level * 2 * STEPS + (r if r < STEPS else r - near)
-            here = pl.ds(pl.multiple_of(at * SPAN, 2 * SPAN), 2 * SPAN)
-            both = blocks[:, here, :].astype(jnp.float32)
+            both = blocks[:, at * SPAN : (at + 2) * SPAN, :].astype(jnp.float32)
             for i in range(2):
                 one = both[:, i * SPAN : (i + 1) * SPAN, :].reshape(columns, lanes)
                 made.append((r + i, dot_rows(identity, one.astype(jnp.bfloat16))))
         for r, rows in made:
-            turned[slot, pl.ds(r, lanes, stride=span), :] = rows
-        for var in range(variables):
-            half = turned[slot, var * members * span : (var + 1) * members * span, :]
-            out[:, var, level] = half.reshape(members, span, columns).astype(jnp.bfloat16)
+            turned[level, pl.ds(r, lanes, stride=span), :] = rows
+
+    chunks = staged.shape[0]
+    size = members // chunks
+    copies = []
+    for i in range(chunks):
+        for level in range(levels):
+            for var in range(variables):
+                at = (var * members + i * size) * span
+                part = turned[level, at : at + size * span, :].reshape(size, span, columns)
+                staged[i, :, var, level] = part.astype(jnp.bfloat16)
+        place = out.at[pl.ds(i * size, size)]
+        copies.append(pltpu.make_async_copy(staged.at[i], place, sems.at[i]))
+        copies[-1].start()
+    for copy in copies:
+        copy.wait()
 
 
 def restore(dims, blocks):
     members, variables, levels, span, columns = dims
+    chunks = next(n for n in (4, 2, 1) if members % n == 0)
     return pl.pallas_call(
         restore_kernel,
         out_shape=jax.ShapeDtypeStruct((members, variables, levels, span, columns), jnp.bfloat16),
         in_specs=vmem(1),
-        out_specs=pl.BlockSpec(memory_space=pltpu.VMEM),
-        scratch_shapes=[pltpu.VMEM((2, variables * members * span, columns), jnp.float32)],
-        compiler_params=params(8),
+        out_specs=pl.BlockSpec(memory_space=pltpu.HBM),
+        scratch_shapes=[
+            pltpu.VMEM((levels, variables * members * span, columns), jnp.float32),
+            pltpu.VMEM((chunks, members // chunks, variables, levels, span, columns), jnp.bfloat16),
+            pltpu.SemaphoreType.DMA((chunks,)),
+        ],
+        compiler_params=params(10),
         cost_estimate=cost(2 * 10**9, 2 * 2**20),
     )(blocks)
 

time: 92.2 us -> 91.7 us (level)
  Pallas kernels: 19.4 us -> 18.3 us
  transfers between devices with their start and end apart: 3 -> 3, of which waited for: 2 -> 2; matrix products, arithmetic and copies ran while one was open for 0% -> 0% of each run, Pallas kernels for 11% -> 10%
where the time goes in v6:
time: 91.7 us; the launch traced here: 91.3 us
  blocking collectives  30.6 us (33%)
  waiting for transfers between devices  29.1 us (32%)
  Pallas kernels  18.3 us (20%)
  starting transfers between devices  12.6 us (14%)
    all_to_all x1, blocking collectives, exchange(): lax.all_to_all(blocks, 'grp', split_axis=0, concat_axis=0, tiled=True)  30.6 us
    all_to_all x2, waiting for transfers between devices, exchange(): lax.all_to_all(blocks, 'grp', split_axis=0, concat_axis=0, tiled=True)  29.1 us
    all_to_all x2, starting transfers between devices, exchange(): lax.all_to_all(blocks, 'grp', split_axis=0, concat_axis=0, tiled=True)  12.1 us
    pallas_call x1, Pallas kernels, outer(): pl.pallas_call(functools.partial(outer_kernel, near), out_shape=[jax.Shap...  5.21 us
    pallas_call x1, Pallas kernels, inner(): pl.pallas_call(functools.partial(inner_kernel, variables), out_shape=[jax...  4.24 us
    pallas_call x1, Pallas kernels, pick(): pl.pallas_call(functools.partial(pick_kernel, variables, together), out_s...  3.74 us
    pallas_call x1, Pallas kernels, analyse(): pl.pallas_call(analyse_kernel, out_shape=jax.ShapeDtypeStruct((groups, ne...  2.7 us
    pallas_call x1, Pallas kernels, restore(): pl.pallas_call(restore_kernel, out_shape=jax.ShapeDtypeStruct((members, v...  1.93 us
  transfers between devices with their start and end apart: 3, of which 2 were waited for; matrix products, arithmetic and copies ran while one was open for 0% of the time, Pallas kernels for 10%

profile of v6, /device:TPU:0, one launch (start us, length us, event | category | flops | bytes accessed | tf_op | source)
XLA Modules:
  0.0 91.3 jit_solution(11212577220924258973)
XLA Ops:
  0.0 4.2 %shard_map.82 = (f32[2,4,8,64,128]{4,3,2,1,0:T(8,128)S(1)}, bf16[4,4,128,128]{3,2,1,0:T(8,128)(2,1)S(1)}, bf16[16,128,128]{2,1,0:T(8,128)(2,1)}, f32[4,5,8,128]{3,2,1,0:T(8,128)S(1)}) custom-call(f32[128,4,8,128]{3,2,1,0:T(8,128)} %bitcast.7, f32[4,128]{1,0:T(4,128)} %refs_0_.1, f32[4]{0:T(128)} %refs_1_.1, f32[4]{0:T(128)} %refs_2_.1), custom_call_target="tpu_custom_call" | custom-call | flops 2000000000 | bytes 4194304 | tf_op jit(solution)/shard_map/pallas_call | solution.py:194
  4.3 0.5 collective-permute-start
  4.8 7.9 %all-to-all-start = ((bf16[16,128,128]{2,1,0:T(8,128)(2,1)}), bf16[16,128,128]{2,1,0:T(8,128)(2,1)S(1)}, u32[]{:S(2)}, u32[]{:S(2)}) async-start(bf16[16,128,128]{2,1,0:T(8,128)(2,1)} %get-tuple-element.13), calls=%async_computation | async-start | bytes 1048576 | tf_op jit(solution)/shard_map/all_to_all | solution.py:628
  12.7 0.0 collective-permute-done.rest_0_
  12.7 0.0 copy-start
  12.7 5.2 %shard_map.84 = (bf16[4,8,256,128]{3,2,1,0:T(8,128)(2,1)S(1)}, bf16[16,256,128]{2,1,0:T(8,128)(2,1)}) custom-call(f32[2,4,8,64,128]{4,3,2,1,0:T(8,128)S(1)} %get-tuple-element.16.own, f32[2,4,8,64,128]{4,3,2,1,0:T(8,128)} %collective-permute-done.rest_0_, f32[4,5,8,128]{3,2,1,0:T(8,128)S(1)} %get-tuple-element.17.rest_1_, ...), custom_call_target="tpu_custom_call" | custom-call | flops 2000000000 | bytes 8388608 | tf_op jit(solution)/shard_map/pallas_call | solution.py:286
  17.9 0.0 copy-done
  17.9 3.7 %shard_map.85 = bf16[16,256,128]{2,1,0:T(8,128)(2,1)} custom-call(bf16[4,8,256,128]{3,2,1,0:T(8,128)(2,1)S(1)} %get-tuple-element.19.grid, bf16[16,256,128]{2,1,0:T(8,128)(2,1)} %get-tuple-element.20._, s32[16,256]{1,0:T(8,128)S(1)} %bitcast.4), custom_call_target="tpu_custom_call", output_to_operand_aliasing={{}: (1, {})} | custom-call | flops 4000000000 | bytes 4194304 | tf_op jit(solution)/shard_map/pallas_call | solution.py:380
  21.7 0.0 copy-start.1
  21.7 0.0 copy-start.2
  21.7 6.4 %all-to-all-done.states = bf16[16,128,128]{2,1,0:T(8,128)(2,1)S(1)} async-done(((bf16[16,128,128]{2,1,0:T(8,128)(2,1)}), bf16[16,128,128]{2,1,0:T(8,128)(2,1)S(1)}, u32[]{:S(2)}, u32[]{:S(2)}) %all-to-all-start) | async-done | bytes 524320 | tf_op jit(solution)/shard_map/all_to_all | solution.py:628
  28.1 4.2 %all-to-all-start.1 = ((bf16[16,256,128]{2,1,0:T(8,128)(2,1)}), bf16[16,256,128]{2,1,0:T(8,128)(2,1)S(1)}, u32[]{:S(2)}, u32[]{:S(2)}) async-start(bf16[16,256,128]{2,1,0:T(8,128)(2,1)} %shard_map.85), calls=%async_computation.1 | async-start | bytes 2097152 | tf_op jit(solution)/shard_map/all_to_all | solution.py:628
  33.0 0.4 shard_map.83
  33.5 22.6 %all-to-all-done.1.second = bf16[16,256,128]{2,1,0:T(8,128)(2,1)S(1)} async-done(((bf16[16,256,128]{2,1,0:T(8,128)(2,1)}), bf16[16,256,128]{2,1,0:T(8,128)(2,1)S(1)}, u32[]{:S(2)}, u32[]{:S(2)}) %all-to-all-start.1) | async-done | bytes 1048608 | tf_op jit(solution)/shard_map/all_to_all | solution.py:628
  56.1 0.0 copy-done.1
  56.1 0.0 copy-done.2
  56.1 2.7 %shard_map.86 = bf16[16,256,128]{2,1,0:T(8,128)(2,1)S(1)} custom-call(bf16[256,1024]{1,0:T(8,128)(2,1)S(1)} %get-tuple-element.14.first, f32[256,128]{1,0:T(8,128)S(1)} %get-tuple-element.15.means, bf16[16,256,128]{2,1,0:T(8,128)(2,1)S(1)} %all-to-all-done.1.second, s32[1,1]{1,0:T(1,128)S(6)} %copy.11.count, f32[1,256]{1,0:T(1,128)S(1)} %bitcast.5, ...), custom_call_target="tpu_custom_call" | custom-call | flops 4000000000 | bytes 4194304 | tf_op jit(solution)/shard_map/pallas_call | solution.py:550
  58.8 30.6 %all_to_all.15.blocks = bf16[16,256,128]{2,1,0:T(8,128)(2,1)S(1)} all-to-all(bf16[16,256,128]{2,1,0:T(8,128)(2,1)S(1)} %shard_map.86), channel_id=1, replica_groups=mesh['grp'=16,'tile'=2] {'grp'}, dimensions={0} | all-to-all | bytes 2097152 | tf_op jit(solution)/shard_map/all_to_all | solution.py:628
  89.4 1.9 %shard_map.87 = bf16[64,2,4,8,128]{4,3,2,1,0:T(8,128)(2,1)} custom-call(bf16[16,256,128]{2,1,0:T(8,128)(2,1)S(1)} %all_to_all.15.blocks), custom_call_target="tpu_custom_call" | custom-call | flops 2000000000 | bytes 2097152 | tf_op jit(solution)/shard_map/pallas_call | solution.py:604
Async XLA Ops:
  4.3 8.4 %collective-permute-start = (f32[2,4,8,64,128]{4,3,2,1,0:T(8,128)S(1)}, f32[2,4,8,64,128]{4,3,2,1,0:T(8,128)}, u32[]{:S(2)}, u32[]{:S(2)}) collective-permute-start(f32[2,4,8,64,128]{4,3,2,1,0:T(8,128)S(1)} %get-tuple-element.16.own), channel_id=1, source_target_pairs={{0,1},{1,0},{2,3},{3,2},{4,5},{5,4},{6,7},{7,6},{8,9},{9,8},{10,11... | collective-permute-start | bytes 6291464 | tf_op jit(solution)/shard_map/ppermute | solution.py:621
  4.8 23.4 %all-to-all-start = ((bf16[16,128,128]{2,1,0:T(8,128)(2,1)}), bf16[16,128,128]{2,1,0:T(8,128)(2,1)S(1)}, u32[]{:S(2)}, u32[]{:S(2)}) async-start(bf16[16,128,128]{2,1,0:T(8,128)(2,1)} %get-tuple-element.13), calls=%async_computation | async-start | bytes 1048576 | tf_op jit(solution)/shard_map/all_to_all | solution.py:628
  12.7 5.2 %copy-start = (s32[1,16,256]{2,1,0:T(8,128)S(1)}, s32[1,16,256]{2,1,0:T(8,128)}, u32[]{:S(2)}) copy-start(s32[1,16,256]{2,1,0:T(8,128)} %param.12) | copy-start | bytes 49156
  21.7 34.4 %copy-start.1 = (f32[1,1,256]{2,1,0:T(1,128)S(1)}, f32[1,1,256]{2,1,0:T(1,128)}, u32[]{:S(2)}) copy-start(f32[1,1,256]{2,1,0:T(1,128)} %param.14) | copy-start | bytes 3076
  21.7 34.4 %copy-start.2 = (f32[1,1,256]{2,1,0:T(1,128)S(1)}, f32[1,1,256]{2,1,0:T(1,128)}, u32[]{:S(2)}) copy-start(f32[1,1,256]{2,1,0:T(1,128)} %param.15) | copy-start | bytes 3076
  28.1 28.0 %all-to-all-start.1 = ((bf16[16,256,128]{2,1,0:T(8,128)(2,1)}), bf16[16,256,128]{2,1,0:T(8,128)(2,1)S(1)}, u32[]{:S(2)}, u32[]{:S(2)}) async-start(bf16[16,256,128]{2,1,0:T(8,128)(2,1)} %shard_map.85), calls=%async_computation.1 | async-start | bytes 2097152 | tf_op jit(solution)/shard_map/all_to_all | solution.py:628

commit v7 on v6

--- a/solution.py
+++ b/solution.py
@@ -124,14 +124,17 @@
         store[:, at : at + 2 * SPAN, :] = value
 
 
-def inner_kernel(variables, own, *refs):
+def inner_kernel(own, *refs):
     raw, (slabs, fields, packed, model) = refs[:3], refs[3:7]
     local, (whole, staged, in_sems, raw_sems, out_sems) = refs[7:10], refs[10:]
-    lanes, levels, span, columns = own.shape
-    members = lanes // variables
+    members, variables, levels, span, columns = own.shape
     count = span - 2 * STEPS
+
     def arrive(level):
-        return pltpu.make_async_copy(own.at[:, level], whole.at[level], in_sems.at[level])
+        return [
+            pltpu.make_async_copy(own.at[:, var, level], whole.at[level, var], in_sems.at[level, var])
+            for var in range(variables)
+        ]
 
     def leave(level):
         size = count * SPAN
@@ -142,7 +145,8 @@
     for copy in copies:
         copy.start()
     for level in range(min(2, levels)):
-        arrive(level).start()
+        for copy in arrive(level):
+            copy.start()
     identity = permutation(columns, 0)
     shifts = both_ways(columns)
     for copy in copies:
@@ -153,18 +157,20 @@
         coefficients = coefficients_of(level, *local)
         for i, one in enumerate(coefficients):
             model[level, i] = one
-        arrive(level).wait()
+        for copy in arrive(level):
+            copy.wait()
 
         @pl.when(level + 2 < levels)
         def _():
-            arrive(level + 2).start()
-
-        view = whole.at[level].reshape(lanes * span, columns)
+            for copy in arrive(level + 2):
+                copy.start()
+
         reads, made = [], []
         for var in range(variables):
+            view = whole.at[level, var].reshape(members * span, columns)
 
             def read(r):
-                rows = view[pl.ds(var * span + r, members, stride=variables * span), :]
+                rows = view[pl.ds(r, members, stride=span), :]
                 reads.append((var, r, rows))
                 return rows.reshape(-1, 8, columns)
 
@@ -185,14 +191,14 @@
         leave(level).wait()
 
 
-def inner(own, raw, variables):
-    lanes, levels, span, columns = own.shape
-    members = lanes // variables
+def inner(own, raw):
+    members, variables, levels, span, columns = own.shape
+    lanes = variables * members
     blocks = columns // SPAN
     count = span - 2 * STEPS
     fixed = [pltpu.with_memory_space_constraint(x, pltpu.HBM) for x in (own, *raw)]
     return pl.pallas_call(
-        functools.partial(inner_kernel, variables),
+        inner_kernel,
         out_shape=[
             jax.ShapeDtypeStruct((variables, levels, span, members, columns), jnp.float32),
             jax.ShapeDtypeStruct((levels, count, lanes, columns), jnp.bfloat16),
@@ -205,9 +211,9 @@
             pltpu.VMEM(raw[0].shape, jnp.float32),
             pltpu.SMEM(raw[1].shape, jnp.float32),
             pltpu.SMEM(raw[2].shape, jnp.float32),
-            pltpu.VMEM((levels, lanes, span, columns), jnp.float32),
+            pltpu.VMEM((levels, variables, members, span, columns), jnp.float32),
             pltpu.VMEM((levels, blocks, count * SPAN, lanes), jnp.bfloat16),
-            pltpu.SemaphoreType.DMA((levels,)),
+            pltpu.SemaphoreType.DMA((levels, variables)),
             pltpu.SemaphoreType.DMA((3,)),
             pltpu.SemaphoreType.DMA((levels,)),
         ],
@@ -630,8 +636,7 @@
 
 def on_device(start, diffusivity, eastward, northward, cells, count, value, weight):
     members, variables, levels, span, columns = dims = start.shape
-    whole = start.reshape(members * variables, levels, span, columns)
-    own, centre, near, model = inner(whole, (diffusivity, eastward, northward), variables)
+    own, centre, near, model = inner(start, (diffusivity, eastward, northward))
     sides = neighbours(own, "tile")
     first, means = prepare(exchange(near))
     grid, packed = outer(dims, own, sides, model, centre, cells.shape[2])

time: 91.7 us -> 91.6 us (level)
  no operation moved by 1% of the time
where the time goes in v7:
time: 91.6 us; the launch traced here: 91.2 us
  blocking collectives  30.6 us (33%)
  waiting for transfers between devices  29.1 us (32%)
  Pallas kernels  18.2 us (20%)
  starting transfers between devices  12.6 us (14%)
    all_to_all x1, blocking collectives, exchange(): lax.all_to_all(blocks, 'grp', split_axis=0, concat_axis=0, tiled=True)  30.6 us
    all_to_all x2, waiting for transfers between devices, exchange(): lax.all_to_all(blocks, 'grp', split_axis=0, concat_axis=0, tiled=True)  29.1 us
    all_to_all x2, starting transfers between devices, exchange(): lax.all_to_all(blocks, 'grp', split_axis=0, concat_axis=0, tiled=True)  12.1 us
    pallas_call x1, Pallas kernels, outer(): pl.pallas_call(functools.partial(outer_kernel, near), out_shape=[jax.Shap...  5.21 us
    pallas_call x1, Pallas kernels, inner(): pl.pallas_call(inner_kernel, out_shape=[jax.ShapeDtypeStruct((variables,...  4.18 us
    pallas_call x1, Pallas kernels, pick(): pl.pallas_call(functools.partial(pick_kernel, variables, together), out_s...  3.74 us
    pallas_call x1, Pallas kernels, analyse(): pl.pallas_call(analyse_kernel, out_shape=jax.ShapeDtypeStruct((groups, ne...  2.7 us
    pallas_call x1, Pallas kernels, restore(): pl.pallas_call(restore_kernel, out_shape=jax.ShapeDtypeStruct((members, v...  1.93 us
  transfers between devices with their start and end apart: 3, of which 2 were waited for; matrix products, arithmetic and copies ran while one was open for 0% of the time, Pallas kernels for 10%

profile of v7, /device:TPU:0, one launch (start us, length us, event | category | flops | bytes accessed | tf_op | source)
XLA Modules:
  0.0 91.2 jit_solution(1780891752097167817)
XLA Ops:
  0.0 4.2 %shard_map.82 = (f32[2,4,8,64,128]{4,3,2,1,0:T(8,128)S(1)}, bf16[4,4,128,128]{3,2,1,0:T(8,128)(2,1)S(1)}, bf16[16,128,128]{2,1,0:T(8,128)(2,1)}, f32[4,5,8,128]{3,2,1,0:T(8,128)S(1)}) custom-call(f32[64,2,4,8,128]{4,3,2,1,0:T(8,128)} %own.1, f32[4,128]{1,0:T(4,128)} %refs_0_.1, f32[4]{0:T(128)} %refs_1_.1, f32[4]{0:T(128)} %refs_2_.1), custom_call_target="tpu_custom_call" | custom-call | flops 2000000000 | bytes 4194304 | tf_op jit(solution)/shard_map/pallas_call | solution.py:200
  4.2 0.5 collective-permute-start
  4.7 7.9 %all-to-all-start = ((bf16[16,128,128]{2,1,0:T(8,128)(2,1)}), bf16[16,128,128]{2,1,0:T(8,128)(2,1)S(1)}, u32[]{:S(2)}, u32[]{:S(2)}) async-start(bf16[16,128,128]{2,1,0:T(8,128)(2,1)} %get-tuple-element.13), calls=%async_computation | async-start | bytes 1048576 | tf_op jit(solution)/shard_map/all_to_all | solution.py:634
  12.6 0.0 collective-permute-done.rest_0_
  12.6 0.0 copy-start
  12.6 5.2 %shard_map.84 = (bf16[4,8,256,128]{3,2,1,0:T(8,128)(2,1)S(1)}, bf16[16,256,128]{2,1,0:T(8,128)(2,1)}) custom-call(f32[2,4,8,64,128]{4,3,2,1,0:T(8,128)S(1)} %get-tuple-element.16.own, f32[2,4,8,64,128]{4,3,2,1,0:T(8,128)} %collective-permute-done.rest_0_, f32[4,5,8,128]{3,2,1,0:T(8,128)S(1)} %get-tuple-element.17.rest_1_, ...), custom_call_target="tpu_custom_call" | custom-call | flops 2000000000 | bytes 8388608 | tf_op jit(solution)/shard_map/pallas_call | solution.py:292
  17.8 0.0 copy-done
  17.8 3.7 %shard_map.85 = bf16[16,256,128]{2,1,0:T(8,128)(2,1)} custom-call(bf16[4,8,256,128]{3,2,1,0:T(8,128)(2,1)S(1)} %get-tuple-element.19.grid, bf16[16,256,128]{2,1,0:T(8,128)(2,1)} %get-tuple-element.20._, s32[16,256]{1,0:T(8,128)S(1)} %bitcast.3), custom_call_target="tpu_custom_call", output_to_operand_aliasing={{}: (1, {})} | custom-call | flops 4000000000 | bytes 4194304 | tf_op jit(solution)/shard_map/pallas_call | solution.py:386
  21.6 0.0 copy-start.1
  21.6 0.0 copy-start.2
  21.6 6.4 %all-to-all-done.states = bf16[16,128,128]{2,1,0:T(8,128)(2,1)S(1)} async-done(((bf16[16,128,128]{2,1,0:T(8,128)(2,1)}), bf16[16,128,128]{2,1,0:T(8,128)(2,1)S(1)}, u32[]{:S(2)}, u32[]{:S(2)}) %all-to-all-start) | async-done | bytes 524320 | tf_op jit(solution)/shard_map/all_to_all | solution.py:634
  28.1 4.2 %all-to-all-start.1 = ((bf16[16,256,128]{2,1,0:T(8,128)(2,1)}), bf16[16,256,128]{2,1,0:T(8,128)(2,1)S(1)}, u32[]{:S(2)}, u32[]{:S(2)}) async-start(bf16[16,256,128]{2,1,0:T(8,128)(2,1)} %shard_map.85), calls=%async_computation.1 | async-start | bytes 2097152 | tf_op jit(solution)/shard_map/all_to_all | solution.py:634
  32.9 0.4 shard_map.83
  33.4 22.6 %all-to-all-done.1.second = bf16[16,256,128]{2,1,0:T(8,128)(2,1)S(1)} async-done(((bf16[16,256,128]{2,1,0:T(8,128)(2,1)}), bf16[16,256,128]{2,1,0:T(8,128)(2,1)S(1)}, u32[]{:S(2)}, u32[]{:S(2)}) %all-to-all-start.1) | async-done | bytes 1048608 | tf_op jit(solution)/shard_map/all_to_all | solution.py:634
  56.0 0.0 copy-done.1
  56.0 0.0 copy-done.2
  56.0 2.7 %shard_map.86 = bf16[16,256,128]{2,1,0:T(8,128)(2,1)S(1)} custom-call(bf16[256,1024]{1,0:T(8,128)(2,1)S(1)} %get-tuple-element.14.first, f32[256,128]{1,0:T(8,128)S(1)} %get-tuple-element.15.means, bf16[16,256,128]{2,1,0:T(8,128)(2,1)S(1)} %all-to-all-done.1.second, s32[1,1]{1,0:T(1,128)S(6)} %copy.11.count, f32[1,256]{1,0:T(1,128)S(1)} %bitcast.4, ...), custom_call_target="tpu_custom_call" | custom-call | flops 4000000000 | bytes 4194304 | tf_op jit(solution)/shard_map/pallas_call | solution.py:556
  58.7 30.6 %all_to_all.15.blocks = bf16[16,256,128]{2,1,0:T(8,128)(2,1)S(1)} all-to-all(bf16[16,256,128]{2,1,0:T(8,128)(2,1)S(1)} %shard_map.86), channel_id=1, replica_groups=mesh['grp'=16,'tile'=2] {'grp'}, dimensions={0} | all-to-all | bytes 2097152 | tf_op jit(solution)/shard_map/all_to_all | solution.py:634
  89.3 1.9 %shard_map.87 = bf16[64,2,4,8,128]{4,3,2,1,0:T(8,128)(2,1)} custom-call(bf16[16,256,128]{2,1,0:T(8,128)(2,1)S(1)} %all_to_all.15.blocks), custom_call_target="tpu_custom_call" | custom-call | flops 2000000000 | bytes 2097152 | tf_op jit(solution)/shard_map/pallas_call | solution.py:610
Async XLA Ops:
  4.2 8.4 %collective-permute-start = (f32[2,4,8,64,128]{4,3,2,1,0:T(8,128)S(1)}, f32[2,4,8,64,128]{4,3,2,1,0:T(8,128)}, u32[]{:S(2)}, u32[]{:S(2)}) collective-permute-start(f32[2,4,8,64,128]{4,3,2,1,0:T(8,128)S(1)} %get-tuple-element.16.own), channel_id=1, source_target_pairs={{0,1},{1,0},{2,3},{3,2},{4,5},{5,4},{6,7},{7,6},{8,9},{9,8},{10,11... | collective-permute-start | bytes 6291464 | tf_op jit(solution)/shard_map/ppermute | solution.py:627
  4.7 23.4 %all-to-all-start = ((bf16[16,128,128]{2,1,0:T(8,128)(2,1)}), bf16[16,128,128]{2,1,0:T(8,128)(2,1)S(1)}, u32[]{:S(2)}, u32[]{:S(2)}) async-start(bf16[16,128,128]{2,1,0:T(8,128)(2,1)} %get-tuple-element.13), calls=%async_computation | async-start | bytes 1048576 | tf_op jit(solution)/shard_map/all_to_all | solution.py:634
  12.6 5.2 %copy-start = (s32[1,16,256]{2,1,0:T(8,128)S(1)}, s32[1,16,256]{2,1,0:T(8,128)}, u32[]{:S(2)}) copy-start(s32[1,16,256]{2,1,0:T(8,128)} %param.12) | copy-start | bytes 49156
  21.6 34.4 %copy-start.1 = (f32[1,1,256]{2,1,0:T(1,128)S(1)}, f32[1,1,256]{2,1,0:T(1,128)}, u32[]{:S(2)}) copy-start(f32[1,1,256]{2,1,0:T(1,128)} %param.14) | copy-start | bytes 3076
  21.6 34.4 %copy-start.2 = (f32[1,1,256]{2,1,0:T(1,128)S(1)}, f32[1,1,256]{2,1,0:T(1,128)}, u32[]{:S(2)}) copy-start(f32[1,1,256]{2,1,0:T(1,128)} %param.15) | copy-start | bytes 3076
  28.1 28.0 %all-to-all-start.1 = ((bf16[16,256,128]{2,1,0:T(8,128)(2,1)}), bf16[16,256,128]{2,1,0:T(8,128)(2,1)S(1)}, u32[]{:S(2)}, u32[]{:S(2)}) async-start(bf16[16,256,128]{2,1,0:T(8,128)(2,1)} %shard_map.85), calls=%async_computation.1 | async-start | bytes 2097152 | tf_op jit(solution)/shard_map/all_to_all | solution.py:634

commit v8 on v7

--- a/solution.py
+++ b/solution.py
@@ -130,11 +130,10 @@
     members, variables, levels, span, columns = own.shape
     count = span - 2 * STEPS
 
-    def arrive(level):
-        return [
-            pltpu.make_async_copy(own.at[:, var, level], whole.at[level, var], in_sems.at[level, var])
-            for var in range(variables)
-        ]
+    arrivals = [
+        pltpu.make_async_copy(own.at[:, var], whole.at[var], in_sems.at[var])
+        for var in range(variables)
+    ]
 
     def leave(level):
         size = count * SPAN
@@ -144,48 +143,44 @@
     copies = [pltpu.make_async_copy(x, y, raw_sems.at[i]) for i, (x, y) in enumerate(zip(raw, local))]
     for copy in copies:
         copy.start()
-    for level in range(min(2, levels)):
-        for copy in arrive(level):
-            copy.start()
+    for copy in arrivals:
+        copy.start()
     identity = permutation(columns, 0)
     shifts = both_ways(columns)
     for copy in copies:
         copy.wait()
 
-    @pl.loop(0, levels)
-    def _(level):
-        coefficients = coefficients_of(level, *local)
-        for i, one in enumerate(coefficients):
-            model[level, i] = one
-        for copy in arrive(level):
-            copy.wait()
-
-        @pl.when(level + 2 < levels)
-        def _():
-            for copy in arrive(level + 2):
-                copy.start()
-
-        reads, made = [], []
-        for var in range(variables):
-            view = whole.at[level, var].reshape(members * span, columns)
+    for var in range(variables):
+        arrivals[var].wait()
+        view = whole.at[var].reshape(members * levels * span, columns)
+
+        @pl.loop(0, levels)
+        def _(level):
+            coefficients = coefficients_of(level, *local)
+            reads = []
 
             def read(r):
-                rows = view[pl.ds(r, members, stride=span), :]
-                reads.append((var, r, rows))
+                rows = view[pl.ds(level * span + r, members, stride=levels * span), :]
+                reads.append((r, rows))
                 return rows.reshape(-1, 8, columns)
 
-            for r, value in forecast_rows(read, STEPS, span - STEPS, coefficients, shifts):
-                made.append((var, r, value))
-        pairs = []
-        for first in range(STEPS, span - STEPS, 2):
-            rows = [one for r in (first, first + 1) for _, at, one in made if at == r]
-            pairs.append(jnp.concatenate(rows, axis=0))
-        pack_rows(pairs, identity, staged.at[level], 0)
-        leave(level).start()
-        for var, r, value in made:
-            fields[level, r - STEPS, var * members : (var + 1) * members, :] = value
-        for var, r, rows in reads:
-            slabs[var, level, r] = rows
+            made = forecast_rows(read, STEPS, span - STEPS, coefficients, shifts)
+            if var == variables - 1:
+                pairs = []
+                for first in range(STEPS, span - STEPS, 2):
+                    rows = []
+                    for r in (first, first + 1):
+                        rows += [fields[level, r - STEPS, : var * members, :]] if var else []
+                        rows += [one for at, one in made if at == r]
+                    pairs.append(jnp.concatenate(rows, axis=0))
+                pack_rows(pairs, identity, staged.at[level], 0)
+                leave(level).start()
+                for i, one in enumerate(coefficients):
+                    model[level, i] = one
+            for r, value in made:
+                fields[level, r - STEPS, var * members : (var + 1) * members, :] = value
+            for r, rows in reads:
+                slabs[var, level, r] = rows
 
     for level in range(levels):
         leave(level).wait()
@@ -211,9 +206,9 @@
             pltpu.VMEM(raw[0].shape, jnp.float32),
             pltpu.SMEM(raw[1].shape, jnp.float32),
             pltpu.SMEM(raw[2].shape, jnp.float32),
-            pltpu.VMEM((levels, variables, members, span, columns), jnp.float32),
+            pltpu.VMEM((variables, members, levels, span, columns), jnp.float32),
             pltpu.VMEM((levels, blocks, count * SPAN, lanes), jnp.bfloat16),
-            pltpu.SemaphoreType.DMA((levels, variables)),
+            pltpu.SemaphoreType.DMA((variables,)),
             pltpu.SemaphoreType.DMA((3,)),
             pltpu.SemaphoreType.DMA((levels,)),
         ],

time: 91.6 us -> 92.8 us (1.013)
  Pallas kernels: 18.2 us -> 19.4 us
    pallas_call x1, Pallas kernels: 4.18 us -> 5.37 us  [inner(): pl.pallas_call(inner_kernel, out_shape=[jax.ShapeDtypeStruct((variables,...]
where the time goes in v8:
time: 92.8 us; the launch traced here: 92.4 us
  blocking collectives  30.6 us (33%)
  waiting for transfers between devices  29.1 us (31%)
  Pallas kernels  19.4 us (21%)
  starting transfers between devices  12.6 us (14%)
    all_to_all x1, blocking collectives, exchange(): lax.all_to_all(blocks, 'grp', split_axis=0, concat_axis=0, tiled=True)  30.6 us
    all_to_all x2, waiting for transfers between devices, exchange(): lax.all_to_all(blocks, 'grp', split_axis=0, concat_axis=0, tiled=True)  29.1 us
    all_to_all x2, starting transfers between devices, exchange(): lax.all_to_all(blocks, 'grp', split_axis=0, concat_axis=0, tiled=True)  12.1 us
    pallas_call x1, Pallas kernels, inner(): pl.pallas_call(inner_kernel, out_shape=[jax.ShapeDtypeStruct((variables,...  5.37 us
    pallas_call x1, Pallas kernels, outer(): pl.pallas_call(functools.partial(outer_kernel, near), out_shape=[jax.Shap...  5.21 us
    pallas_call x1, Pallas kernels, pick(): pl.pallas_call(functools.partial(pick_kernel, variables, together), out_s...  3.74 us
    pallas_call x1, Pallas kernels, analyse(): pl.pallas_call(analyse_kernel, out_shape=jax.ShapeDtypeStruct((groups, ne...  2.7 us
    pallas_call x1, Pallas kernels, restore(): pl.pallas_call(restore_kernel, out_shape=jax.ShapeDtypeStruct((members, v...  1.93 us
  transfers between devices with their start and end apart: 3, of which 2 were waited for; matrix products, arithmetic and copies ran while one was open for 0% of the time, Pallas kernels for 10%

profile of v8, /device:TPU:0, one launch (start us, length us, event | category | flops | bytes accessed | tf_op | source)
XLA Modules:
  0.0 92.4 jit_solution(3994409179464960660)
XLA Ops:
  0.0 5.4 %shard_map.82 = (f32[2,4,8,64,128]{4,3,2,1,0:T(8,128)S(1)}, bf16[4,4,128,128]{3,2,1,0:T(8,128)(2,1)S(1)}, bf16[16,128,128]{2,1,0:T(8,128)(2,1)}, f32[4,5,8,128]{3,2,1,0:T(8,128)S(1)}) custom-call(f32[64,2,4,8,128]{4,3,2,1,0:T(8,128)} %own.1, f32[4,128]{1,0:T(4,128)} %refs_0_.1, f32[4]{0:T(128)} %refs_1_.1, f32[4]{0:T(128)} %refs_2_.1), custom_call_target="tpu_custom_call" | custom-call | flops 2000000000 | bytes 4194304 | tf_op jit(solution)/shard_map/pallas_call | solution.py:195
  5.4 0.5 collective-permute-start
  5.9 7.9 %all-to-all-start = ((bf16[16,128,128]{2,1,0:T(8,128)(2,1)}), bf16[16,128,128]{2,1,0:T(8,128)(2,1)S(1)}, u32[]{:S(2)}, u32[]{:S(2)}) async-start(bf16[16,128,128]{2,1,0:T(8,128)(2,1)} %get-tuple-element.13), calls=%async_computation | async-start | bytes 1048576 | tf_op jit(solution)/shard_map/all_to_all | solution.py:629
  13.8 0.0 collective-permute-done.rest_0_
  13.8 0.0 copy-start
  13.8 5.2 %shard_map.84 = (bf16[4,8,256,128]{3,2,1,0:T(8,128)(2,1)S(1)}, bf16[16,256,128]{2,1,0:T(8,128)(2,1)}) custom-call(f32[2,4,8,64,128]{4,3,2,1,0:T(8,128)S(1)} %get-tuple-element.16.own, f32[2,4,8,64,128]{4,3,2,1,0:T(8,128)} %collective-permute-done.rest_0_, f32[4,5,8,128]{3,2,1,0:T(8,128)S(1)} %get-tuple-element.17.rest_1_, ...), custom_call_target="tpu_custom_call" | custom-call | flops 2000000000 | bytes 8388608 | tf_op jit(solution)/shard_map/pallas_call | solution.py:287
  19.0 0.0 copy-done
  19.0 3.7 %shard_map.85 = bf16[16,256,128]{2,1,0:T(8,128)(2,1)} custom-call(bf16[4,8,256,128]{3,2,1,0:T(8,128)(2,1)S(1)} %get-tuple-element.19.grid, bf16[16,256,128]{2,1,0:T(8,128)(2,1)} %get-tuple-element.20._, s32[16,256]{1,0:T(8,128)S(1)} %bitcast.3), custom_call_target="tpu_custom_call", output_to_operand_aliasing={{}: (1, {})} | custom-call | flops 4000000000 | bytes 4194304 | tf_op jit(solution)/shard_map/pallas_call | solution.py:381
  22.8 0.0 copy-start.1
  22.8 0.0 copy-start.2
  22.8 6.4 %all-to-all-done.states = bf16[16,128,128]{2,1,0:T(8,128)(2,1)S(1)} async-done(((bf16[16,128,128]{2,1,0:T(8,128)(2,1)}), bf16[16,128,128]{2,1,0:T(8,128)(2,1)S(1)}, u32[]{:S(2)}, u32[]{:S(2)}) %all-to-all-start) | async-done | bytes 524320 | tf_op jit(solution)/shard_map/all_to_all | solution.py:629
  29.2 4.2 %all-to-all-start.1 = ((bf16[16,256,128]{2,1,0:T(8,128)(2,1)}), bf16[16,256,128]{2,1,0:T(8,128)(2,1)S(1)}, u32[]{:S(2)}, u32[]{:S(2)}) async-start(bf16[16,256,128]{2,1,0:T(8,128)(2,1)} %shard_map.85), calls=%async_computation.1 | async-start | bytes 2097152 | tf_op jit(solution)/shard_map/all_to_all | solution.py:629
  34.1 0.4 shard_map.83
  34.6 22.6 %all-to-all-done.1.second = bf16[16,256,128]{2,1,0:T(8,128)(2,1)S(1)} async-done(((bf16[16,256,128]{2,1,0:T(8,128)(2,1)}), bf16[16,256,128]{2,1,0:T(8,128)(2,1)S(1)}, u32[]{:S(2)}, u32[]{:S(2)}) %all-to-all-start.1) | async-done | bytes 1048608 | tf_op jit(solution)/shard_map/all_to_all | solution.py:629
  57.2 0.0 copy-done.1
  57.2 0.0 copy-done.2
  57.2 2.7 %shard_map.86 = bf16[16,256,128]{2,1,0:T(8,128)(2,1)S(1)} custom-call(bf16[256,1024]{1,0:T(8,128)(2,1)S(1)} %get-tuple-element.14.first, f32[256,128]{1,0:T(8,128)S(1)} %get-tuple-element.15.means, bf16[16,256,128]{2,1,0:T(8,128)(2,1)S(1)} %all-to-all-done.1.second, s32[1,1]{1,0:T(1,128)S(6)} %copy.11.count, f32[1,256]{1,0:T(1,128)S(1)} %bitcast.4, ...), custom_call_target="tpu_custom_call" | custom-call | flops 4000000000 | bytes 4194304 | tf_op jit(solution)/shard_map/pallas_call | solution.py:551
  59.9 30.6 %all_to_all.15.blocks = bf16[16,256,128]{2,1,0:T(8,128)(2,1)S(1)} all-to-all(bf16[16,256,128]{2,1,0:T(8,128)(2,1)S(1)} %shard_map.86), channel_id=1, replica_groups=mesh['grp'=16,'tile'=2] {'grp'}, dimensions={0} | all-to-all | bytes 2097152 | tf_op jit(solution)/shard_map/all_to_all | solution.py:629
  90.5 1.9 %shard_map.87 = bf16[64,2,4,8,128]{4,3,2,1,0:T(8,128)(2,1)} custom-call(bf16[16,256,128]{2,1,0:T(8,128)(2,1)S(1)} %all_to_all.15.blocks), custom_call_target="tpu_custom_call" | custom-call | flops 2000000000 | bytes 2097152 | tf_op jit(solution)/shard_map/pallas_call | solution.py:605
Async XLA Ops:
  5.4 8.4 %collective-permute-start = (f32[2,4,8,64,128]{4,3,2,1,0:T(8,128)S(1)}, f32[2,4,8,64,128]{4,3,2,1,0:T(8,128)}, u32[]{:S(2)}, u32[]{:S(2)}) collective-permute-start(f32[2,4,8,64,128]{4,3,2,1,0:T(8,128)S(1)} %get-tuple-element.16.own), channel_id=1, source_target_pairs={{0,1},{1,0},{2,3},{3,2},{4,5},{5,4},{6,7},{7,6},{8,9},{9,8},{10,11... | collective-permute-start | bytes 6291464 | tf_op jit(solution)/shard_map/ppermute | solution.py:622
  5.9 23.4 %all-to-all-start = ((bf16[16,128,128]{2,1,0:T(8,128)(2,1)}), bf16[16,128,128]{2,1,0:T(8,128)(2,1)S(1)}, u32[]{:S(2)}, u32[]{:S(2)}) async-start(bf16[16,128,128]{2,1,0:T(8,128)(2,1)} %get-tuple-element.13), calls=%async_computation | async-start | bytes 1048576 | tf_op jit(solution)/shard_map/all_to_all | solution.py:629
  13.8 5.2 %copy-start = (s32[1,16,256]{2,1,0:T(8,128)S(1)}, s32[1,16,256]{2,1,0:T(8,128)}, u32[]{:S(2)}) copy-start(s32[1,16,256]{2,1,0:T(8,128)} %param.12) | copy-start | bytes 49156
  22.8 34.4 %copy-start.1 = (f32[1,1,256]{2,1,0:T(1,128)S(1)}, f32[1,1,256]{2,1,0:T(1,128)}, u32[]{:S(2)}) copy-start(f32[1,1,256]{2,1,0:T(1,128)} %param.14) | copy-start | bytes 3076
  22.8 34.4 %copy-start.2 = (f32[1,1,256]{2,1,0:T(1,128)S(1)}, f32[1,1,256]{2,1,0:T(1,128)}, u32[]{:S(2)}) copy-start(f32[1,1,256]{2,1,0:T(1,128)} %param.15) | copy-start | bytes 3076
  29.2 28.0 %all-to-all-start.1 = ((bf16[16,256,128]{2,1,0:T(8,128)(2,1)}), bf16[16,256,128]{2,1,0:T(8,128)(2,1)S(1)}, u32[]{:S(2)}, u32[]{:S(2)}) async-start(bf16[16,256,128]{2,1,0:T(8,128)(2,1)} %shard_map.85), calls=%async_computation.1 | async-start | bytes 2097152 | tf_op jit(solution)/shard_map/all_to_all | solution.py:629

commit v9 on v7

--- a/solution.py
+++ b/solution.py
@@ -131,10 +131,13 @@
     count = span - 2 * STEPS
 
     def arrive(level):
-        return [
-            pltpu.make_async_copy(own.at[:, var, level], whole.at[level, var], in_sems.at[level, var])
-            for var in range(variables)
-        ]
+        copies = []
+        for var in range(variables):
+            for half in range(2):
+                here = pl.ds(half * (members // 2), members // 2)
+                source, place = own.at[here, var, level], whole.at[level, var, here]
+                copies.append(pltpu.make_async_copy(source, place, in_sems.at[level, var, half]))
+        return copies
 
     def leave(level):
         size = count * SPAN
@@ -144,7 +147,7 @@
     copies = [pltpu.make_async_copy(x, y, raw_sems.at[i]) for i, (x, y) in enumerate(zip(raw, local))]
     for copy in copies:
         copy.start()
-    for level in range(min(2, levels)):
+    for level in range(levels):
         for copy in arrive(level):
             copy.start()
     identity = permutation(columns, 0)
@@ -159,12 +162,6 @@
             model[level, i] = one
         for copy in arrive(level):
             copy.wait()
-
-        @pl.when(level + 2 < levels)
-        def _():
-            for copy in arrive(level + 2):
-                copy.start()
-
         reads, made = [], []
         for var in range(variables):
             view = whole.at[level, var].reshape(members * span, columns)
@@ -213,7 +210,7 @@
             pltpu.SMEM(raw[2].shape, jnp.float32),
             pltpu.VMEM((levels, variables, members, span, columns), jnp.float32),
             pltpu.VMEM((levels, blocks, count * SPAN, lanes), jnp.bfloat16),
-            pltpu.SemaphoreType.DMA((levels, variables)),
+            pltpu.SemaphoreType.DMA((levels, variables, 2)),
             pltpu.SemaphoreType.DMA((3,)),
             pltpu.SemaphoreType.DMA((levels,)),
         ],
@@ -582,9 +579,9 @@
             else:
                 at = levels * near + level * 2 * STEPS + (r if r < STEPS else r - near)
             both = blocks[:, at * SPAN : (at + 2) * SPAN, :].astype(jnp.float32)
-            for i in range(2):
-                one = both[:, i * SPAN : (i + 1) * SPAN, :].reshape(columns, lanes)
-                made.append((r + i, dot_rows(identity, one.astype(jnp.bfloat16))))
+            pair = [both[:, i * SPAN : (i + 1) * SPAN, :].reshape(columns, lanes) for i in range(2)]
+            rows = dot_rows(identity, jnp.concatenate(pair, axis=0).astype(jnp.bfloat16))
+            made += [(r + i, rows[:, i * columns : (i + 1) * columns]) for i in range(2)]
         for r, rows in made:
             turned[level, pl.ds(r, lanes, stride=span), :] = rows
 

time: 91.6 us -> 91.8 us (level)
  no operation moved by 1% of the time
where the time goes in v9:
time: 91.8 us; the launch traced here: 91.4 us
  blocking collectives  30.6 us (33%)
  waiting for transfers between devices  29.1 us (32%)
  Pallas kernels  18.4 us (20%)
  starting transfers between devices  12.6 us (14%)
    all_to_all x1, blocking collectives, exchange(): lax.all_to_all(blocks, 'grp', split_axis=0, concat_axis=0, tiled=True)  30.6 us
    all_to_all x2, waiting for transfers between devices, exchange(): lax.all_to_all(blocks, 'grp', split_axis=0, concat_axis=0, tiled=True)  29.1 us
    all_to_all x2, starting transfers between devices, exchange(): lax.all_to_all(blocks, 'grp', split_axis=0, concat_axis=0, tiled=True)  12.1 us
    pallas_call x1, Pallas kernels, outer(): pl.pallas_call(functools.partial(outer_kernel, near), out_shape=[jax.Shap...  5.22 us
    pallas_call x1, Pallas kernels, inner(): pl.pallas_call(inner_kernel, out_shape=[jax.ShapeDtypeStruct((variables,...  4.58 us
    pallas_call x1, Pallas kernels, pick(): pl.pallas_call(functools.partial(pick_kernel, variables, together), out_s...  3.74 us
    pallas_call x1, Pallas kernels, analyse(): pl.pallas_call(analyse_kernel, out_shape=jax.ShapeDtypeStruct((groups, ne...  2.7 us
  transfers between devices with their start and end apart: 3, of which 2 were waited for; matrix products, arithmetic and copies ran while one was open for 0% of the time, Pallas kernels for 10%

profile of v9, /device:TPU:0, one launch (start us, length us, event | category | flops | bytes accessed | tf_op | source)
XLA Modules:
  0.0 91.4 jit_solution(12469932462488656147)
XLA Ops:
  0.0 4.6 %shard_map.82 = (f32[2,4,8,64,128]{4,3,2,1,0:T(8,128)S(1)}, bf16[4,4,128,128]{3,2,1,0:T(8,128)(2,1)S(1)}, bf16[16,128,128]{2,1,0:T(8,128)(2,1)}, f32[4,5,8,128]{3,2,1,0:T(8,128)S(1)}) custom-call(f32[64,2,4,8,128]{4,3,2,1,0:T(8,128)} %own.1, f32[4,128]{1,0:T(4,128)} %refs_0_.1, f32[4]{0:T(128)} %refs_1_.1, f32[4]{0:T(128)} %refs_2_.1), custom_call_target="tpu_custom_call" | custom-call | flops 2000000000 | bytes 4194304 | tf_op jit(solution)/shard_map/pallas_call | solution.py:197
  4.6 0.5 collective-permute-start
  5.1 7.9 %all-to-all-start = ((bf16[16,128,128]{2,1,0:T(8,128)(2,1)}), bf16[16,128,128]{2,1,0:T(8,128)(2,1)S(1)}, u32[]{:S(2)}, u32[]{:S(2)}) async-start(bf16[16,128,128]{2,1,0:T(8,128)(2,1)} %get-tuple-element.13), calls=%async_computation | async-start | bytes 1048576 | tf_op jit(solution)/shard_map/all_to_all | solution.py:631
  13.0 0.0 collective-permute-done.rest_0_
  13.0 0.0 copy-start
  13.0 5.2 %shard_map.84 = (bf16[4,8,256,128]{3,2,1,0:T(8,128)(2,1)S(1)}, bf16[16,256,128]{2,1,0:T(8,128)(2,1)}) custom-call(f32[2,4,8,64,128]{4,3,2,1,0:T(8,128)S(1)} %get-tuple-element.16.own, f32[2,4,8,64,128]{4,3,2,1,0:T(8,128)} %collective-permute-done.rest_0_, f32[4,5,8,128]{3,2,1,0:T(8,128)S(1)} %get-tuple-element.17.rest_1_, ...), custom_call_target="tpu_custom_call" | custom-call | flops 2000000000 | bytes 8388608 | tf_op jit(solution)/shard_map/pallas_call | solution.py:289
  18.3 0.0 copy-done
  18.3 3.7 %shard_map.85 = bf16[16,256,128]{2,1,0:T(8,128)(2,1)} custom-call(bf16[4,8,256,128]{3,2,1,0:T(8,128)(2,1)S(1)} %get-tuple-element.19.grid, bf16[16,256,128]{2,1,0:T(8,128)(2,1)} %get-tuple-element.20._, s32[16,256]{1,0:T(8,128)S(1)} %bitcast.3), custom_call_target="tpu_custom_call", output_to_operand_aliasing={{}: (1, {})} | custom-call | flops 4000000000 | bytes 4194304 | tf_op jit(solution)/shard_map/pallas_call | solution.py:383
  22.0 0.0 copy-start.1
  22.0 0.0 copy-start.2
  22.0 6.4 %all-to-all-done.states = bf16[16,128,128]{2,1,0:T(8,128)(2,1)S(1)} async-done(((bf16[16,128,128]{2,1,0:T(8,128)(2,1)}), bf16[16,128,128]{2,1,0:T(8,128)(2,1)S(1)}, u32[]{:S(2)}, u32[]{:S(2)}) %all-to-all-start) | async-done | bytes 524320 | tf_op jit(solution)/shard_map/all_to_all | solution.py:631
  28.5 4.2 %all-to-all-start.1 = ((bf16[16,256,128]{2,1,0:T(8,128)(2,1)}), bf16[16,256,128]{2,1,0:T(8,128)(2,1)S(1)}, u32[]{:S(2)}, u32[]{:S(2)}) async-start(bf16[16,256,128]{2,1,0:T(8,128)(2,1)} %shard_map.85), calls=%async_computation.1 | async-start | bytes 2097152 | tf_op jit(solution)/shard_map/all_to_all | solution.py:631
  33.3 0.4 shard_map.83
  33.8 22.6 %all-to-all-done.1.second = bf16[16,256,128]{2,1,0:T(8,128)(2,1)S(1)} async-done(((bf16[16,256,128]{2,1,0:T(8,128)(2,1)}), bf16[16,256,128]{2,1,0:T(8,128)(2,1)S(1)}, u32[]{:S(2)}, u32[]{:S(2)}) %all-to-all-start.1) | async-done | bytes 1048608 | tf_op jit(solution)/shard_map/all_to_all | solution.py:631
  56.4 0.0 copy-done.1
  56.4 0.0 copy-done.2
  56.4 2.7 %shard_map.86 = bf16[16,256,128]{2,1,0:T(8,128)(2,1)S(1)} custom-call(bf16[256,1024]{1,0:T(8,128)(2,1)S(1)} %get-tuple-element.14.first, f32[256,128]{1,0:T(8,128)S(1)} %get-tuple-element.15.means, bf16[16,256,128]{2,1,0:T(8,128)(2,1)S(1)} %all-to-all-done.1.second, s32[1,1]{1,0:T(1,128)S(6)} %copy.11.count, f32[1,256]{1,0:T(1,128)S(1)} %bitcast.4, ...), custom_call_target="tpu_custom_call" | custom-call | flops 4000000000 | bytes 4194304 | tf_op jit(solution)/shard_map/pallas_call | solution.py:553
  59.1 30.6 %all_to_all.15.blocks = bf16[16,256,128]{2,1,0:T(8,128)(2,1)S(1)} all-to-all(bf16[16,256,128]{2,1,0:T(8,128)(2,1)S(1)} %shard_map.86), channel_id=1, replica_groups=mesh['grp'=16,'tile'=2] {'grp'}, dimensions={0} | all-to-all | bytes 2097152 | tf_op jit(solution)/shard_map/all_to_all | solution.py:631
  89.7 1.7 %shard_map.87 = bf16[64,2,4,8,128]{4,3,2,1,0:T(8,128)(2,1)} custom-call(bf16[16,256,128]{2,1,0:T(8,128)(2,1)S(1)} %all_to_all.15.blocks), custom_call_target="tpu_custom_call" | custom-call | flops 2000000000 | bytes 2097152 | tf_op jit(solution)/shard_map/pallas_call | solution.py:607
Async XLA Ops:
  4.6 8.4 %collective-permute-start = (f32[2,4,8,64,128]{4,3,2,1,0:T(8,128)S(1)}, f32[2,4,8,64,128]{4,3,2,1,0:T(8,128)}, u32[]{:S(2)}, u32[]{:S(2)}) collective-permute-start(f32[2,4,8,64,128]{4,3,2,1,0:T(8,128)S(1)} %get-tuple-element.16.own), channel_id=1, source_target_pairs={{0,1},{1,0},{2,3},{3,2},{4,5},{5,4},{6,7},{7,6},{8,9},{9,8},{10,11... | collective-permute-start | bytes 6291464 | tf_op jit(solution)/shard_map/ppermute | solution.py:624
  5.1 23.4 %all-to-all-start = ((bf16[16,128,128]{2,1,0:T(8,128)(2,1)}), bf16[16,128,128]{2,1,0:T(8,128)(2,1)S(1)}, u32[]{:S(2)}, u32[]{:S(2)}) async-start(bf16[16,128,128]{2,1,0:T(8,128)(2,1)} %get-tuple-element.13), calls=%async_computation | async-start | bytes 1048576 | tf_op jit(solution)/shard_map/all_to_all | solution.py:631
  13.0 5.2 %copy-start = (s32[1,16,256]{2,1,0:T(8,128)S(1)}, s32[1,16,256]{2,1,0:T(8,128)}, u32[]{:S(2)}) copy-start(s32[1,16,256]{2,1,0:T(8,128)} %param.12) | copy-start | bytes 49156
  22.0 34.4 %copy-start.1 = (f32[1,1,256]{2,1,0:T(1,128)S(1)}, f32[1,1,256]{2,1,0:T(1,128)}, u32[]{:S(2)}) copy-start(f32[1,1,256]{2,1,0:T(1,128)} %param.14) | copy-start | bytes 3076
  22.0 34.4 %copy-start.2 = (f32[1,1,256]{2,1,0:T(1,128)S(1)}, f32[1,1,256]{2,1,0:T(1,128)}, u32[]{:S(2)}) copy-start(f32[1,1,256]{2,1,0:T(1,128)} %param.15) | copy-start | bytes 3076
  28.5 28.0 %all-to-all-start.1 = ((bf16[16,256,128]{2,1,0:T(8,128)(2,1)}), bf16[16,256,128]{2,1,0:T(8,128)(2,1)S(1)}, u32[]{:S(2)}, u32[]{:S(2)}) async-start(bf16[16,256,128]{2,1,0:T(8,128)(2,1)} %shard_map.85), calls=%async_computation.1 | async-start | bytes 2097152 | tf_op jit(solution)/shard_map/all_to_all | solution.py:631

commit v10 on v7

--- a/solution.py
+++ b/solution.py
@@ -400,34 +400,27 @@
     )(grid, packed, cells)
 
 
-def join(a, b, left, members):
+def join(a, b, members):
     return (
-        jnp.where(left, a, pltpu.roll(b, members, 1)),
-        jnp.where(left, pltpu.roll(a, members, 1), b),
+        jnp.concatenate([a[:, :members], b[:, :members]], axis=1),
+        jnp.concatenate([a[:, members:], b[:, members:]], axis=1),
     )
 
 
 def batches(count, size):
     return [range(at, min(count, at + size)) for at in range(0, count, size)]
-
-
-def left_lanes(shape):
-    return lax.broadcasted_iota(jnp.int32, shape, 1) < shape[1] // 2
 
 
 def deviations(states, raw, dev, at, size):
     groups, _, lanes = states.shape
     members = lanes // 2
-    left = left_lanes((size, lanes))
     sums = [jnp.zeros((size, lanes), jnp.float32)] * 2
     for batch in batches(groups // 2, 4):
         made = [
-            join(
-                states[2 * j, :size, :].astype(jnp.float32),
-                states[2 * j + 1, :size, :].astype(jnp.float32),
-                left,
-                members,
-            )
+            [
+                x.astype(jnp.float32)
+                for x in join(states[2 * j, :size, :], states[2 * j + 1, :size, :], members)
+            ]
             for j in batch
         ]
         for j, pair in zip(batch, made):
@@ -472,16 +465,13 @@
     slots = 2 * half
     members = lanes // 2
     total_members = groups * members
-    left = left_lanes((half, lanes))
 
     for batch in batches(groups // 2, 4):
         made = [
-            join(
-                second[2 * j, far:, :].astype(jnp.float32),
-                second[2 * j + 1, far:, :].astype(jnp.float32),
-                left,
-                members,
-            )
+            [
+                x.astype(jnp.float32)
+                for x in join(second[2 * j, far:, :], second[2 * j + 1, far:, :], members)
+            ]
             for j in batch
         ]
         for j, pair in zip(batch, made):
@@ -541,8 +531,9 @@
             new = both[:, (j - batch[0]) * lanes :][:, :lanes]
             for ref, at, size, row in parts:
                 one = new[at : at + 2 * size] + alpha * ref[:, here].astype(jnp.float32)
-                pair = join(one[:size], one[size:], left_lanes((size, lanes)), members)
-                made += [(2 * j + i, row, x.astype(jnp.bfloat16)) for i, x in enumerate(pair)]
+                one = one.astype(jnp.bfloat16)
+                pair = join(one[:size], one[size:], members)
+                made += [(2 * j + i, row, x) for i, x in enumerate(pair)]
         for group, row, value in made:
             out[group, row : row + value.shape[0], :] = value
 
@@ -582,9 +573,9 @@
             else:
                 at = levels * near + level * 2 * STEPS + (r if r < STEPS else r - near)
             both = blocks[:, at * SPAN : (at + 2) * SPAN, :].astype(jnp.float32)
-            for i in range(2):
-                one = both[:, i * SPAN : (i + 1) * SPAN, :].reshape(columns, lanes)
-                made.append((r + i, dot_rows(identity, one.astype(jnp.bfloat16))))
+            pair = [both[:, i * SPAN : (i + 1) * SPAN, :].reshape(columns, lanes) for i in range(2)]
+            rows = dot_rows(identity, jnp.concatenate(pair, axis=0).astype(jnp.bfloat16))
+            made += [(r + i, rows[:, i * columns : (i + 1) * columns]) for i in range(2)]
         for r, rows in made:
             turned[level, pl.ds(r, lanes, stride=span), :] = rows
 

time: 91.6 us -> 91.1 us (level)
  no operation moved by 1% of the time
where the time goes in v10:
time: 91.1 us; the launch traced here: 90.7 us
  blocking collectives  30.6 us (34%)
  waiting for transfers between devices  29.1 us (32%)
  Pallas kernels  17.7 us (19%)
  starting transfers between devices  12.6 us (14%)
    all_to_all x1, blocking collectives, exchange(): lax.all_to_all(blocks, 'grp', split_axis=0, concat_axis=0, tiled=True)  30.6 us
    all_to_all x2, waiting for transfers between devices, exchange(): lax.all_to_all(blocks, 'grp', split_axis=0, concat_axis=0, tiled=True)  29.1 us
    all_to_all x2, starting transfers between devices, exchange(): lax.all_to_all(blocks, 'grp', split_axis=0, concat_axis=0, tiled=True)  12.1 us
    pallas_call x1, Pallas kernels, outer(): pl.pallas_call(functools.partial(outer_kernel, near), out_shape=[jax.Shap...  5.21 us
    pallas_call x1, Pallas kernels, inner(): pl.pallas_call(inner_kernel, out_shape=[jax.ShapeDtypeStruct((variables,...  4.18 us
    pallas_call x1, Pallas kernels, pick(): pl.pallas_call(functools.partial(pick_kernel, variables, together), out_s...  3.74 us
    pallas_call x1, Pallas kernels, analyse(): pl.pallas_call(analyse_kernel, out_shape=jax.ShapeDtypeStruct((groups, ne...  2.39 us
  transfers between devices with their start and end apart: 3, of which 2 were waited for; matrix products, arithmetic and copies ran while one was open for 0% of the time, Pallas kernels for 10%

profile of v10, /device:TPU:0, one launch (start us, length us, event | category | flops | bytes accessed | tf_op | source)
XLA Modules:
  0.0 90.7 jit_solution(15307368616297311637)
XLA Ops:
  0.0 4.2 %shard_map.82 = (f32[2,4,8,64,128]{4,3,2,1,0:T(8,128)S(1)}, bf16[4,4,128,128]{3,2,1,0:T(8,128)(2,1)S(1)}, bf16[16,128,128]{2,1,0:T(8,128)(2,1)}, f32[4,5,8,128]{3,2,1,0:T(8,128)S(1)}) custom-call(f32[64,2,4,8,128]{4,3,2,1,0:T(8,128)} %own.1, f32[4,128]{1,0:T(4,128)} %refs_0_.1, f32[4]{0:T(128)} %refs_1_.1, f32[4]{0:T(128)} %refs_2_.1), custom_call_target="tpu_custom_call" | custom-call | flops 2000000000 | bytes 4194304 | tf_op jit(solution)/shard_map/pallas_call | solution.py:200
  4.2 0.5 collective-permute-start
  4.7 7.9 %all-to-all-start = ((bf16[16,128,128]{2,1,0:T(8,128)(2,1)}), bf16[16,128,128]{2,1,0:T(8,128)(2,1)S(1)}, u32[]{:S(2)}, u32[]{:S(2)}) async-start(bf16[16,128,128]{2,1,0:T(8,128)(2,1)} %get-tuple-element.13), calls=%async_computation | async-start | bytes 1048576 | tf_op jit(solution)/shard_map/all_to_all | solution.py:625
  12.6 0.0 collective-permute-done.rest_0_
  12.6 0.0 copy-start
  12.6 5.2 %shard_map.84 = (bf16[4,8,256,128]{3,2,1,0:T(8,128)(2,1)S(1)}, bf16[16,256,128]{2,1,0:T(8,128)(2,1)}) custom-call(f32[2,4,8,64,128]{4,3,2,1,0:T(8,128)S(1)} %get-tuple-element.16.own, f32[2,4,8,64,128]{4,3,2,1,0:T(8,128)} %collective-permute-done.rest_0_, f32[4,5,8,128]{3,2,1,0:T(8,128)S(1)} %get-tuple-element.17.rest_1_, ...), custom_call_target="tpu_custom_call" | custom-call | flops 2000000000 | bytes 8388608 | tf_op jit(solution)/shard_map/pallas_call | solution.py:292
  17.8 0.0 copy-done
  17.8 3.7 %shard_map.85 = bf16[16,256,128]{2,1,0:T(8,128)(2,1)} custom-call(bf16[4,8,256,128]{3,2,1,0:T(8,128)(2,1)S(1)} %get-tuple-element.19.grid, bf16[16,256,128]{2,1,0:T(8,128)(2,1)} %get-tuple-element.20._, s32[16,256]{1,0:T(8,128)S(1)} %bitcast.3), custom_call_target="tpu_custom_call", output_to_operand_aliasing={{}: (1, {})} | custom-call | flops 4000000000 | bytes 4194304 | tf_op jit(solution)/shard_map/pallas_call | solution.py:386
  21.6 0.0 copy-start.1
  21.6 0.0 copy-start.2
  21.6 6.4 %all-to-all-done.states = bf16[16,128,128]{2,1,0:T(8,128)(2,1)S(1)} async-done(((bf16[16,128,128]{2,1,0:T(8,128)(2,1)}), bf16[16,128,128]{2,1,0:T(8,128)(2,1)S(1)}, u32[]{:S(2)}, u32[]{:S(2)}) %all-to-all-start) | async-done | bytes 524320 | tf_op jit(solution)/shard_map/all_to_all | solution.py:625
  28.1 4.2 %all-to-all-start.1 = ((bf16[16,256,128]{2,1,0:T(8,128)(2,1)}), bf16[16,256,128]{2,1,0:T(8,128)(2,1)S(1)}, u32[]{:S(2)}, u32[]{:S(2)}) async-start(bf16[16,256,128]{2,1,0:T(8,128)(2,1)} %shard_map.85), calls=%async_computation.1 | async-start | bytes 2097152 | tf_op jit(solution)/shard_map/all_to_all | solution.py:625
  32.9 0.4 shard_map.83
  33.4 22.6 %all-to-all-done.1.second = bf16[16,256,128]{2,1,0:T(8,128)(2,1)S(1)} async-done(((bf16[16,256,128]{2,1,0:T(8,128)(2,1)}), bf16[16,256,128]{2,1,0:T(8,128)(2,1)S(1)}, u32[]{:S(2)}, u32[]{:S(2)}) %all-to-all-start.1) | async-done | bytes 1048608 | tf_op jit(solution)/shard_map/all_to_all | solution.py:625
  56.0 0.0 copy-done.1
  56.0 0.0 copy-done.2
  56.0 2.4 %shard_map.86 = bf16[16,256,128]{2,1,0:T(8,128)(2,1)S(1)} custom-call(bf16[256,1024]{1,0:T(8,128)(2,1)S(1)} %get-tuple-element.14.first, f32[256,128]{1,0:T(8,128)S(1)} %get-tuple-element.15.means, bf16[16,256,128]{2,1,0:T(8,128)(2,1)S(1)} %all-to-all-done.1.second, s32[1,1]{1,0:T(1,128)S(6)} %copy.11.count, f32[1,256]{1,0:T(1,128)S(1)} %bitcast.4, ...), custom_call_target="tpu_custom_call" | custom-call | flops 4000000000 | bytes 4194304 | tf_op jit(solution)/shard_map/pallas_call | solution.py:547
  58.4 30.6 %all_to_all.15.blocks = bf16[16,256,128]{2,1,0:T(8,128)(2,1)S(1)} all-to-all(bf16[16,256,128]{2,1,0:T(8,128)(2,1)S(1)} %shard_map.86), channel_id=1, replica_groups=mesh['grp'=16,'tile'=2] {'grp'}, dimensions={0} | all-to-all | bytes 2097152 | tf_op jit(solution)/shard_map/all_to_all | solution.py:625
  89.0 1.7 %shard_map.87 = bf16[64,2,4,8,128]{4,3,2,1,0:T(8,128)(2,1)} custom-call(bf16[16,256,128]{2,1,0:T(8,128)(2,1)S(1)} %all_to_all.15.blocks), custom_call_target="tpu_custom_call" | custom-call | flops 2000000000 | bytes 2097152 | tf_op jit(solution)/shard_map/pallas_call | solution.py:601
Async XLA Ops:
  4.2 8.4 %collective-permute-start = (f32[2,4,8,64,128]{4,3,2,1,0:T(8,128)S(1)}, f32[2,4,8,64,128]{4,3,2,1,0:T(8,128)}, u32[]{:S(2)}, u32[]{:S(2)}) collective-permute-start(f32[2,4,8,64,128]{4,3,2,1,0:T(8,128)S(1)} %get-tuple-element.16.own), channel_id=1, source_target_pairs={{0,1},{1,0},{2,3},{3,2},{4,5},{5,4},{6,7},{7,6},{8,9},{9,8},{10,11... | collective-permute-start | bytes 6291464 | tf_op jit(solution)/shard_map/ppermute | solution.py:618
  4.7 23.4 %all-to-all-start = ((bf16[16,128,128]{2,1,0:T(8,128)(2,1)}), bf16[16,128,128]{2,1,0:T(8,128)(2,1)S(1)}, u32[]{:S(2)}, u32[]{:S(2)}) async-start(bf16[16,128,128]{2,1,0:T(8,128)(2,1)} %get-tuple-element.13), calls=%async_computation | async-start | bytes 1048576 | tf_op jit(solution)/shard_map/all_to_all | solution.py:625
  12.6 5.2 %copy-start = (s32[1,16,256]{2,1,0:T(8,128)S(1)}, s32[1,16,256]{2,1,0:T(8,128)}, u32[]{:S(2)}) copy-start(s32[1,16,256]{2,1,0:T(8,128)} %param.12) | copy-start | bytes 49156
  21.6 34.4 %copy-start.1 = (f32[1,1,256]{2,1,0:T(1,128)S(1)}, f32[1,1,256]{2,1,0:T(1,128)}, u32[]{:S(2)}) copy-start(f32[1,1,256]{2,1,0:T(1,128)} %param.14) | copy-start | bytes 3076
  21.6 34.4 %copy-start.2 = (f32[1,1,256]{2,1,0:T(1,128)S(1)}, f32[1,1,256]{2,1,0:T(1,128)}, u32[]{:S(2)}) copy-start(f32[1,1,256]{2,1,0:T(1,128)} %param.15) | copy-start | bytes 3076
  28.1 28.0 %all-to-all-start.1 = ((bf16[16,256,128]{2,1,0:T(8,128)(2,1)}), bf16[16,256,128]{2,1,0:T(8,128)(2,1)S(1)}, u32[]{:S(2)}, u32[]{:S(2)}) async-start(bf16[16,256,128]{2,1,0:T(8,128)(2,1)} %shard_map.85), calls=%async_computation.1 | async-start | bytes 2097152 | tf_op jit(solution)/shard_map/all_to_all | solution.py:625

commit v11 on v10

--- a/solution.py
+++ b/solution.py
@@ -152,11 +152,46 @@
     for copy in copies:
         copy.wait()
 
-    @pl.loop(0, levels)
+    def pack(level):
+        pairs = [
+            fields[level, r : r + 2].reshape(2 * variables * members, columns)
+            for r in range(0, count, 2)
+        ]
+        pack_rows(pairs, identity, staged.at[level], 0)
+
+    def advance(level):
+        coefficients = coefficients_of(level, *local)
+        reads, made = [], []
+        for var in range(variables):
+            view = whole.at[level, var].reshape(members * span, columns)
+
+            def read(r):
+                rows = view[pl.ds(r, members, stride=span), :]
+                reads.append((var, r, rows))
+                return rows.reshape(-1, 8, columns)
+
+            for r, value in forecast_rows(read, STEPS, span - STEPS, coefficients, shifts):
+                made.append((var, r, value))
+
+        def store():
+            for i, one in enumerate(coefficients):
+                model[level, i] = one
+            for var, r, value in made:
+                fields[level, r - STEPS, var * members : (var + 1) * members, :] = value
+            for var, r, rows in reads:
+                slabs[var, level, r] = rows
+
+        return store
+
+    for copy in arrive(0):
+        copy.wait()
+    if levels > 2:
+        for copy in arrive(2):
+            copy.start()
+    advance(0)()
+
+    @pl.loop(1, levels)
     def _(level):
-        coefficients = coefficients_of(level, *local)
-        for i, one in enumerate(coefficients):
-            model[level, i] = one
         for copy in arrive(level):
             copy.wait()
 
@@ -165,28 +200,13 @@
             for copy in arrive(level + 2):
                 copy.start()
 
-        reads, made = [], []
-        for var in range(variables):
-            view = whole.at[level, var].reshape(members * span, columns)
-
-            def read(r):
-                rows = view[pl.ds(r, members, stride=span), :]
-                reads.append((var, r, rows))
-                return rows.reshape(-1, 8, columns)
-
-            for r, value in forecast_rows(read, STEPS, span - STEPS, coefficients, shifts):
-                made.append((var, r, value))
-        pairs = []
-        for first in range(STEPS, span - STEPS, 2):
-            rows = [one for r in (first, first + 1) for _, at, one in made if at == r]
-            pairs.append(jnp.concatenate(rows, axis=0))
-        pack_rows(pairs, identity, staged.at[level], 0)
-        leave(level).start()
-        for var, r, value in made:
-            fields[level, r - STEPS, var * members : (var + 1) * members, :] = value
-        for var, r, rows in reads:
-            slabs[var, level, r] = rows
-
+        store = advance(level)
+        pack(level - 1)
+        store()
+        leave(level - 1).start()
+
+    pack(levels - 1)
+    leave(levels - 1).start()
     for level in range(levels):
         leave(level).wait()
 

time: 91.1 us -> 90.9 us (level)
  no operation moved by 1% of the time
where the time goes in v11:
time: 90.9 us; the launch traced here: 90.5 us
  blocking collectives  30.6 us (34%)
  waiting for transfers between devices  29.1 us (32%)
  Pallas kernels  17.5 us (19%)
  starting transfers between devices  12.6 us (14%)
    all_to_all x1, blocking collectives, exchange(): lax.all_to_all(blocks, 'grp', split_axis=0, concat_axis=0, tiled=True)  30.6 us
    all_to_all x2, waiting for transfers between devices, exchange(): lax.all_to_all(blocks, 'grp', split_axis=0, concat_axis=0, tiled=True)  29.1 us
    all_to_all x2, starting transfers between devices, exchange(): lax.all_to_all(blocks, 'grp', split_axis=0, concat_axis=0, tiled=True)  12.1 us
    pallas_call x1, Pallas kernels, outer(): pl.pallas_call(functools.partial(outer_kernel, near), out_shape=[jax.Shap...  5.21 us
    pallas_call x1, Pallas kernels, inner(): pl.pallas_call(inner_kernel, out_shape=[jax.ShapeDtypeStruct((variables,...  4.01 us
    pallas_call x1, Pallas kernels, pick(): pl.pallas_call(functools.partial(pick_kernel, variables, together), out_s...  3.74 us
    pallas_call x1, Pallas kernels, analyse(): pl.pallas_call(analyse_kernel, out_shape=jax.ShapeDtypeStruct((groups, ne...  2.39 us
  transfers between devices with their start and end apart: 3, of which 2 were waited for; matrix products, arithmetic and copies ran while one was open for 0% of the time, Pallas kernels for 10%

profile of v11, /device:TPU:0, one launch (start us, length us, event | category | flops | bytes accessed | tf_op | source)
XLA Modules:
  0.0 90.5 jit_solution(431281487377105505)
XLA Ops:
  0.0 4.0 %shard_map.82 = (f32[2,4,8,64,128]{4,3,2,1,0:T(8,128)S(1)}, bf16[4,4,128,128]{3,2,1,0:T(8,128)(2,1)S(1)}, bf16[16,128,128]{2,1,0:T(8,128)(2,1)}, f32[4,5,8,128]{3,2,1,0:T(8,128)S(1)}) custom-call(f32[64,2,4,8,128]{4,3,2,1,0:T(8,128)} %own.1, f32[4,128]{1,0:T(4,128)} %refs_0_.1, f32[4]{0:T(128)} %refs_1_.1, f32[4]{0:T(128)} %refs_2_.1), custom_call_target="tpu_custom_call" | custom-call | flops 2000000000 | bytes 4194304 | tf_op jit(solution)/shard_map/pallas_call | solution.py:220
  4.0 0.5 collective-permute-start
  4.5 7.9 %all-to-all-start = ((bf16[16,128,128]{2,1,0:T(8,128)(2,1)}), bf16[16,128,128]{2,1,0:T(8,128)(2,1)S(1)}, u32[]{:S(2)}, u32[]{:S(2)}) async-start(bf16[16,128,128]{2,1,0:T(8,128)(2,1)} %get-tuple-element.13), calls=%async_computation | async-start | bytes 1048576 | tf_op jit(solution)/shard_map/all_to_all | solution.py:645
  12.4 0.0 collective-permute-done.rest_0_
  12.4 0.0 copy-start
  12.5 5.2 %shard_map.84 = (bf16[4,8,256,128]{3,2,1,0:T(8,128)(2,1)S(1)}, bf16[16,256,128]{2,1,0:T(8,128)(2,1)}) custom-call(f32[2,4,8,64,128]{4,3,2,1,0:T(8,128)S(1)} %get-tuple-element.16.own, f32[2,4,8,64,128]{4,3,2,1,0:T(8,128)} %collective-permute-done.rest_0_, f32[4,5,8,128]{3,2,1,0:T(8,128)S(1)} %get-tuple-element.17.rest_1_, ...), custom_call_target="tpu_custom_call" | custom-call | flops 2000000000 | bytes 8388608 | tf_op jit(solution)/shard_map/pallas_call | solution.py:312
  17.7 0.0 copy-done
  17.7 3.7 %shard_map.85 = bf16[16,256,128]{2,1,0:T(8,128)(2,1)} custom-call(bf16[4,8,256,128]{3,2,1,0:T(8,128)(2,1)S(1)} %get-tuple-element.19.grid, bf16[16,256,128]{2,1,0:T(8,128)(2,1)} %get-tuple-element.20._, s32[16,256]{1,0:T(8,128)S(1)} %bitcast.3), custom_call_target="tpu_custom_call", output_to_operand_aliasing={{}: (1, {})} | custom-call | flops 4000000000 | bytes 4194304 | tf_op jit(solution)/shard_map/pallas_call | solution.py:406
  21.4 0.0 copy-start.1
  21.4 0.0 copy-start.2
  21.5 6.4 %all-to-all-done.states = bf16[16,128,128]{2,1,0:T(8,128)(2,1)S(1)} async-done(((bf16[16,128,128]{2,1,0:T(8,128)(2,1)}), bf16[16,128,128]{2,1,0:T(8,128)(2,1)S(1)}, u32[]{:S(2)}, u32[]{:S(2)}) %all-to-all-start) | async-done | bytes 524320 | tf_op jit(solution)/shard_map/all_to_all | solution.py:645
  27.9 4.2 %all-to-all-start.1 = ((bf16[16,256,128]{2,1,0:T(8,128)(2,1)}), bf16[16,256,128]{2,1,0:T(8,128)(2,1)S(1)}, u32[]{:S(2)}, u32[]{:S(2)}) async-start(bf16[16,256,128]{2,1,0:T(8,128)(2,1)} %shard_map.85), calls=%async_computation.1 | async-start | bytes 2097152 | tf_op jit(solution)/shard_map/all_to_all | solution.py:645
  32.8 0.4 shard_map.83
  33.2 22.6 %all-to-all-done.1.second = bf16[16,256,128]{2,1,0:T(8,128)(2,1)S(1)} async-done(((bf16[16,256,128]{2,1,0:T(8,128)(2,1)}), bf16[16,256,128]{2,1,0:T(8,128)(2,1)S(1)}, u32[]{:S(2)}, u32[]{:S(2)}) %all-to-all-start.1) | async-done | bytes 1048608 | tf_op jit(solution)/shard_map/all_to_all | solution.py:645
  55.8 0.0 copy-done.1
  55.9 0.0 copy-done.2
  55.9 2.4 %shard_map.86 = bf16[16,256,128]{2,1,0:T(8,128)(2,1)S(1)} custom-call(bf16[256,1024]{1,0:T(8,128)(2,1)S(1)} %get-tuple-element.14.first, f32[256,128]{1,0:T(8,128)S(1)} %get-tuple-element.15.means, bf16[16,256,128]{2,1,0:T(8,128)(2,1)S(1)} %all-to-all-done.1.second, s32[1,1]{1,0:T(1,128)S(6)} %copy.11.count, f32[1,256]{1,0:T(1,128)S(1)} %bitcast.4, ...), custom_call_target="tpu_custom_call" | custom-call | flops 4000000000 | bytes 4194304 | tf_op jit(solution)/shard_map/pallas_call | solution.py:567
  58.2 30.6 %all_to_all.15.blocks = bf16[16,256,128]{2,1,0:T(8,128)(2,1)S(1)} all-to-all(bf16[16,256,128]{2,1,0:T(8,128)(2,1)S(1)} %shard_map.86), channel_id=1, replica_groups=mesh['grp'=16,'tile'=2] {'grp'}, dimensions={0} | all-to-all | bytes 2097152 | tf_op jit(solution)/shard_map/all_to_all | solution.py:645
  88.8 1.7 %shard_map.87 = bf16[64,2,4,8,128]{4,3,2,1,0:T(8,128)(2,1)} custom-call(bf16[16,256,128]{2,1,0:T(8,128)(2,1)S(1)} %all_to_all.15.blocks), custom_call_target="tpu_custom_call" | custom-call | flops 2000000000 | bytes 2097152 | tf_op jit(solution)/shard_map/pallas_call | solution.py:621
Async XLA Ops:
  4.0 8.4 %collective-permute-start = (f32[2,4,8,64,128]{4,3,2,1,0:T(8,128)S(1)}, f32[2,4,8,64,128]{4,3,2,1,0:T(8,128)}, u32[]{:S(2)}, u32[]{:S(2)}) collective-permute-start(f32[2,4,8,64,128]{4,3,2,1,0:T(8,128)S(1)} %get-tuple-element.16.own), channel_id=1, source_target_pairs={{0,1},{1,0},{2,3},{3,2},{4,5},{5,4},{6,7},{7,6},{8,9},{9,8},{10,11... | collective-permute-start | bytes 6291464 | tf_op jit(solution)/shard_map/ppermute | solution.py:638
  4.5 23.4 %all-to-all-start = ((bf16[16,128,128]{2,1,0:T(8,128)(2,1)}), bf16[16,128,128]{2,1,0:T(8,128)(2,1)S(1)}, u32[]{:S(2)}, u32[]{:S(2)}) async-start(bf16[16,128,128]{2,1,0:T(8,128)(2,1)} %get-tuple-element.13), calls=%async_computation | async-start | bytes 1048576 | tf_op jit(solution)/shard_map/all_to_all | solution.py:645
  12.4 5.2 %copy-start = (s32[1,16,256]{2,1,0:T(8,128)S(1)}, s32[1,16,256]{2,1,0:T(8,128)}, u32[]{:S(2)}) copy-start(s32[1,16,256]{2,1,0:T(8,128)} %param.12) | copy-start | bytes 49156
  21.4 34.4 %copy-start.1 = (f32[1,1,256]{2,1,0:T(1,128)S(1)}, f32[1,1,256]{2,1,0:T(1,128)}, u32[]{:S(2)}) copy-start(f32[1,1,256]{2,1,0:T(1,128)} %param.14) | copy-start | bytes 3076
  21.4 34.4 %copy-start.2 = (f32[1,1,256]{2,1,0:T(1,128)S(1)}, f32[1,1,256]{2,1,0:T(1,128)}, u32[]{:S(2)}) copy-start(f32[1,1,256]{2,1,0:T(1,128)} %param.15) | copy-start | bytes 3076
  27.9 28.0 %all-to-all-start.1 = ((bf16[16,256,128]{2,1,0:T(8,128)(2,1)}), bf16[16,256,128]{2,1,0:T(8,128)(2,1)S(1)}, u32[]{:S(2)}, u32[]{:S(2)}) async-start(bf16[16,256,128]{2,1,0:T(8,128)(2,1)} %shard_map.85), calls=%async_computation.1 | async-start | bytes 2097152 | tf_op jit(solution)/shard_map/all_to_all | solution.py:645

commit v12 on v11

--- a/solution.py
+++ b/solution.py
@@ -454,29 +454,36 @@
     return centre
 
 
-def prepare_kernel(states, dev, centre, raw):
+def prepare_kernel(states, count, value, weight, dev, centre, roots, values, raw):
     mean = deviations(states, raw, dev, 0, states.shape[1])
     centre[...] = jnp.broadcast_to(mean, centre.shape)
-
-
-def prepare(states):
+    used = lax.broadcasted_iota(jnp.int32, weight.shape, 1) < count[0, 0]
+    root = column_of(jnp.where(used, jnp.sqrt(weight[...]), 0.0))
+    roots[...] = jnp.broadcast_to(root, roots.shape)
+    values[...] = jnp.broadcast_to(column_of(value[...]), values.shape)
+
+
+def prepare(states, count, value, weight):
     groups, near, lanes = states.shape
     total = groups * lanes // 2
+    column = jax.ShapeDtypeStruct((value.shape[1], lanes), jnp.float32)
     return pl.pallas_call(
         prepare_kernel,
         out_shape=[
             jax.ShapeDtypeStruct((2 * near, total), jnp.bfloat16),
             jax.ShapeDtypeStruct((2 * near, lanes), jnp.float32),
-        ],
-        in_specs=vmem(1),
-        out_specs=vmem(2),
+            column,
+            column,
+        ],
+        in_specs=vmem(1) + smem(1) + vmem(2),
+        out_specs=vmem(4),
         scratch_shapes=[pltpu.VMEM((2 * near, total), jnp.float32)],
         compiler_params=params(6),
         cost_estimate=cost(10**8, 2 * 2**20),
-    )(states)
-
-
-def analyse_kernel(first, means, second, count, value, weight, out, raw, dev, obs, scaled_ref):
+    )(states, count, value, weight)
+
+
+def analyse_kernel(first, means, roots, values, second, out, raw, dev, obs, scaled_ref):
     groups, _, lanes = second.shape
     near = first.shape[0] // 2
     half = obs.shape[0] // 2
@@ -498,14 +505,13 @@
             here = slice(j * lanes, (j + 1) * lanes)
             obs[:half, here], obs[half:, here] = pair
 
-    used = lax.broadcasted_iota(jnp.int32, (1, slots), 1) < count[0, 0]
-    root = column_of(jnp.where(used, jnp.sqrt(weight[...]), 0.0))
+    root = roots[:, 0:1]
     observed = obs[...]
     mean = jnp.sum(observed, axis=1, keepdims=True) * (1.0 / total_members)
     scaled = (observed - mean) * root
     energy = jnp.sum(jnp.sum(scaled * scaled, axis=1, keepdims=True), axis=0, keepdims=True)
     scaled_ref[...] = scaled.astype(jnp.bfloat16)
-    misfit = row_of(root * (column_of(value[...]) - mean))
+    misfit = row_of(root * (values[:, 0:1] - mean))
 
     c = total_members - 1.0
     s = energy * (1.0 / total_members) + c
@@ -558,16 +564,16 @@
             out[group, row : row + value.shape[0], :] = value
 
 
-def analyse(first, means, second, count, value, weight):
+def analyse(first, means, roots, values, second):
     groups, _, lanes = second.shape
     near = first.shape[0] // 2
-    slots = value.shape[1]
+    slots = values.shape[0]
     far = second.shape[1] - slots // 2
     total = groups * lanes // 2
     return pl.pallas_call(
         analyse_kernel,
         out_shape=jax.ShapeDtypeStruct((groups, near + far, lanes), jnp.bfloat16),
-        in_specs=vmem(3) + smem(1) + vmem(2),
+        in_specs=vmem(5),
         out_specs=pl.BlockSpec(memory_space=pltpu.VMEM),
         scratch_shapes=[
             pltpu.VMEM((2 * far, total), jnp.float32),
@@ -577,7 +583,7 @@
         ],
         compiler_params=params(16),
         cost_estimate=cost(4 * 10**9, 4 * 2**20),
-    )(first, means, second, count, value, weight)
+    )(first, means, roots, values, second)
 
 
 def restore_kernel(blocks, out, turned, staged, sems):
@@ -649,10 +655,10 @@
     members, variables, levels, span, columns = dims = start.shape
     own, centre, near, model = inner(start, (diffusivity, eastward, northward))
     sides = neighbours(own, "tile")
-    first, means = prepare(exchange(near))
+    prepared = prepare(exchange(near), count, value[0], weight[0])
     grid, packed = outer(dims, own, sides, model, centre, cells.shape[2])
     second = exchange(pick(variables, grid, packed, cells[0]))
-    updated = analyse(first, means, second, count, value[0], weight[0])
+    updated = analyse(*prepared, second)
     return restore(dims, exchange(updated))
 
 

time: 90.9 us -> 90.9 us (level)
  no operation moved by 1% of the time
where the time goes in v12:
time: 90.9 us; the launch traced here: 90.5 us
  blocking collectives  30.6 us (34%)
  waiting for transfers between devices  29 us (32%)
  Pallas kernels  17.6 us (19%)
  starting transfers between devices  12.6 us (14%)
    all_to_all x1, blocking collectives, exchange(): lax.all_to_all(blocks, 'grp', split_axis=0, concat_axis=0, tiled=True)  30.6 us
    all_to_all x2, waiting for transfers between devices, exchange(): lax.all_to_all(blocks, 'grp', split_axis=0, concat_axis=0, tiled=True)  29 us
    all_to_all x2, starting transfers between devices, exchange(): lax.all_to_all(blocks, 'grp', split_axis=0, concat_axis=0, tiled=True)  12.1 us
    pallas_call x1, Pallas kernels, outer(): pl.pallas_call(functools.partial(outer_kernel, near), out_shape=[jax.Shap...  5.21 us
    pallas_call x1, Pallas kernels, inner(): pl.pallas_call(inner_kernel, out_shape=[jax.ShapeDtypeStruct((variables,...  4.01 us
    pallas_call x1, Pallas kernels, pick(): pl.pallas_call(functools.partial(pick_kernel, variables, together), out_s...  3.74 us
    pallas_call x1, Pallas kernels, analyse(): pl.pallas_call(analyse_kernel, out_shape=jax.ShapeDtypeStruct((groups, ne...  2.36 us
  transfers between devices with their start and end apart: 3, of which 2 were waited for; matrix products, arithmetic and copies ran while one was open for 0% of the time, Pallas kernels for 10%

profile of v12, /device:TPU:0, one launch (start us, length us, event | category | flops | bytes accessed | tf_op | source)
XLA Modules:
  0.0 90.5 jit_solution(16888209782002119111)
XLA Ops:
  0.0 4.0 %shard_map.82 = (f32[2,4,8,64,128]{4,3,2,1,0:T(8,128)S(1)}, bf16[4,4,128,128]{3,2,1,0:T(8,128)(2,1)S(1)}, bf16[16,128,128]{2,1,0:T(8,128)(2,1)}, f32[4,5,8,128]{3,2,1,0:T(8,128)S(1)}) custom-call(f32[64,2,4,8,128]{4,3,2,1,0:T(8,128)} %own.1, f32[4,128]{1,0:T(4,128)} %refs_0_.1, f32[4]{0:T(128)} %refs_1_.1, f32[4]{0:T(128)} %refs_2_.1), custom_call_target="tpu_custom_call" | custom-call | flops 2000000000 | bytes 4194304 | tf_op jit(solution)/shard_map/pallas_call | solution.py:220
  4.0 0.5 collective-permute-start
  4.5 7.9 %all-to-all-start = ((bf16[16,128,128]{2,1,0:T(8,128)(2,1)}), bf16[16,128,128]{2,1,0:T(8,128)(2,1)S(1)}, u32[]{:S(2)}, u32[]{:S(2)}) async-start(bf16[16,128,128]{2,1,0:T(8,128)(2,1)} %get-tuple-element.15), calls=%async_computation | async-start | bytes 1048576 | tf_op jit(solution)/shard_map/all_to_all | solution.py:651
  12.4 0.0 collective-permute-done.rest_0_
  12.4 0.0 copy-start.2
  12.5 5.2 %shard_map.84 = (bf16[4,8,256,128]{3,2,1,0:T(8,128)(2,1)S(1)}, bf16[16,256,128]{2,1,0:T(8,128)(2,1)}) custom-call(f32[2,4,8,64,128]{4,3,2,1,0:T(8,128)S(1)} %get-tuple-element.20.own, f32[2,4,8,64,128]{4,3,2,1,0:T(8,128)} %collective-permute-done.rest_0_, f32[4,5,8,128]{3,2,1,0:T(8,128)S(1)} %get-tuple-element.21.rest_1_, ...), custom_call_target="tpu_custom_call" | custom-call | flops 2000000000 | bytes 8388608 | tf_op jit(solution)/shard_map/pallas_call | solution.py:312
  17.7 0.0 copy-done.2
  17.7 3.7 %shard_map.85 = bf16[16,256,128]{2,1,0:T(8,128)(2,1)} custom-call(bf16[4,8,256,128]{3,2,1,0:T(8,128)(2,1)S(1)} %get-tuple-element.23.grid, bf16[16,256,128]{2,1,0:T(8,128)(2,1)} %get-tuple-element.24._, s32[16,256]{1,0:T(8,128)S(1)} %bitcast.5), custom_call_target="tpu_custom_call", output_to_operand_aliasing={{}: (1, {})} | custom-call | flops 4000000000 | bytes 4194304 | tf_op jit(solution)/shard_map/pallas_call | solution.py:406
  21.4 0.0 copy-start
  21.4 0.0 copy-start.1
  21.5 6.4 %all-to-all-done.states = bf16[16,128,128]{2,1,0:T(8,128)(2,1)S(1)} async-done(((bf16[16,128,128]{2,1,0:T(8,128)(2,1)}), bf16[16,128,128]{2,1,0:T(8,128)(2,1)S(1)}, u32[]{:S(2)}, u32[]{:S(2)}) %all-to-all-start) | async-done | bytes 524320 | tf_op jit(solution)/shard_map/all_to_all | solution.py:651
  27.9 4.2 %all-to-all-start.1 = ((bf16[16,256,128]{2,1,0:T(8,128)(2,1)}), bf16[16,256,128]{2,1,0:T(8,128)(2,1)S(1)}, u32[]{:S(2)}, u32[]{:S(2)}) async-start(bf16[16,256,128]{2,1,0:T(8,128)(2,1)} %shard_map.85), calls=%async_computation.1 | async-start | bytes 2097152 | tf_op jit(solution)/shard_map/all_to_all | solution.py:651
  32.8 0.0 copy-done
  32.8 0.0 copy-done.1
  32.8 0.5 shard_map.83
  33.3 22.5 %all-to-all-done.1.second = bf16[16,256,128]{2,1,0:T(8,128)(2,1)S(1)} async-done(((bf16[16,256,128]{2,1,0:T(8,128)(2,1)}), bf16[16,256,128]{2,1,0:T(8,128)(2,1)S(1)}, u32[]{:S(2)}, u32[]{:S(2)}) %all-to-all-start.1) | async-done | bytes 1048608 | tf_op jit(solution)/shard_map/all_to_all | solution.py:651
  55.8 2.4 %shard_map.86 = bf16[16,256,128]{2,1,0:T(8,128)(2,1)S(1)} custom-call(bf16[256,1024]{1,0:T(8,128)(2,1)S(1)} %get-tuple-element.16.first, f32[256,128]{1,0:T(8,128)S(1)} %get-tuple-element.17.means, f32[256,128]{1,0:T(8,128)S(1)} %get-tuple-element.18.roots, f32[256,128]{1,0:T(8,128)S(1)} %get-tuple-element.19.values, ...), custom_call_target="tpu_custom_call" | custom-call | flops 4000000000 | bytes 4194304 | tf_op jit(solution)/shard_map/pallas_call | solution.py:573
  58.2 30.6 %all_to_all.15.blocks = bf16[16,256,128]{2,1,0:T(8,128)(2,1)S(1)} all-to-all(bf16[16,256,128]{2,1,0:T(8,128)(2,1)S(1)} %shard_map.86), channel_id=1, replica_groups=mesh['grp'=16,'tile'=2] {'grp'}, dimensions={0} | all-to-all | bytes 2097152 | tf_op jit(solution)/shard_map/all_to_all | solution.py:651
  88.8 1.7 %shard_map.87 = bf16[64,2,4,8,128]{4,3,2,1,0:T(8,128)(2,1)} custom-call(bf16[16,256,128]{2,1,0:T(8,128)(2,1)S(1)} %all_to_all.15.blocks), custom_call_target="tpu_custom_call" | custom-call | flops 2000000000 | bytes 2097152 | tf_op jit(solution)/shard_map/pallas_call | solution.py:627
Async XLA Ops:
  4.0 8.4 %collective-permute-start = (f32[2,4,8,64,128]{4,3,2,1,0:T(8,128)S(1)}, f32[2,4,8,64,128]{4,3,2,1,0:T(8,128)}, u32[]{:S(2)}, u32[]{:S(2)}) collective-permute-start(f32[2,4,8,64,128]{4,3,2,1,0:T(8,128)S(1)} %get-tuple-element.20.own), channel_id=1, source_target_pairs={{0,1},{1,0},{2,3},{3,2},{4,5},{5,4},{6,7},{7,6},{8,9},{9,8},{10,11... | collective-permute-start | bytes 6291464 | tf_op jit(solution)/shard_map/ppermute | solution.py:644
  4.5 23.4 %all-to-all-start = ((bf16[16,128,128]{2,1,0:T(8,128)(2,1)}), bf16[16,128,128]{2,1,0:T(8,128)(2,1)S(1)}, u32[]{:S(2)}, u32[]{:S(2)}) async-start(bf16[16,128,128]{2,1,0:T(8,128)(2,1)} %get-tuple-element.15), calls=%async_computation | async-start | bytes 1048576 | tf_op jit(solution)/shard_map/all_to_all | solution.py:651
  12.4 5.2 %copy-start.2 = (s32[1,16,256]{2,1,0:T(8,128)S(1)}, s32[1,16,256]{2,1,0:T(8,128)}, u32[]{:S(2)}) copy-start(s32[1,16,256]{2,1,0:T(8,128)} %param.12) | copy-start | bytes 49156
  21.4 11.3 %copy-start = (f32[1,1,256]{2,1,0:T(1,128)S(1)}, f32[1,1,256]{2,1,0:T(1,128)}, u32[]{:S(2)}) copy-start(f32[1,1,256]{2,1,0:T(1,128)} %param.14) | copy-start | bytes 3076
  21.4 11.3 %copy-start.1 = (f32[1,1,256]{2,1,0:T(1,128)S(1)}, f32[1,1,256]{2,1,0:T(1,128)}, u32[]{:S(2)}) copy-start(f32[1,1,256]{2,1,0:T(1,128)} %param.15) | copy-start | bytes 3076
  27.9 28.0 %all-to-all-start.1 = ((bf16[16,256,128]{2,1,0:T(8,128)(2,1)}), bf16[16,256,128]{2,1,0:T(8,128)(2,1)S(1)}, u32[]{:S(2)}, u32[]{:S(2)}) async-start(bf16[16,256,128]{2,1,0:T(8,128)(2,1)} %shard_map.85), calls=%async_computation.1 | async-start | bytes 2097152 | tf_op jit(solution)/shard_map/all_to_all | solution.py:651

commit v13 on v12

--- a/solution.py
+++ b/solution.py
@@ -548,7 +548,7 @@
     mix = sum(dot(once, part) for part in split(poly))
     mix = (mix * factor).astype(jnp.bfloat16)
     parts = ((first, 0, near, 0), (dev, 2 * near, far, near))
-    for batch in batches(groups // 2, 2):
+    for batch in batches(groups // 2, 4):
         made = []
         wide = slice(batch[0] * lanes, (batch[-1] + 1) * lanes)
         both = dot(mix, scaled_ref[:, wide]) + shift

time: 90.9 us -> 90.9 us (level)
  no operation moved by 1% of the time
where the time goes in v13:
time: 90.9 us; the launch traced here: 90.5 us
  blocking collectives  30.6 us (34%)
  waiting for transfers between devices  29 us (32%)
  Pallas kernels  17.6 us (19%)
  starting transfers between devices  12.6 us (14%)
    all_to_all x1, blocking collectives, exchange(): lax.all_to_all(blocks, 'grp', split_axis=0, concat_axis=0, tiled=True)  30.6 us
    all_to_all x2, waiting for transfers between devices, exchange(): lax.all_to_all(blocks, 'grp', split_axis=0, concat_axis=0, tiled=True)  29 us
    all_to_all x2, starting transfers between devices, exchange(): lax.all_to_all(blocks, 'grp', split_axis=0, concat_axis=0, tiled=True)  12.1 us
    pallas_call x1, Pallas kernels, outer(): pl.pallas_call(functools.partial(outer_kernel, near), out_shape=[jax.Shap...  5.21 us
    pallas_call x1, Pallas kernels, inner(): pl.pallas_call(inner_kernel, out_shape=[jax.ShapeDtypeStruct((variables,...  4.01 us
    pallas_call x1, Pallas kernels, pick(): pl.pallas_call(functools.partial(pick_kernel, variables, together), out_s...  3.74 us
    pallas_call x1, Pallas kernels, analyse(): pl.pallas_call(analyse_kernel, out_shape=jax.ShapeDtypeStruct((groups, ne...  2.36 us
  transfers between devices with their start and end apart: 3, of which 2 were waited for; matrix products, arithmetic and copies ran while one was open for 0% of the time, Pallas kernels for 10%

profile of v13, /device:TPU:0, one launch (start us, length us, event | category | flops | bytes accessed | tf_op | source)
XLA Modules:
  0.0 90.5 jit_solution(16888209782002119111)
XLA Ops:
  0.0 4.0 %shard_map.82 = (f32[2,4,8,64,128]{4,3,2,1,0:T(8,128)S(1)}, bf16[4,4,128,128]{3,2,1,0:T(8,128)(2,1)S(1)}, bf16[16,128,128]{2,1,0:T(8,128)(2,1)}, f32[4,5,8,128]{3,2,1,0:T(8,128)S(1)}) custom-call(f32[64,2,4,8,128]{4,3,2,1,0:T(8,128)} %own.1, f32[4,128]{1,0:T(4,128)} %refs_0_.1, f32[4]{0:T(128)} %refs_1_.1, f32[4]{0:T(128)} %refs_2_.1), custom_call_target="tpu_custom_call" | custom-call | flops 2000000000 | bytes 4194304 | tf_op jit(solution)/shard_map/pallas_call | solution.py:220
  4.0 0.5 collective-permute-start
  4.5 7.9 %all-to-all-start = ((bf16[16,128,128]{2,1,0:T(8,128)(2,1)}), bf16[16,128,128]{2,1,0:T(8,128)(2,1)S(1)}, u32[]{:S(2)}, u32[]{:S(2)}) async-start(bf16[16,128,128]{2,1,0:T(8,128)(2,1)} %get-tuple-element.15), calls=%async_computation | async-start | bytes 1048576 | tf_op jit(solution)/shard_map/all_to_all | solution.py:651
  12.4 0.0 collective-permute-done.rest_0_
  12.4 0.0 copy-start.2
  12.5 5.2 %shard_map.84 = (bf16[4,8,256,128]{3,2,1,0:T(8,128)(2,1)S(1)}, bf16[16,256,128]{2,1,0:T(8,128)(2,1)}) custom-call(f32[2,4,8,64,128]{4,3,2,1,0:T(8,128)S(1)} %get-tuple-element.20.own, f32[2,4,8,64,128]{4,3,2,1,0:T(8,128)} %collective-permute-done.rest_0_, f32[4,5,8,128]{3,2,1,0:T(8,128)S(1)} %get-tuple-element.21.rest_1_, ...), custom_call_target="tpu_custom_call" | custom-call | flops 2000000000 | bytes 8388608 | tf_op jit(solution)/shard_map/pallas_call | solution.py:312
  17.7 0.0 copy-done.2
  17.7 3.7 %shard_map.85 = bf16[16,256,128]{2,1,0:T(8,128)(2,1)} custom-call(bf16[4,8,256,128]{3,2,1,0:T(8,128)(2,1)S(1)} %get-tuple-element.23.grid, bf16[16,256,128]{2,1,0:T(8,128)(2,1)} %get-tuple-element.24._, s32[16,256]{1,0:T(8,128)S(1)} %bitcast.5), custom_call_target="tpu_custom_call", output_to_operand_aliasing={{}: (1, {})} | custom-call | flops 4000000000 | bytes 4194304 | tf_op jit(solution)/shard_map/pallas_call | solution.py:406
  21.4 0.0 copy-start
  21.4 0.0 copy-start.1
  21.5 6.4 %all-to-all-done.states = bf16[16,128,128]{2,1,0:T(8,128)(2,1)S(1)} async-done(((bf16[16,128,128]{2,1,0:T(8,128)(2,1)}), bf16[16,128,128]{2,1,0:T(8,128)(2,1)S(1)}, u32[]{:S(2)}, u32[]{:S(2)}) %all-to-all-start) | async-done | bytes 524320 | tf_op jit(solution)/shard_map/all_to_all | solution.py:651
  27.9 4.2 %all-to-all-start.1 = ((bf16[16,256,128]{2,1,0:T(8,128)(2,1)}), bf16[16,256,128]{2,1,0:T(8,128)(2,1)S(1)}, u32[]{:S(2)}, u32[]{:S(2)}) async-start(bf16[16,256,128]{2,1,0:T(8,128)(2,1)} %shard_map.85), calls=%async_computation.1 | async-start | bytes 2097152 | tf_op jit(solution)/shard_map/all_to_all | solution.py:651
  32.8 0.0 copy-done
  32.8 0.0 copy-done.1
  32.8 0.5 shard_map.83
  33.3 22.5 %all-to-all-done.1.second = bf16[16,256,128]{2,1,0:T(8,128)(2,1)S(1)} async-done(((bf16[16,256,128]{2,1,0:T(8,128)(2,1)}), bf16[16,256,128]{2,1,0:T(8,128)(2,1)S(1)}, u32[]{:S(2)}, u32[]{:S(2)}) %all-to-all-start.1) | async-done | bytes 1048608 | tf_op jit(solution)/shard_map/all_to_all | solution.py:651
  55.8 2.4 %shard_map.86 = bf16[16,256,128]{2,1,0:T(8,128)(2,1)S(1)} custom-call(bf16[256,1024]{1,0:T(8,128)(2,1)S(1)} %get-tuple-element.16.first, f32[256,128]{1,0:T(8,128)S(1)} %get-tuple-element.17.means, f32[256,128]{1,0:T(8,128)S(1)} %get-tuple-element.18.roots, f32[256,128]{1,0:T(8,128)S(1)} %get-tuple-element.19.values, ...), custom_call_target="tpu_custom_call" | custom-call | flops 4000000000 | bytes 4194304 | tf_op jit(solution)/shard_map/pallas_call | solution.py:573
  58.2 30.6 %all_to_all.15.blocks = bf16[16,256,128]{2,1,0:T(8,128)(2,1)S(1)} all-to-all(bf16[16,256,128]{2,1,0:T(8,128)(2,1)S(1)} %shard_map.86), channel_id=1, replica_groups=mesh['grp'=16,'tile'=2] {'grp'}, dimensions={0} | all-to-all | bytes 2097152 | tf_op jit(solution)/shard_map/all_to_all | solution.py:651
  88.8 1.7 %shard_map.87 = bf16[64,2,4,8,128]{4,3,2,1,0:T(8,128)(2,1)} custom-call(bf16[16,256,128]{2,1,0:T(8,128)(2,1)S(1)} %all_to_all.15.blocks), custom_call_target="tpu_custom_call" | custom-call | flops 2000000000 | bytes 2097152 | tf_op jit(solution)/shard_map/pallas_call | solution.py:627
Async XLA Ops:
  4.0 8.4 %collective-permute-start = (f32[2,4,8,64,128]{4,3,2,1,0:T(8,128)S(1)}, f32[2,4,8,64,128]{4,3,2,1,0:T(8,128)}, u32[]{:S(2)}, u32[]{:S(2)}) collective-permute-start(f32[2,4,8,64,128]{4,3,2,1,0:T(8,128)S(1)} %get-tuple-element.20.own), channel_id=1, source_target_pairs={{0,1},{1,0},{2,3},{3,2},{4,5},{5,4},{6,7},{7,6},{8,9},{9,8},{10,11... | collective-permute-start | bytes 6291464 | tf_op jit(solution)/shard_map/ppermute | solution.py:644
  4.5 23.4 %all-to-all-start = ((bf16[16,128,128]{2,1,0:T(8,128)(2,1)}), bf16[16,128,128]{2,1,0:T(8,128)(2,1)S(1)}, u32[]{:S(2)}, u32[]{:S(2)}) async-start(bf16[16,128,128]{2,1,0:T(8,128)(2,1)} %get-tuple-element.15), calls=%async_computation | async-start | bytes 1048576 | tf_op jit(solution)/shard_map/all_to_all | solution.py:651
  12.4 5.2 %copy-start.2 = (s32[1,16,256]{2,1,0:T(8,128)S(1)}, s32[1,16,256]{2,1,0:T(8,128)}, u32[]{:S(2)}) copy-start(s32[1,16,256]{2,1,0:T(8,128)} %param.12) | copy-start | bytes 49156
  21.4 11.3 %copy-start = (f32[1,1,256]{2,1,0:T(1,128)S(1)}, f32[1,1,256]{2,1,0:T(1,128)}, u32[]{:S(2)}) copy-start(f32[1,1,256]{2,1,0:T(1,128)} %param.14) | copy-start | bytes 3076
  21.4 11.3 %copy-start.1 = (f32[1,1,256]{2,1,0:T(1,128)S(1)}, f32[1,1,256]{2,1,0:T(1,128)}, u32[]{:S(2)}) copy-start(f32[1,1,256]{2,1,0:T(1,128)} %param.15) | copy-start | bytes 3076
  27.9 28.0 %all-to-all-start.1 = ((bf16[16,256,128]{2,1,0:T(8,128)(2,1)}), bf16[16,256,128]{2,1,0:T(8,128)(2,1)S(1)}, u32[]{:S(2)}, u32[]{:S(2)}) async-start(bf16[16,256,128]{2,1,0:T(8,128)(2,1)} %shard_map.85), calls=%async_computation.1 | async-start | bytes 2097152 | tf_op jit(solution)/shard_map/all_to_all | solution.py:651
